TPU v7x, 256 devices: a whole 4x4x8 slice. The times are simulated.
256 devices in a mesh: row: 8 (over z), col: 16 (over x_hi, y, core), slab: 2 (over x_lo).
Axes of the slice: x: 4 (x_hi: 2, x_lo: 2; x = x_hi * 2 + x_lo), y: 4, z: 8, core: 2. Of those that a mesh axis runs over, the one named last changes fastest.
Arguments:
- amplitudes: bfloat16 [2, 8192, 2048], P('slab', 'row', 'col'), may hold values from -6 to 6
- integrals: bfloat16 [2048, 24576], P(('row', 'slab'), 'col'), may hold values from -0.125 to 0.125
- pair_count: int32 [2], replicated, may hold values from 4096 to 8192, as said below
- pair_sym: int32 [2, 64], P('slab', 'row'), may hold values from 0 to 1, as said below
- vir_sym: int32 [16], replicated, may hold values from 0 to 1
- out_sym: int32 [192], P('col'), may hold values from 0 to 1, as said below
Outputs:
- ladder: bfloat16 [2, 8192, 24576], P('slab', 'row', 'col')
Inputs may be any that keep to these rules, and one draw needn't show every extreme that they name: `pair_count`: one slab has all 8192 pairs live. `pair_sym`: in each slab, of the 8 row tiles j * 8 to j * 8 + 8 - 1 (those of one device), exactly half have block id 0 and half block id 1. `out_sym`: of the 12 output tiles j * 12 to j * 12 + 12 - 1 (those of one device), exactly half have block id 0 and half block id 1.
All inputs are finite; a program needn't handle non-finite values.
Results may differ from a plain program's by a relative error of at most 0.003.
Values may be sent and summed in bfloat16 or wider, within the bound.
No kernel may reach another device: no remote copies, remote signals or barrier semaphores. Data moves between devices by JAX's collectives and lax.ppermute only.
A program may use at most 64 MiB of HBM per device.

v0:
```python
import jax
import jax.numpy as jnp
from jax import lax
from jax.sharding import PartitionSpec as P

TILE = 128


def body(amplitudes, integrals, pair_count, pair_sym, vir_sym, out_sym):
    zero = jnp.zeros((), jnp.bfloat16)
    vir_cols = jnp.repeat(vir_sym, TILE)
    slab_now = lax.axis_index("slab")
    row_now = lax.axis_index("row")
    local_rows = amplitudes.shape[1]
    amp_width = amplitudes.shape[2]
    pair_tiles = pair_sym[0]
    pair_rows = jnp.repeat(pair_tiles, TILE)
    amp_start = lax.axis_index("col") * amp_width
    amp_cols = lax.dynamic_slice_in_dim(vir_cols, amp_start, amp_width)
    amps_kept = jnp.where(pair_rows[:, None] == amp_cols[None, :], amplitudes[0], zero)
    int_height = integrals.shape[0]
    int_start = (row_now * lax.axis_size("slab") + slab_now) * int_height
    int_rows = lax.dynamic_slice_in_dim(vir_cols, int_start, int_height)
    out_cols = jnp.repeat(out_sym, TILE)
    ints_kept = jnp.where(int_rows[:, None] == out_cols[None, :], integrals, zero)
    gathered = lax.all_gather(ints_kept, ("row", "slab"), axis=0, tiled=True)
    dense = lax.all_gather(amps_kept, "col", axis=1, tiled=True)
    product = jnp.dot(dense, gathered, preferred_element_type=jnp.float32)
    global_rows = row_now * local_rows + jnp.arange(local_rows, dtype=jnp.int32)
    live = global_rows < pair_count[slab_now]
    return jnp.where(live[:, None], product, 0.0).astype(jnp.bfloat16)[None]


def solution(mesh):
    in_specs = (
        P("slab", "row", "col"),
        P(("row", "slab"), "col"),
        P(),
        P("slab", "row"),
        P(),
        P("col"),
    )
    out_specs = P("slab", "row", "col")
    return jax.shard_map(body, mesh=mesh, in_specs=in_specs, out_specs=out_specs, check_vma=False)
```

profile of v0, /device:TPU:1, one launch (start us, length us, event | category | flops | bytes accessed | tf_op | source)
XLA Modules:
  0.0 233.4 jit_solution(13653378723304986393)
XLA Ops:
  6.5 0.0 copy-start
  6.5 0.0 all-gather.3.cloned.1.call-start
  6.5 0.7 broadcast_bitcast_fusion.2
  7.3 0.0 copy-done
  7.3 0.1 broadcast_bitcast_fusion.1
  7.3 0.1 fusion.1
  7.4 1.9 compare_select_fusion.1
  9.3 0.0 all-gather.3.cloned.1.call-update
  9.3 0.0 all-gather.5.cloned.1.call-start
  9.4 0.7 broadcast_bitcast_fusion
  10.1 1.9 compare_select_fusion
  12.0 0.0 all-gather.5.cloned.1.call-update
  12.0 1.2 dynamic_slice.9
  13.3 0.6 add_compare_fusion
  13.8 62.1 %all-gather.3.cloned.1.call-done = bf16[1024,2048]{1,0:T(8,128)(2,1)} async-done(((bf16[1024,128]{1,0:T(8,128)(2,1)}), bf16[1024,2048]{1,0:T(8,128)(2,1)}) %all-gather.3.cloned.1.call-update) | async-done | bytes 4194320 | tf_op jit(solution)/shard_map/all_gather | solution.py:27
  75.9 139.5 %all-gather.5.cloned.1.call-done = bf16[2048,1536]{1,0:T(8,128)(2,1)} async-done(((bf16[128,1536]{1,0:T(8,128)(2,1)}), bf16[2048,1536]{1,0:T(8,128)(2,1)}) %all-gather.5.cloned.1.call-update) | async-done | bytes 6291472 | tf_op jit(solution)/shard_map/all_gather | solution.py:26
  215.4 11.1 %fusion = bf16[1,1024,1536]{2,1,0:T(8,128)(2,1)} fusion(bf16[1024,2048]{1,0:T(8,128)(2,1)} %all-gather.3.cloned.1.call-done, bf16[2048,1536]{1,0:T(8,128)(2,1)} %all-gather.5.cloned.1.call-done, pred[1024]{0:T(1024)(128)(4,1)S(1)} %add_compare_fusion), kind=kOutput, calls=%fused_computation.1 | convolution fusion | flops 6445596672 | bytes 13632512 | tf_op jit(solution)/shard_map/dot_general | solution.py:28
Async XLA Ops:
  6.5 0.7 copy-start
  6.5 69.4 %all-gather.3.cloned.1.call-start = ((), (), s32[]{:S(2)}) async-start(), calls=%async_computation | async-start | bytes 4456448 | tf_op jit(solution)/shard_map/all_gather | solution.py:27
  9.3 206.1 %all-gather.5.cloned.1.call-start = ((), (), s32[]{:S(2)}) async-start(), calls=%async_computation.1 | async-start | bytes 6684672 | tf_op jit(solution)/shard_map/all_gather | solution.py:26
Sparse Core Ops, SparseCore 0:
  9.9 65.9 all-gather.2
  77.7 137.6 all-gather.4
where the time goes:
time: 234 us; the launch traced here: 233 us
  waiting for transfers between devices  202 us (86%)
  between operations  13.4 us (6%)
  matrix products  11.1 us (5%)
  other arithmetic  4.33 us (2%)
  local copies, waits for them, and re-layouts  2.86 us (1%)
    all_gather x1, waiting for transfers between devices, body(): gathered = lax.all_gather(ints_kept, ('row', 'slab'), axis=0, tiled=True)  140 us
    all_gather x1, waiting for transfers between devices, body(): dense = lax.all_gather(amps_kept, 'col', axis=1, tiled=True)  62.1 us
    dot_general x1, matrix products, body(): product = jnp.dot(dense, gathered, preferred_element_type=jnp.float32)  11.1 us
  transfers between devices with their start and end apart: 2, of which 2 were waited for; matrix products, arithmetic and copies ran while one was open for 2% of the time, Pallas kernels for 0%

commit v1 on v0

v1 whole, which is shorter than its diff:
```python
import functools

import jax
import jax.numpy as jnp
from jax import lax
from jax.experimental import pallas as pl
from jax.experimental.pallas import tpu as pltpu
from jax.sharding import PartitionSpec as P

TILE = 128
VMEM_LIMIT = 48 * 1024 * 1024


def pack_kernel(pair_tiles, vir, out_tiles, amp, ints, amp_out, int_out):
    amp_id = vir[lax.axis_index("col")]
    int_id = vir[lax.axis_index("row") * lax.axis_size("slab") + lax.axis_index("slab")]
    count = jnp.int32(0)
    for tile in range(pair_tiles.shape[1]):
        match = pair_tiles[0, tile] == amp_id

        @pl.when(match)
        def _():
            start = pl.multiple_of(count * TILE, TILE)
            amp_out[pl.ds(start, TILE), :] = amp[0, tile * TILE : (tile + 1) * TILE, :]

        count = count + match.astype(jnp.int32)
    count = jnp.int32(0)
    for tile in range(out_tiles.shape[0]):
        match = out_tiles[tile] == int_id

        @pl.when(match)
        def _():
            start = pl.multiple_of(count * TILE, TILE)
            int_out[:, pl.ds(start, TILE)] = ints[:, tile * TILE : (tile + 1) * TILE]

        count = count + match.astype(jnp.int32)


def pack(amplitudes, integrals, pair_sym, vir_sym, out_sym):
    smem = pl.BlockSpec(memory_space=pltpu.SMEM)
    vmem = pl.BlockSpec(memory_space=pltpu.VMEM)
    rows, width = amplitudes.shape[1:]
    depth, cols = integrals.shape
    return pl.pallas_call(
        pack_kernel,
        out_shape=(
            jax.ShapeDtypeStruct((rows // 2, width), jnp.bfloat16),
            jax.ShapeDtypeStruct((depth, cols // 2), jnp.bfloat16),
        ),
        in_specs=[smem, smem, smem, vmem, vmem],
        out_specs=(vmem, vmem),
    )(pair_sym, vir_sym, out_sym, amplitudes, integrals)


def ladder_kernel(pairs, k_tiles, rows, cols, *refs):
    pair_count, pair_tiles, vir, out_tiles, amp_own, amp_other = refs[:6]
    blocks = refs[6 : 6 + k_tiles]
    out = refs[6 + k_tiles]
    amp_buf, int_buf, acc, out_buf, where_k, row_at, col_at, amp_sem, int_sem, out_sem = refs[7 + k_tiles :]
    mt, nt = pair_tiles.shape[1], out_tiles.shape[0]
    col_now, row_now, slab_now = (lax.axis_index(name) for name in ("col", "row", "slab"))
    n_slab, n_row = lax.axis_size("slab"), lax.axis_size("row")

    ones = jnp.int32(0)
    for k in range(k_tiles):
        ones = ones + vir[k]
    zeros = k_tiles - ones
    zero_chunks = (zeros + 1) // 2
    one_chunks = (ones + 1) // 2
    chunks = zero_chunks + one_chunks
    nzero, none = jnp.int32(0), jnp.int32(0)
    for k in range(k_tiles):
        is_one = vir[k]
        where_k[k] = jnp.where(is_one == 1, 2 * zero_chunks + none, nzero)
        none = none + is_one
        nzero = nzero + 1 - is_one

    half = k_tiles // 2
    copies = []
    for core in range(2):
        source = amp_own if core == 0 else amp_other
        for j in range(half):
            y, hi = j // 2, j % 2
            k = (hi * (half // 2) + y) * 2 + jnp.bitwise_xor(col_now % 2, core)
            copies.append(
                pltpu.make_async_copy(
                    source.at[pl.ds(j * (rows // 2), rows // 2)],
                    amp_buf.at[where_k[k]],
                    amp_sem.at[core * half + j],
                )
            )
    for index, (step, other) in enumerate(pairs):
        k = lax.rem(row_now + step + n_row, n_row) * n_slab + (slab_now if other == 0 else 1 - slab_now)
        copies.append(pltpu.make_async_copy(blocks[index], int_buf.at[where_k[k]], int_sem.at[index]))
    for copy in copies:
        copy.start()

    @pl.when(zeros % 2 == 1)
    def _():
        amp_buf[zeros] = jnp.zeros(amp_buf.shape[1:], amp_buf.dtype)
        int_buf[zeros] = jnp.zeros(int_buf.shape[1:], int_buf.dtype)

    @pl.when(ones % 2 == 1)
    def _():
        last = 2 * zero_chunks + ones
        amp_buf[last] = jnp.zeros(amp_buf.shape[1:], amp_buf.dtype)
        int_buf[last] = jnp.zeros(int_buf.shape[1:], int_buf.dtype)

    out_buf[...] = jnp.zeros(out_buf.shape, out_buf.dtype)
    nzero, none = jnp.int32(0), jnp.int32(0)
    for tile in range(mt):
        is_one = pair_tiles[0, tile]
        row_at[jnp.where(is_one == 1, mt // 2 + none, nzero)] = tile
        none = none + is_one
        nzero = nzero + 1 - is_one
    nzero, none = jnp.int32(0), jnp.int32(0)
    for tile in range(nt):
        is_one = out_tiles[tile]
        col_at[jnp.where(is_one == 1, nt // 2 + none, nzero)] = tile
        none = none + is_one
        nzero = nzero + 1 - is_one

    for copy in copies:
        copy.wait()

    live = pair_count[slab_now] - row_now * rows
    for group in range(2):
        acc[...] = jnp.zeros(acc.shape, acc.dtype)
        first = 0 if group == 0 else zero_chunks
        last = zero_chunks if group == 0 else chunks

        @pl.loop(first, last)
        def _(chunk):
            left = jnp.concatenate([amp_buf[2 * chunk], amp_buf[2 * chunk + 1]], axis=1)
            right = jnp.concatenate([int_buf[2 * chunk], int_buf[2 * chunk + 1]], axis=0)
            acc[...] += jnp.dot(left, right, preferred_element_type=jnp.float32)

        for r in range(mt // 2):
            tile = row_at[group * (mt // 2) + r]
            row_start = pl.multiple_of(tile * TILE, TILE)
            keep = row_start + lax.broadcasted_iota(jnp.int32, (TILE, TILE), 0) < live
            for c in range(nt // 2):
                col_start = pl.multiple_of(col_at[group * (nt // 2) + c] * TILE, TILE)
                value = acc[r * TILE : (r + 1) * TILE, c * TILE : (c + 1) * TILE]
                out_buf[pl.ds(row_start, TILE), pl.ds(col_start, TILE)] = jnp.where(keep, value, 0.0).astype(jnp.bfloat16)
            pltpu.make_async_copy(
                out_buf.at[pl.ds(row_start, TILE)],
                out.at[0, pl.ds(row_start, TILE)],
                out_sem.at[group * (mt // 2) + r],
            ).start()
    for index in range(mt):
        row_start = pl.multiple_of(row_at[index] * TILE, TILE)
        pltpu.make_async_copy(
            out_buf.at[pl.ds(row_start, TILE)], out.at[0, pl.ds(row_start, TILE)], out_sem.at[index]
        ).wait()


def ladder(rows, cols, pairs, pair_count, pair_sym, vir_sym, out_sym, amp_own, amp_other, blocks):
    k_tiles = len(blocks)
    smem = pl.BlockSpec(memory_space=pltpu.SMEM)
    any_space = pl.BlockSpec(memory_space=pl.ANY)
    mt, nt = rows // TILE, cols // TILE
    return pl.pallas_call(
        functools.partial(ladder_kernel, pairs, k_tiles, rows, cols),
        out_shape=jax.ShapeDtypeStruct((1, rows, cols), jnp.bfloat16),
        in_specs=[smem] * 4 + [any_space] * (2 + k_tiles),
        out_specs=any_space,
        scratch_shapes=[
            pltpu.VMEM((k_tiles + 2, rows // 2, TILE), jnp.bfloat16),
            pltpu.VMEM((k_tiles + 2, TILE, cols // 2), jnp.bfloat16),
            pltpu.VMEM((rows // 2, cols // 2), jnp.float32),
            pltpu.VMEM((rows, cols), jnp.bfloat16),
            pltpu.SMEM((k_tiles,), jnp.int32),
            pltpu.SMEM((mt,), jnp.int32),
            pltpu.SMEM((nt,), jnp.int32),
            pltpu.SemaphoreType.DMA((k_tiles,)),
            pltpu.SemaphoreType.DMA((k_tiles,)),
            pltpu.SemaphoreType.DMA((mt,)),
        ],
        compiler_params=pltpu.CompilerParams(vmem_limit_bytes=VMEM_LIMIT),
    )(pair_count, pair_sym, vir_sym, out_sym, amp_own, amp_other, *blocks)


def body(amplitudes, integrals, pair_count, pair_sym, vir_sym, out_sym):
    rows, cols = amplitudes.shape[1], integrals.shape[1]
    n_row, n_col = lax.axis_size("row"), lax.axis_size("col")
    amp, block = pack(amplitudes, integrals, pair_sym, vir_sym, out_sym)

    half = n_col // 2
    across = [[c, c + half] for c in range(half)]
    round_y = [[h * half + y * 2 + core for y in range(half // 2)] for h in range(2) for core in range(2)]
    amp = lax.all_gather(amp, "col", axis=0, tiled=True, axis_index_groups=across)
    amp = lax.all_gather(amp, "col", axis=0, tiled=True, axis_index_groups=round_y)
    amp_other = lax.ppermute(amp, "col", [(c, c ^ 1) for c in range(n_col)])

    up = [(i, (i + 1) % n_row) for i in range(n_row)]
    down = [(i, (i - 1) % n_row) for i in range(n_row)]
    other = lax.ppermute(block, "slab", [(0, 1), (1, 0)])
    blocks = {(0, 0): block, (0, 1): other}
    for step in range(1, n_row // 2 + 1):
        for slab in range(2):
            if step < n_row // 2 or slab == 0:
                blocks[(-step, slab)] = lax.ppermute(blocks[(1 - step, slab)], "row", up)
            if step < n_row // 2 or slab == 1:
                blocks[(step, slab)] = lax.ppermute(blocks[(step - 1, slab)], "row", down)
    pairs = tuple(blocks)
    return ladder(
        rows, cols, pairs, pair_count, pair_sym, vir_sym, out_sym, amp, amp_other, [blocks[p] for p in pairs]
    )


def solution(mesh):
    in_specs = (
        P("slab", "row", "col"),
        P(("row", "slab"), "col"),
        P(),
        P("slab", "row"),
        P(),
        P("col"),
    )
    out_specs = P("slab", "row", "col")
    return jax.shard_map(body, mesh=mesh, in_specs=in_specs, out_specs=out_specs, check_vma=False)
```

time: 234 us -> 114 us (0.49)
  the two profiles are of different devices: /device:TPU:1 before, /device:TPU:2 now
where the time goes in v1:
time: 114 us
  waiting for transfers between devices  45.6 us (40%)
  starting transfers between devices  25.7 us (23%)
  Pallas kernels  16.1 us (14%)
  between operations  13.4 us (12%)
  blocking collectives  8.13 us (7%)
  local copies, waits for them, and re-layouts  4.77 us (4%)
    all_gather x1, waiting for transfers between devices, body(): lax.all_gather(amp, 'col', axis=0, tiled=True, axis_index_groups=round_y)  29.2 us
    ppermute x7, starting transfers between devices, body(): blocks[step, slab] = lax.ppermute(blocks[step - 1, slab], 'row', down)  22.8 us
    pallas_call x1, Pallas kernels, ladder(): pl.pallas_call(functools.partial(ladder_kernel, pairs, k_tiles, rows, col...  14.1 us
    all_gather x1, blocking collectives, body(): lax.all_gather(amp, 'col', axis=0, tiled=True, axis_index_groups=across)  8.13 us
    ppermute x7, waiting for transfers between devices, body(): blocks[step, slab] = lax.ppermute(blocks[step - 1, slab], 'row', down)  5.86 us
    ppermute x1, waiting for transfers between devices, body(): other = lax.ppermute(block, 'slab', [(0, 1), (1, 0)])  5.41 us
    ppermute x7, waiting for transfers between devices, body(): blocks[-step, slab] = lax.ppermute(blocks[1 - step, slab], 'row', up)  5.08 us
    unnamed x12, local copies, waits for them, and re-layouts  4.77 us
  transfers between devices with their start and end apart: 17, of which 10 were waited for; matrix products, arithmetic and copies ran while one was open for 0% of the time, Pallas kernels for 0%

profile of v1, /device:TPU:2, one launch (start us, length us, event | category | flops | bytes accessed | tf_op | source)
XLA Modules:
  0.0 113.8 jit_solution(17278601818745896293)
XLA Ops:
  6.5 2.0 %shard_map.64 = (bf16[512,128]{1,0:T(8,128)(2,1)}, bf16[128,768]{1,0:T(8,128)(2,1)}) custom-call(s32[1,8]{1,0:T(1,128)} %refs_1_.1, s32[16]{0:T(128)} %refs_2_.1, s32[12]{0:T(128)} %refs_3_.1, bf16[1,1024,128]{2,1,0:T(8,128)(2,1)} %amp.1, bf16[128,1536]{1,0:T(8,128)(2,1)} %ints.1), custom_call_target="tpu_custom_call" | custom-call | tf_op jit(solution)/shard_map/pallas_call | solution.py:44
  8.5 8.1 %all_gather.6 = bf16[1024,128]{1,0:T(8,128)(2,1)} all-gather(bf16[512,128]{1,0:T(8,128)(2,1)} %get-tuple-element.7), channel_id=1, replica_groups={{0,16},{2,18},{4,20},{6,22},{8,24},{10,26},{12,28},{14,30},{1,17},{3,19..., dimensions={0}, use_global_device_ids=true | all-gather | bytes 393216 | tf_op jit(solution)/shard_map/all_gather | solution.py:192
  16.7 0.0 all-gather.2.cloned.1.call-update
  16.7 29.2 %all-gather.2.cloned.1.call-done.refs_4_ = bf16[4096,128]{1,0:T(8,128)(2,1)} async-done(((bf16[1024,128]{1,0:T(8,128)(2,1)}), bf16[4096,128]{1,0:T(8,128)(2,1)}) %all-gather.2.cloned.1.call-update) | async-done | bytes 1048592 | tf_op jit(solution)/shard_map/all_gather | solution.py:193
  45.9 0.6 collective-permute-start.1
  46.5 1.6 %collective-permute-start.2 = (bf16[128,768]{1,0:T(8,128)(2,1)}, bf16[128,768]{1,0:T(8,128)(2,1)S(1)}, u32[]{:S(2)}, u32[]{:S(2)}) collective-permute-start(bf16[128,768]{1,0:T(8,128)(2,1)} %get-tuple-element.8.refs_6_), channel_id=1, source_target_pairs={{0,32},{32,64},{64,96},{96,128},{128,160},{160,192},{192,224},{224... | collective-permute-start | bytes 589832 | tf_op jit(solution)/shard_map/ppermute | solution.py:203
  48.1 5.4 %collective-permute-done.1.refs_7_ = bf16[128,768]{1,0:T(8,128)(2,1)S(1)} collective-permute-done((bf16[128,768]{1,0:T(8,128)(2,1)}, bf16[128,768]{1,0:T(8,128)(2,1)S(1)}, u32[]{:S(2)}, u32[]{:S(2)}) %collective-permute-start.1) | collective-permute-done | bytes 196640 | tf_op jit(solution)/shard_map/ppermute | solution.py:198
  53.5 3.3 %collective-permute-start.5 = (bf16[128,768]{1,0:T(8,128)(2,1)S(1)}, bf16[128,768]{1,0:T(8,128)(2,1)S(1)}, u32[]{:S(2)}, u32[]{:S(2)}) collective-permute-start(bf16[128,768]{1,0:T(8,128)(2,1)S(1)} %collective-permute-done.1.refs_7_), channel_id=1, source_target_pairs={{0,224},{32,0},{64,32},{96,64},{128,96},{160,128},{192,160},{224,1... | collective-permute-start | bytes 589832 | tf_op jit(solution)/shard_map/ppermute | solution.py:205
  56.8 1.4 %collective-permute-start.3 = (bf16[128,768]{1,0:T(8,128)(2,1)}, bf16[128,768]{1,0:T(8,128)(2,1)S(1)}, u32[]{:S(2)}, u32[]{:S(2)}) collective-permute-start(bf16[128,768]{1,0:T(8,128)(2,1)} %get-tuple-element.8.refs_6_), channel_id=1, source_target_pairs={{0,224},{32,0},{64,32},{96,64},{128,96},{160,128},{192,160},{224,1... | collective-permute-start | bytes 589832 | tf_op jit(solution)/shard_map/ppermute | solution.py:205
  58.2 0.7 collective-permute-start.6
  58.8 0.0 collective-permute-start.4
  58.9 3.3 %collective-permute-done.5.refs_11_ = bf16[128,768]{1,0:T(8,128)(2,1)S(1)} collective-permute-done((bf16[128,768]{1,0:T(8,128)(2,1)S(1)}, bf16[128,768]{1,0:T(8,128)(2,1)S(1)}, u32[]{:S(2)}, u32[]{:S(2)}) %collective-permute-start.5) | collective-permute-done | bytes 196640 | tf_op jit(solution)/shard_map/ppermute | solution.py:205
  62.1 3.7 %collective-permute-start.9 = (bf16[128,768]{1,0:T(8,128)(2,1)S(1)}, bf16[128,768]{1,0:T(8,128)(2,1)S(1)}, u32[]{:S(2)}, u32[]{:S(2)}) collective-permute-start(bf16[128,768]{1,0:T(8,128)(2,1)S(1)} %collective-permute-done.5.refs_11_), channel_id=1, source_target_pairs={{0,224},{32,0},{64,32},{96,64},{128,96},{160,128},{192,160},{224,1... | collective-permute-start | bytes 589832 | tf_op jit(solution)/shard_map/ppermute | solution.py:205
  65.8 0.6 collective-permute-done.3.refs_9_
  66.4 3.6 %collective-permute-start.7 = (bf16[128,768]{1,0:T(8,128)(2,1)S(1)}, bf16[128,768]{1,0:T(8,128)(2,1)S(1)}, u32[]{:S(2)}, u32[]{:S(2)}) collective-permute-start(bf16[128,768]{1,0:T(8,128)(2,1)S(1)} %collective-permute-done.3.refs_9_), channel_id=1, source_target_pairs={{0,224},{32,0},{64,32},{96,64},{128,96},{160,128},{192,160},{224,1... | collective-permute-start | bytes 589832 | tf_op jit(solution)/shard_map/ppermute | solution.py:205
  70.0 0.1 collective-permute-start.8
  70.1 0.7 collective-permute-done.9.refs_15_
  70.9 3.7 %collective-permute-start.13 = (bf16[128,768]{1,0:T(8,128)(2,1)S(1)}, bf16[128,768]{1,0:T(8,128)(2,1)S(1)}, u32[]{:S(2)}, u32[]{:S(2)}) collective-permute-start(bf16[128,768]{1,0:T(8,128)(2,1)S(1)} %collective-permute-done.9.refs_15_), channel_id=1, source_target_pairs={{0,224},{32,0},{64,32},{96,64},{128,96},{160,128},{192,160},{224,1... | collective-permute-start | bytes 589832 | tf_op jit(solution)/shard_map/ppermute | solution.py:205
  74.6 0.8 collective-permute-done.7.refs_13_
  75.4 3.7 %collective-permute-start.11 = (bf16[128,768]{1,0:T(8,128)(2,1)S(1)}, bf16[128,768]{1,0:T(8,128)(2,1)S(1)}, u32[]{:S(2)}, u32[]{:S(2)}) collective-permute-start(bf16[128,768]{1,0:T(8,128)(2,1)S(1)} %collective-permute-done.7.refs_13_), channel_id=1, source_target_pairs={{0,224},{32,0},{64,32},{96,64},{128,96},{160,128},{192,160},{224,1... | collective-permute-start | bytes 589832 | tf_op jit(solution)/shard_map/ppermute | solution.py:205
  79.1 1.0 collective-permute-done.8.refs_14_
  80.1 3.5 %collective-permute-start.15 = (bf16[128,768]{1,0:T(8,128)(2,1)S(1)}, bf16[128,768]{1,0:T(8,128)(2,1)S(1)}, u32[]{:S(2)}, u32[]{:S(2)}) collective-permute-start(bf16[128,768]{1,0:T(8,128)(2,1)S(1)} %collective-permute-done.13.refs_19_), channel_id=1, source_target_pairs={{0,224},{32,0},{64,32},{96,64},{128,96},{160,128},{192,160},{224,1... | collective-permute-start | bytes 589832 | tf_op jit(solution)/shard_map/ppermute | solution.py:205
  83.6 0.4 collective-permute-done.11.refs_17_
  84.0 1.9 %collective-permute-done.14.refs_20_ = bf16[128,768]{1,0:T(8,128)(2,1)S(1)} collective-permute-done((bf16[128,768]{1,0:T(8,128)(2,1)S(1)}, bf16[128,768]{1,0:T(8,128)(2,1)S(1)}, u32[]{:S(2)}, u32[]{:S(2)}) %collective-permute-start.14) | collective-permute-done | bytes 196640 | tf_op jit(solution)/shard_map/ppermute | solution.py:203
  86.0 2.1 %collective-permute-done.12.refs_18_ = bf16[128,768]{1,0:T(8,128)(2,1)S(1)} collective-permute-done((bf16[128,768]{1,0:T(8,128)(2,1)S(1)}, bf16[128,768]{1,0:T(8,128)(2,1)S(1)}, u32[]{:S(2)}, u32[]{:S(2)}) %collective-permute-start.12) | collective-permute-done | bytes 196640 | tf_op jit(solution)/shard_map/ppermute | solution.py:203
  88.1 1.2 %copy-done = bf16[4096,128]{1,0:T(8,128)(2,1)S(1)} copy-done((bf16[4096,128]{1,0:T(8,128)(2,1)S(1)}, bf16[4096,128]{1,0:T(8,128)(2,1)}, u32[]{:S(2)}) %copy-start) | copy-done | bytes 1048600
  89.3 0.9 copy-done.1
  90.2 0.7 copy-done.2
  90.9 0.7 copy-done.3
  91.5 0.7 copy-done.4
  92.2 0.7 copy-done.5
  92.8 14.1 %shard_map.65 = bf16[1,1024,1536]{2,1,0:T(8,128)(2,1)} custom-call(s32[2]{0:T(128)S(1)} %copy-done.5, s32[1,8]{1,0:T(1,128)S(1)} %copy-done.2, s32[16]{0:T(128)S(1)} %copy-done.3, s32[12]{0:T(128)S(1)} %copy-done.4, bf16[4096,128]{1,0:T(8,128)(2,1)S(1)} %copy-done, bf16[4096,128]{1,0:T(8,128)(2,1)S(1)} %collective-permute-done.refs_5_, ...), custom_call_target="tpu_custom_call" | custom-call | tf_op jit(solution)/shard_map/pallas_call | solution.py:163
  (18 shorter events, 0.0 us)
Async XLA Ops:
  6.5 39.4 %all-gather.2.cloned.1.call-start = ((), (), s32[]{:S(2)}) async-start(), calls=%async_computation | async-start | bytes 1310720 | tf_op jit(solution)/shard_map/all_gather | solution.py:193
  45.9 42.1 %collective-permute-start = (bf16[4096,128]{1,0:T(8,128)(2,1)}, bf16[4096,128]{1,0:T(8,128)(2,1)S(1)}, u32[]{:S(2)}, u32[]{:S(2)}) collective-permute-start(bf16[4096,128]{1,0:T(8,128)(2,1)} %all-gather.2.cloned.1.call-done.refs_4_), channel_id=1, source_target_pairs={{0,2},{2,0},{4,6},{6,4},{8,10},{10,8},{12,14},{14,12},{16,18},{18,... | collective-permute-start | bytes 3145736 | tf_op jit(solution)/shard_map/ppermute | solution.py:194
  45.9 7.5 %collective-permute-start.1 = (bf16[128,768]{1,0:T(8,128)(2,1)}, bf16[128,768]{1,0:T(8,128)(2,1)S(1)}, u32[]{:S(2)}, u32[]{:S(2)}) collective-permute-start(bf16[128,768]{1,0:T(8,128)(2,1)} %get-tuple-element.8.refs_6_), channel_id=1, source_target_pairs={{0,1},{1,0},{2,3},{3,2},{4,5},{5,4},{6,7},{7,6},{8,9},{9,8},{10,11... | collective-permute-start | bytes 589832 | tf_op jit(solution)/shard_map/ppermute | solution.py:198
  46.5 11.7 %collective-permute-start.2 = (bf16[128,768]{1,0:T(8,128)(2,1)}, bf16[128,768]{1,0:T(8,128)(2,1)S(1)}, u32[]{:S(2)}, u32[]{:S(2)}) collective-permute-start(bf16[128,768]{1,0:T(8,128)(2,1)} %get-tuple-element.8.refs_6_), channel_id=1, source_target_pairs={{0,32},{32,64},{64,96},{96,128},{128,160},{160,192},{192,224},{224... | collective-permute-start | bytes 589832 | tf_op jit(solution)/shard_map/ppermute | solution.py:203
  53.5 8.6 %collective-permute-start.5 = (bf16[128,768]{1,0:T(8,128)(2,1)S(1)}, bf16[128,768]{1,0:T(8,128)(2,1)S(1)}, u32[]{:S(2)}, u32[]{:S(2)}) collective-permute-start(bf16[128,768]{1,0:T(8,128)(2,1)S(1)} %collective-permute-done.1.refs_7_), channel_id=1, source_target_pairs={{0,224},{32,0},{64,32},{96,64},{128,96},{160,128},{192,160},{224,1... | collective-permute-start | bytes 589832 | tf_op jit(solution)/shard_map/ppermute | solution.py:205
  56.8 9.6 %collective-permute-start.3 = (bf16[128,768]{1,0:T(8,128)(2,1)}, bf16[128,768]{1,0:T(8,128)(2,1)S(1)}, u32[]{:S(2)}, u32[]{:S(2)}) collective-permute-start(bf16[128,768]{1,0:T(8,128)(2,1)} %get-tuple-element.8.refs_6_), channel_id=1, source_target_pairs={{0,224},{32,0},{64,32},{96,64},{128,96},{160,128},{192,160},{224,1... | collective-permute-start | bytes 589832 | tf_op jit(solution)/shard_map/ppermute | solution.py:205
  58.2 11.9 %collective-permute-start.6 = (bf16[128,768]{1,0:T(8,128)(2,1)S(1)}, bf16[128,768]{1,0:T(8,128)(2,1)S(1)}, u32[]{:S(2)}, u32[]{:S(2)}) collective-permute-start(bf16[128,768]{1,0:T(8,128)(2,1)S(1)} %collective-permute-done.2.refs_8_), channel_id=1, source_target_pairs={{0,32},{32,64},{64,96},{96,128},{128,160},{160,192},{192,224},{224... | collective-permute-start | bytes 589832 | tf_op jit(solution)/shard_map/ppermute | solution.py:203
  58.8 11.2 %collective-permute-start.4 = (bf16[128,768]{1,0:T(8,128)(2,1)S(1)}, bf16[128,768]{1,0:T(8,128)(2,1)S(1)}, u32[]{:S(2)}, u32[]{:S(2)}) collective-permute-start(bf16[128,768]{1,0:T(8,128)(2,1)S(1)} %collective-permute-done.1.refs_7_), channel_id=1, source_target_pairs={{0,32},{32,64},{64,96},{96,128},{128,160},{160,192},{192,224},{224... | collective-permute-start | bytes 589832 | tf_op jit(solution)/shard_map/ppermute | solution.py:203
  62.1 8.7 %collective-permute-start.9 = (bf16[128,768]{1,0:T(8,128)(2,1)S(1)}, bf16[128,768]{1,0:T(8,128)(2,1)S(1)}, u32[]{:S(2)}, u32[]{:S(2)}) collective-permute-start(bf16[128,768]{1,0:T(8,128)(2,1)S(1)} %collective-permute-done.5.refs_11_), channel_id=1, source_target_pairs={{0,224},{32,0},{64,32},{96,64},{128,96},{160,128},{192,160},{224,1... | collective-permute-start | bytes 589832 | tf_op jit(solution)/shard_map/ppermute | solution.py:205
  66.4 8.9 %collective-permute-start.7 = (bf16[128,768]{1,0:T(8,128)(2,1)S(1)}, bf16[128,768]{1,0:T(8,128)(2,1)S(1)}, u32[]{:S(2)}, u32[]{:S(2)}) collective-permute-start(bf16[128,768]{1,0:T(8,128)(2,1)S(1)} %collective-permute-done.3.refs_9_), channel_id=1, source_target_pairs={{0,224},{32,0},{64,32},{96,64},{128,96},{160,128},{192,160},{224,1... | collective-permute-start | bytes 589832 | tf_op jit(solution)/shard_map/ppermute | solution.py:205
  70.0 9.1 %collective-permute-start.10 = (bf16[128,768]{1,0:T(8,128)(2,1)S(1)}, bf16[128,768]{1,0:T(8,128)(2,1)S(1)}, u32[]{:S(2)}, u32[]{:S(2)}) collective-permute-start(bf16[128,768]{1,0:T(8,128)(2,1)S(1)} %collective-permute-done.6.refs_12_), channel_id=1, source_target_pairs={{0,32},{32,64},{64,96},{96,128},{128,160},{160,192},{192,224},{224... | collective-permute-start | bytes 589832 | tf_op jit(solution)/shard_map/ppermute | solution.py:203
  70.0 10.1 %collective-permute-start.8 = (bf16[128,768]{1,0:T(8,128)(2,1)S(1)}, bf16[128,768]{1,0:T(8,128)(2,1)S(1)}, u32[]{:S(2)}, u32[]{:S(2)}) collective-permute-start(bf16[128,768]{1,0:T(8,128)(2,1)S(1)} %collective-permute-done.4.refs_10_), channel_id=1, source_target_pairs={{0,32},{32,64},{64,96},{96,128},{128,160},{160,192},{192,224},{224... | collective-permute-start | bytes 589832 | tf_op jit(solution)/shard_map/ppermute | solution.py:203
  70.9 9.2 %collective-permute-start.13 = (bf16[128,768]{1,0:T(8,128)(2,1)S(1)}, bf16[128,768]{1,0:T(8,128)(2,1)S(1)}, u32[]{:S(2)}, u32[]{:S(2)}) collective-permute-start(bf16[128,768]{1,0:T(8,128)(2,1)S(1)} %collective-permute-done.9.refs_15_), channel_id=1, source_target_pairs={{0,224},{32,0},{64,32},{96,64},{128,96},{160,128},{192,160},{224,1... | collective-permute-start | bytes 589832 | tf_op jit(solution)/shard_map/ppermute | solution.py:205
  75.4 8.6 %collective-permute-start.11 = (bf16[128,768]{1,0:T(8,128)(2,1)S(1)}, bf16[128,768]{1,0:T(8,128)(2,1)S(1)}, u32[]{:S(2)}, u32[]{:S(2)}) collective-permute-start(bf16[128,768]{1,0:T(8,128)(2,1)S(1)} %collective-permute-done.7.refs_13_), channel_id=1, source_target_pairs={{0,224},{32,0},{64,32},{96,64},{128,96},{160,128},{192,160},{224,1... | collective-permute-start | bytes 589832 | tf_op jit(solution)/shard_map/ppermute | solution.py:205
  79.1 6.9 %collective-permute-start.14 = (bf16[128,768]{1,0:T(8,128)(2,1)S(1)}, bf16[128,768]{1,0:T(8,128)(2,1)S(1)}, u32[]{:S(2)}, u32[]{:S(2)}) collective-permute-start(bf16[128,768]{1,0:T(8,128)(2,1)S(1)} %collective-permute-done.10.refs_16_), channel_id=1, source_target_pairs={{0,32},{32,64},{64,96},{96,128},{128,160},{160,192},{192,224},{224... | collective-permute-start | bytes 589832 | tf_op jit(solution)/shard_map/ppermute | solution.py:203
  80.1 8.0 %collective-permute-start.12 = (bf16[128,768]{1,0:T(8,128)(2,1)S(1)}, bf16[128,768]{1,0:T(8,128)(2,1)S(1)}, u32[]{:S(2)}, u32[]{:S(2)}) collective-permute-start(bf16[128,768]{1,0:T(8,128)(2,1)S(1)} %collective-permute-done.8.refs_14_), channel_id=1, source_target_pairs={{0,32},{32,64},{64,96},{96,128},{128,160},{160,192},{192,224},{224... | collective-permute-start | bytes 589832 | tf_op jit(solution)/shard_map/ppermute | solution.py:203
  80.1 8.0 %collective-permute-start.15 = (bf16[128,768]{1,0:T(8,128)(2,1)S(1)}, bf16[128,768]{1,0:T(8,128)(2,1)S(1)}, u32[]{:S(2)}, u32[]{:S(2)}) collective-permute-start(bf16[128,768]{1,0:T(8,128)(2,1)S(1)} %collective-permute-done.13.refs_19_), channel_id=1, source_target_pairs={{0,224},{32,0},{64,32},{96,64},{128,96},{160,128},{192,160},{224,1... | collective-permute-start | bytes 589832 | tf_op jit(solution)/shard_map/ppermute | solution.py:205
  88.1 1.2 %copy-start = (bf16[4096,128]{1,0:T(8,128)(2,1)S(1)}, bf16[4096,128]{1,0:T(8,128)(2,1)}, u32[]{:S(2)}) copy-start(bf16[4096,128]{1,0:T(8,128)(2,1)} %all-gather.2.cloned.1.call-done.refs_4_) | copy-start | bytes 3145732
  89.3 0.9 copy-start.1
  90.2 0.7 copy-start.2
  90.9 0.7 copy-start.3
  91.5 0.7 copy-start.4
  92.2 0.7 copy-start.5
Sparse Core Ops, SparseCore 0:
  16.8 29.0 all-gather.1

commit v2 on v0

v2 whole, which is shorter than its diff:
```python
import functools

import jax
import jax.numpy as jnp
from jax import lax
from jax.experimental import pallas as pl
from jax.experimental.pallas import tpu as pltpu
from jax.sharding import PartitionSpec as P

TILE = 128
SIDE = ("own", "other")
VMEM_LIMIT = 24 * 1024 * 1024
SMALL_LIMIT = 4 * 1024 * 1024
SMEM = pl.BlockSpec(memory_space=pltpu.SMEM)
VMEM = pl.BlockSpec(memory_space=pltpu.VMEM)
ANY = pl.BlockSpec(memory_space=pl.ANY)


def pack_kernel(rows, pair_count, pair_tiles, vir, out_tiles, amp, ints, amp_out, int_out, meta):
    row_now, slab_now = lax.axis_index("row"), lax.axis_index("slab")
    amp_id = vir[lax.axis_index("col")]
    int_id = vir[row_now * lax.axis_size("slab") + slab_now]
    mt, nt, k_tiles = pair_tiles.shape[1], out_tiles.shape[0], vir.shape[0]
    count = jnp.int32(0)
    for tile in range(mt):
        meta[k_tiles + tile] = pair_tiles[0, tile]
        match = pair_tiles[0, tile] == amp_id

        @pl.when(match)
        def _():
            start = pl.multiple_of(count * TILE, TILE)
            amp_out[pl.ds(start, TILE), :] = amp[0, tile * TILE : (tile + 1) * TILE, :]

        count = count + match.astype(jnp.int32)
    count = jnp.int32(0)
    for tile in range(nt):
        meta[k_tiles + mt + tile] = out_tiles[tile]
        match = out_tiles[tile] == int_id

        @pl.when(match)
        def _():
            start = pl.multiple_of(count * TILE, TILE)
            int_out[:, pl.ds(start, TILE)] = ints[:, tile * TILE : (tile + 1) * TILE]

        count = count + match.astype(jnp.int32)
    for k in range(k_tiles):
        meta[k] = vir[k]
    meta[k_tiles + mt + nt] = pair_count[slab_now] - row_now * rows


def pack(amplitudes, integrals, pair_count, pair_sym, vir_sym, out_sym):
    rows, width = amplitudes.shape[1:]
    depth, cols = integrals.shape
    meta = pair_sym.shape[1] + vir_sym.shape[0] + out_sym.shape[0] + 1
    return pl.pallas_call(
        functools.partial(pack_kernel, rows),
        out_shape=(
            jax.ShapeDtypeStruct((rows // 2, width), jnp.bfloat16),
            jax.ShapeDtypeStruct((depth, cols // 2), jnp.bfloat16),
            jax.ShapeDtypeStruct((meta,), jnp.int32),
        ),
        in_specs=[SMEM] * 4 + [VMEM] * 2,
        out_specs=(VMEM, VMEM, SMEM),
        name="pack",
    )(pair_count, pair_sym, vir_sym, out_sym, amplitudes, integrals)


def join(arrays, passed=(), needed=(), name="join"):
    height, width = arrays[0].shape
    n, p = len(arrays), len(passed)

    def kernel(*refs):
        out = refs[n + p + len(needed)]
        for index in range(n):
            out[index * height : (index + 1) * height, :] = refs[index][...]

    return pl.pallas_call(
        kernel,
        out_shape=[jax.ShapeDtypeStruct((n * height, width), arrays[0].dtype)]
        + [jax.ShapeDtypeStruct(a.shape, a.dtype) for a in passed],
        in_specs=[VMEM] * n + [ANY] * (p + len(needed)),
        out_specs=[VMEM] + [ANY] * p,
        input_output_aliases={n + index: 1 + index for index in range(p)},
        compiler_params=pltpu.CompilerParams(vmem_limit_bytes=SMALL_LIMIT),
        name=name,
    )(*arrays, *passed, *needed)


def tile_of(step, other):
    n_row, n_slab = lax.axis_size("row"), lax.axis_size("slab")
    slab_now = lax.axis_index("slab")
    row = lax.rem(lax.axis_index("row") + step + n_row, n_row)
    return row, row * n_slab + (slab_now if other == 0 else 1 - slab_now)


def gather_tiles(pairs, meta, amps, blocks, amp_buf, int_buf, height):
    n_y = lax.axis_size("col") // 4
    core_now, hi_now, y_now = (
        lax.axis_index("col") % 2,
        lax.axis_index("col") // (2 * n_y),
        lax.axis_index("col") // 2 % n_y,
    )
    rows_ks = [tile_of(*pair) for pair in pairs]
    ids = [meta[k] for _, k in rows_ks]
    ones = sum(ids[1:], ids[0])
    zeros = len(pairs) - ones
    zero_chunks = (zeros + 1) // 2
    chunks = zero_chunks + (ones + 1) // 2

    @pl.when(zeros % 2 == 1)
    def _():
        amp_buf[zeros] = jnp.zeros(amp_buf.shape[1:], amp_buf.dtype)
        int_buf[zeros] = jnp.zeros(int_buf.shape[1:], int_buf.dtype)

    @pl.when(ones % 2 == 1)
    def _():
        last = 2 * zero_chunks + ones
        amp_buf[last] = jnp.zeros(amp_buf.shape[1:], amp_buf.dtype)
        int_buf[last] = jnp.zeros(int_buf.shape[1:], int_buf.dtype)

    nzero, none = jnp.int32(0), jnp.int32(0)
    for index, (row, k) in enumerate(rows_ks):
        spot = jnp.where(ids[index] == 1, 2 * zero_chunks + none, nzero)
        none = none + ids[index]
        nzero = nzero + 1 - ids[index]
        int_buf[spot] = blocks[index][...]
        hi = jnp.where(row // n_y == hi_now, 0, 1)
        y = lax.rem(row % n_y - y_now + n_y, n_y)
        start = pl.multiple_of((y * 2 + hi) * height, height)
        own = k % 2 == core_now

        @pl.when(own)
        def _():
            amp_buf[spot] = amps[0][pl.ds(start, height), :]

        @pl.when(jnp.logical_not(own))
        def _():
            amp_buf[spot] = amps[1][pl.ds(start, height), :]

    return zero_chunks, chunks


def chunk_product(amp_buf, int_buf, chunk):
    left = jnp.concatenate([amp_buf[2 * chunk], amp_buf[2 * chunk + 1]], axis=1)
    right = jnp.concatenate([int_buf[2 * chunk], int_buf[2 * chunk + 1]], axis=0)
    return jnp.dot(left, right, preferred_element_type=jnp.float32)


def early_kernel(pairs, n_pass, *refs):
    n = len(pairs)
    meta, amps, blocks, acc = refs[0], refs[1:3], refs[3 : 3 + n], refs[3 + n + n_pass]
    amp_buf, int_buf = refs[-2:]
    zero_chunks, chunks = gather_tiles(pairs, meta, amps, blocks, amp_buf, int_buf, amp_buf.shape[1])
    acc[...] = jnp.zeros(acc.shape, acc.dtype)

    @pl.loop(0, chunks)
    def _(chunk):
        acc[jnp.where(chunk < zero_chunks, 0, 1)] += chunk_product(amp_buf, int_buf, chunk)


def buffers(n, rows, cols):
    return [pltpu.VMEM((n + 2, rows // 2, TILE), jnp.bfloat16), pltpu.VMEM((n + 2, TILE, cols // 2), jnp.bfloat16)]


def early(rows, cols, pairs, meta, amps, blocks, passed=()):
    n, p = len(pairs), len(passed)
    return pl.pallas_call(
        functools.partial(early_kernel, pairs, p),
        out_shape=[jax.ShapeDtypeStruct((2, rows // 2, cols // 2), jnp.float32)]
        + [jax.ShapeDtypeStruct(a.shape, a.dtype) for a in passed],
        in_specs=[SMEM] + [VMEM] * (2 + n) + [ANY] * p,
        out_specs=[VMEM] + [ANY] * p,
        scratch_shapes=buffers(n, rows, cols),
        input_output_aliases={3 + n + index: 1 + index for index in range(p)},
        compiler_params=pltpu.CompilerParams(vmem_limit_bytes=VMEM_LIMIT),
        name="early_product",
    )(meta, *amps, *blocks, *passed)


def late_kernel(pairs, sizes, *refs):
    n = len(pairs)
    k_tiles, mt, nt = sizes
    meta, amps, acc_in, blocks, out = refs[0], refs[1:3], refs[3], refs[4 : 4 + n], refs[4 + n]
    amp_buf, int_buf, acc, out_buf, row_at, col_at, out_sem = refs[5 + n :]
    zero_chunks, chunks = gather_tiles(pairs, meta, amps, blocks, amp_buf, int_buf, amp_buf.shape[1])

    out_buf[...] = jnp.zeros(out_buf.shape, out_buf.dtype)
    for place, count, base in ((row_at, mt, k_tiles), (col_at, nt, k_tiles + mt)):
        nzero, none = jnp.int32(0), jnp.int32(0)
        for tile in range(count):
            is_one = meta[base + tile]
            place[jnp.where(is_one == 1, count // 2 + none, nzero)] = tile
            none = none + is_one
            nzero = nzero + 1 - is_one

    live = meta[k_tiles + mt + nt]
    for group in range(2):
        acc[...] = acc_in[group]
        first = 0 if group == 0 else zero_chunks
        last = zero_chunks if group == 0 else chunks

        @pl.loop(first, last)
        def _(chunk):
            acc[...] += chunk_product(amp_buf, int_buf, chunk)

        for r in range(mt // 2):
            tile = row_at[group * (mt // 2) + r]
            row_start = pl.multiple_of(tile * TILE, TILE)
            keep = row_start + lax.broadcasted_iota(jnp.int32, (TILE, TILE), 0) < live
            for c in range(nt // 2):
                col_start = pl.multiple_of(col_at[group * (nt // 2) + c] * TILE, TILE)
                value = acc[r * TILE : (r + 1) * TILE, c * TILE : (c + 1) * TILE]
                out_buf[pl.ds(row_start, TILE), pl.ds(col_start, TILE)] = jnp.where(keep, value, 0.0).astype(jnp.bfloat16)
            pltpu.make_async_copy(
                out_buf.at[pl.ds(row_start, TILE)],
                out.at[0, pl.ds(row_start, TILE)],
                out_sem.at[group * (mt // 2) + r],
            ).start()
    for index in range(mt):
        row_start = pl.multiple_of(row_at[index] * TILE, TILE)
        pltpu.make_async_copy(
            out_buf.at[pl.ds(row_start, TILE)], out.at[0, pl.ds(row_start, TILE)], out_sem.at[index]
        ).wait()


def late(rows, cols, k_tiles, pairs, meta, amps, acc, blocks):
    n = len(pairs)
    mt, nt = rows // TILE, cols // TILE
    return pl.pallas_call(
        functools.partial(late_kernel, pairs, (k_tiles, mt, nt)),
        out_shape=jax.ShapeDtypeStruct((1, rows, cols), jnp.bfloat16),
        in_specs=[SMEM] + [VMEM] * (3 + n),
        out_specs=ANY,
        scratch_shapes=buffers(n, rows, cols)
        + [
            pltpu.VMEM((rows // 2, cols // 2), jnp.float32),
            pltpu.VMEM((rows, cols), jnp.bfloat16),
            pltpu.SMEM((mt,), jnp.int32),
            pltpu.SMEM((nt,), jnp.int32),
            pltpu.SemaphoreType.DMA((mt,)),
        ],
        compiler_params=pltpu.CompilerParams(vmem_limit_bytes=VMEM_LIMIT),
        name="late_product",
    )(meta, *amps, acc, *blocks)


def body(amplitudes, integrals, pair_count, pair_sym, vir_sym, out_sym):
    rows, cols = amplitudes.shape[1], integrals.shape[1]
    n_row, n_col = lax.axis_size("row"), lax.axis_size("col")
    k_tiles = vir_sym.shape[0]
    n_y = n_col // 4
    amp, block, meta = pack(amplitudes, integrals, pair_count, pair_sym, vir_sym, out_sym)

    def send(a, axis, hops, name):
        with jax.named_scope(name):
            return lax.ppermute(a, axis, hops)

    def across(a):
        return send(a, "col", [(c, (c + n_col // 2) % n_col) for c in range(n_col)], "across_x")

    def swap(a):
        return send(a, "col", [(c, c ^ 1) for c in range(n_col)], "swap_cores")

    def from_y(a, d):
        hops = [((h * n_y + (y + d) % n_y) * 2 + core, (h * n_y + y) * 2 + core) for h in range(2) for y in range(n_y) for core in range(2)]
        return send(a, "col", hops, f"from_y_{d}")

    def up(a, name):
        return send(a, "row", [(i, (i + 1) % n_row) for i in range(n_row)], "up_" + name)

    def down(a, name):
        return send(a, "row", [(i, (i - 1) % n_row) for i in range(n_row)], "down_" + name)

    blocks = {(0, 0): block}
    blocks[(-1, 0)] = up(block, "own_1")
    blocks[(1, 0)] = down(block, "own_1")
    other = send(block, "slab", [(0, 1), (1, 0)], "swap_slabs")
    amp_two, blocks[(0, 1)] = join([amp, across(amp)], [other], [blocks[(-1, 0)], blocks[(1, 0)]], name="join_two")
    for step in range(1, n_row // 2 + 1):
        for slab in range(2):
            if (step < n_row // 2 or slab == 0) and (-step, slab) not in blocks:
                blocks[(-step, slab)] = up(blocks[(1 - step, slab)], f"{SIDE[slab]}_{step}")
            if (step < n_row // 2 or slab == 1) and (step, slab) not in blocks:
                blocks[(step, slab)] = down(blocks[(step - 1, slab)], f"{SIDE[slab]}_{step}")

    needed = [blocks[p] for p in ((-3, 0), (2, 0), (-2, 1), (2, 1))]
    own = join([amp_two] + [from_y(amp_two, d) for d in range(1, n_y)], needed=needed, name="join_y")[0]
    amps = [own, swap(own)]
    last = [p for p in blocks if abs(p[0]) == n_row // 2 or (abs(p[0]) == n_row // 2 - 1 and p[1] == 1)]
    first = [p for p in blocks if p not in last]
    (acc,) = early(rows, cols, first, meta, amps, [blocks[p] for p in first])
    return late(rows, cols, k_tiles, last, meta, amps, acc, [blocks[p] for p in last])


def solution(mesh):
    in_specs = (
        P("slab", "row", "col"),
        P(("row", "slab"), "col"),
        P(),
        P("slab", "row"),
        P(),
        P("col"),
    )
    out_specs = P("slab", "row", "col")
    return jax.shard_map(body, mesh=mesh, in_specs=in_specs, out_specs=out_specs, check_vma=False)
```

time: 234 us -> 61.1 us (0.26)
  waiting for transfers between devices: 202 us -> 20.5 us
  starting transfers between devices: 0.04 us -> 29.8 us
  between operations: 13.4 us -> 0.23 us
  matrix products: 11.1 us -> 0 us
  Pallas kernels: 0 us -> 9.71 us
  other arithmetic: 4.33 us -> 0 us
    all_gather x2 -> x0, waiting for transfers between devices: 202 us -> none  [the longest x1 140 us: body(): gathered = lax.all_gather(ints_kept, ('row', 'slab'), axis=0, tiled=True)]
    ppermute x0 -> x20, starting transfers between devices: none -> 29.8 us  [send(): return lax.ppermute(a, axis, hops)]
    ppermute x0 -> x20, waiting for transfers between devices: none -> 20.5 us  [send(): return lax.ppermute(a, axis, hops)]
    dot_general x1 -> x0, matrix products: 11.1 us -> none  [body(): product = jnp.dot(dense, gathered, preferred_element_type=jnp.float32)]
    pallas_call x0 -> x5, Pallas kernels: none -> 9.71 us  [the longest x1 3.91 us: early(): pl.pallas_call(functools.partial(early_kernel, pairs, p), out_shape=[jax....]
    select_n x2 -> x0, other arithmetic: 3.76 us -> none  [the longest x1 1.9 us: body(): jnp.where(int_rows[:, None] == out_cols[None, :], integrals, zero)]
  transfers between devices with their start and end apart: 2 -> 20, of which waited for: 2 -> 9; matrix products, arithmetic and copies ran while one was open for 2% -> 0% of each run, Pallas kernels for 0% -> 6%
where the time goes in v2:
time: 61.1 us; the launch traced here: 61.2 us
  starting transfers between devices  29.8 us (49%)
  waiting for transfers between devices  20.5 us (34%)
  Pallas kernels  9.71 us (16%)
  local copies, waits for them, and re-layouts  0.92 us (2%)
    ppermute x20, starting transfers between devices, send(): return lax.ppermute(a, axis, hops)  29.8 us
    ppermute x20, waiting for transfers between devices, send(): return lax.ppermute(a, axis, hops)  20.5 us
    pallas_call x1, Pallas kernels, early(): pl.pallas_call(functools.partial(early_kernel, pairs, p), out_shape=[jax....  3.91 us
    pallas_call x1, Pallas kernels, late(): pl.pallas_call(functools.partial(late_kernel, pairs, (k_tiles, mt, nt)),...  3.69 us
    pallas_call x1, Pallas kernels, pack(): pl.pallas_call(functools.partial(pack_kernel, rows), out_shape=(jax.Shape...  2.03 us
  transfers between devices with their start and end apart: 20, of which 9 were waited for; matrix products, arithmetic and copies ran while one was open for 0% of the time, Pallas kernels for 6%

profile of v2, /device:TPU:1, one launch (start us, length us, event | category | flops | bytes accessed | tf_op | source)
XLA Modules:
  0.0 61.2 jit_solution(11972865683928478543)
XLA Ops:
  0.0 2.0 %pack.1 = (bf16[512,128]{1,0:T(8,128)(2,1)}, bf16[128,768]{1,0:T(8,128)(2,1)}, s32[37]{0:T(128)}) custom-call(s32[2]{0:T(128)} %pair_count.1, s32[1,8]{1,0:T(1,128)} %pair_tiles.1, s32[16]{0:T(128)} %vir.1, s32[12]{0:T(128)} %out_tiles.1, bf16[1,1024,128]{2,1,0:T(8,128)(2,1)} %amp.1, bf16[128,1536]{1,0:T(8,128)(2,1)} %ints.1), custom_call_target="tpu_custom_call" | custom-call | tf_op jit(solution)/shard_map/pack/pallas_call | solution.py:55
  2.0 0.0 copy-start
  2.1 6.5 %collective-permute-start.3 = (bf16[128,768]{1,0:T(8,128)(2,1)}, bf16[128,768]{1,0:T(8,128)(2,1)S(1)}, u32[]{:S(2)}, u32[]{:S(2)}) collective-permute-start(bf16[128,768]{1,0:T(8,128)(2,1)} %get-tuple-element.12.refs_3_), channel_id=1, source_target_pairs={{0,224},{32,0},{64,32},{96,64},{128,96},{160,128},{192,160},{224,1... | collective-permute-start | bytes 589832 | tf_op jit(solution)/shard_map/down_own_1/ppermute | solution.py:256
  8.5 0.0 collective-permute-start.2
  8.5 1.2 %collective-permute-start.1 = (bf16[128,768]{1,0:T(8,128)(2,1)}, bf16[128,768]{1,0:T(8,128)(2,1)S(1)}, u32[]{:S(2)}, u32[]{:S(2)}) collective-permute-start(bf16[128,768]{1,0:T(8,128)(2,1)} %get-tuple-element.12.refs_3_), channel_id=1, source_target_pairs={{0,1},{1,0},{2,3},{3,2},{4,5},{5,4},{6,7},{7,6},{8,9},{9,8},{10,11... | collective-permute-start | bytes 589832 | tf_op jit(solution)/shard_map/swap_slabs/ppermute | solution.py:256
  9.8 2.4 %collective-permute-start = (bf16[512,128]{1,0:T(8,128)(2,1)}, bf16[512,128]{1,0:T(8,128)(2,1)S(1)}, u32[]{:S(2)}, u32[]{:S(2)}) collective-permute-start(bf16[512,128]{1,0:T(8,128)(2,1)} %get-tuple-element.11.refs_0_), channel_id=1, source_target_pairs={{0,16},{2,18},{4,20},{6,22},{8,24},{10,26},{12,28},{14,30},{16,0},... | collective-permute-start | bytes 393224 | tf_op jit(solution)/shard_map/across_x/ppermute | solution.py:256
  12.2 0.2 collective-permute-done.3.refs_4_.refs_5_
  12.4 3.3 %collective-permute-start.9 = (bf16[128,768]{1,0:T(8,128)(2,1)S(1)}, bf16[128,768]{1,0:T(8,128)(2,1)S(1)}, u32[]{:S(2)}, u32[]{:S(2)}) collective-permute-start(bf16[128,768]{1,0:T(8,128)(2,1)S(1)} %collective-permute-done.3.refs_4_.refs_5_), channel_id=1, source_target_pairs={{0,224},{32,0},{64,32},{96,64},{128,96},{160,128},{192,160},{224,1... | collective-permute-start | bytes 589832 | tf_op jit(solution)/shard_map/down_own_2/ppermute | solution.py:256
  15.7 3.2 %collective-permute-done.refs_1_ = bf16[512,128]{1,0:T(8,128)(2,1)S(1)} collective-permute-done((bf16[512,128]{1,0:T(8,128)(2,1)}, bf16[512,128]{1,0:T(8,128)(2,1)S(1)}, u32[]{:S(2)}, u32[]{:S(2)}) %collective-permute-start) | collective-permute-done | bytes 131104 | tf_op jit(solution)/shard_map/across_x/ppermute | solution.py:256
  18.9 0.0 collective-permute-done.1.refs_2_
  18.9 0.9 %copy-done.1 = bf16[512,128]{1,0:T(8,128)(2,1)S(1)} copy-done((bf16[512,128]{1,0:T(8,128)(2,1)S(1)}, bf16[512,128]{1,0:T(8,128)(2,1)}, u32[]{:S(2)}) %copy-start.1) | copy-done | bytes 131096
  19.8 1.4 %collective-permute-start.6 = (bf16[1024,128]{1,0:T(8,128)(2,1)S(1)}, bf16[1024,128]{1,0:T(8,128)(2,1)S(1)}, u32[]{:S(2)}, u32[]{:S(2)}) collective-permute-start(bf16[1024,128]{1,0:T(8,128)(2,1)S(1)} %get-tuple-element.13.refs_0_), channel_id=1, source_target_pairs={{12,0},{14,2},{0,4},{2,6},{4,8},{6,10},{8,12},{10,14},{28,16},{30,... | collective-permute-start | bytes 786440 | tf_op jit(solution)/shard_map/from_y_3/ppermute | solution.py:256
  21.2 2.4 %collective-permute-start.12 = (bf16[128,768]{1,0:T(8,128)(2,1)S(1)}, bf16[128,768]{1,0:T(8,128)(2,1)S(1)}, u32[]{:S(2)}, u32[]{:S(2)}) collective-permute-start(bf16[128,768]{1,0:T(8,128)(2,1)S(1)} %get-tuple-element.14.refs_6_), channel_id=1, source_target_pairs={{0,224},{32,0},{64,32},{96,64},{128,96},{160,128},{192,160},{224,1... | collective-permute-start | bytes 589832 | tf_op jit(solution)/shard_map/down_other_1/ppermute | solution.py:256
  23.6 2.6 %collective-permute-start.5 = (bf16[1024,128]{1,0:T(8,128)(2,1)S(1)}, bf16[1024,128]{1,0:T(8,128)(2,1)S(1)}, u32[]{:S(2)}, u32[]{:S(2)}) collective-permute-start(bf16[1024,128]{1,0:T(8,128)(2,1)S(1)} %get-tuple-element.13.refs_0_), channel_id=1, source_target_pairs={{8,0},{10,2},{12,4},{14,6},{0,8},{2,10},{4,12},{6,14},{24,16},{26,... | collective-permute-start | bytes 786440 | tf_op jit(solution)/shard_map/from_y_2/ppermute | solution.py:256
  26.2 1.1 %collective-permute-start.4 = (bf16[1024,128]{1,0:T(8,128)(2,1)S(1)}, bf16[1024,128]{1,0:T(8,128)(2,1)S(1)}, u32[]{:S(2)}, u32[]{:S(2)}) collective-permute-start(bf16[1024,128]{1,0:T(8,128)(2,1)S(1)} %get-tuple-element.13.refs_0_), channel_id=1, source_target_pairs={{4,0},{6,2},{8,4},{10,6},{12,8},{14,10},{0,12},{2,14},{20,16},{22,... | collective-permute-start | bytes 786440 | tf_op jit(solution)/shard_map/from_y_1/ppermute | solution.py:256
  27.3 2.3 %collective-permute-done.10.refs_7_ = bf16[128,768]{1,0:T(8,128)(2,1)S(1)} collective-permute-done((bf16[128,768]{1,0:T(8,128)(2,1)S(1)}, bf16[128,768]{1,0:T(8,128)(2,1)S(1)}, u32[]{:S(2)}, u32[]{:S(2)}) %collective-permute-start.10) | collective-permute-done | bytes 196640 | tf_op jit(solution)/shard_map/up_other_1/ppermute | solution.py:256
  29.6 0.4 collective-permute-start.13
  30.1 1.0 %collective-permute-start.11 = (bf16[128,768]{1,0:T(8,128)(2,1)S(1)}, bf16[128,768]{1,0:T(8,128)(2,1)S(1)}, u32[]{:S(2)}, u32[]{:S(2)}) collective-permute-start(bf16[128,768]{1,0:T(8,128)(2,1)S(1)} %collective-permute-done.10.refs_7_), channel_id=1, source_target_pairs={{0,32},{32,64},{64,96},{96,128},{128,160},{160,192},{192,224},{224... | collective-permute-start | bytes 589832 | tf_op jit(solution)/shard_map/up_other_2/ppermute | solution.py:256
  31.1 2.5 %collective-permute-done.5.refs_2_ = bf16[1024,128]{1,0:T(8,128)(2,1)S(1)} collective-permute-done((bf16[1024,128]{1,0:T(8,128)(2,1)S(1)}, bf16[1024,128]{1,0:T(8,128)(2,1)S(1)}, u32[]{:S(2)}, u32[]{:S(2)}) %collective-permute-start.5) | collective-permute-done | bytes 262176 | tf_op jit(solution)/shard_map/from_y_2/ppermute | solution.py:256
  33.6 1.6 %collective-permute-done.4.refs_1_ = bf16[1024,128]{1,0:T(8,128)(2,1)S(1)} collective-permute-done((bf16[1024,128]{1,0:T(8,128)(2,1)S(1)}, bf16[1024,128]{1,0:T(8,128)(2,1)S(1)}, u32[]{:S(2)}, u32[]{:S(2)}) %collective-permute-start.4) | collective-permute-done | bytes 262176 | tf_op jit(solution)/shard_map/from_y_1/ppermute | solution.py:256
  35.3 4.0 %collective-permute-done.11.refs_6_.refs_11_ = bf16[128,768]{1,0:T(8,128)(2,1)S(1)} collective-permute-done((bf16[128,768]{1,0:T(8,128)(2,1)S(1)}, bf16[128,768]{1,0:T(8,128)(2,1)S(1)}, u32[]{:S(2)}, u32[]{:S(2)}) %collective-permute-start.11) | collective-permute-done | bytes 196640 | tf_op jit(solution)/shard_map/up_other_2/ppermute | solution.py:256
  39.3 0.1 join_y.1.refs_1_
  39.4 3.0 %collective-permute-start.14 = (bf16[4096,128]{1,0:T(8,128)(2,1)S(1)}, bf16[4096,128]{1,0:T(8,128)(2,1)S(1)}, u32[]{:S(2)}, u32[]{:S(2)}) collective-permute-start(bf16[4096,128]{1,0:T(8,128)(2,1)S(1)} %join_y.1.refs_1_), channel_id=1, source_target_pairs={{0,2},{2,0},{4,6},{6,4},{8,10},{10,8},{12,14},{14,12},{16,18},{18,... | collective-permute-start | bytes 3145736 | tf_op jit(solution)/shard_map/swap_cores/ppermute | solution.py:256
  42.4 0.0 collective-permute-start.15
  42.4 1.5 %collective-permute-start.18 = (bf16[128,768]{1,0:T(8,128)(2,1)S(1)}, bf16[128,768]{1,0:T(8,128)(2,1)S(1)}, u32[]{:S(2)}, u32[]{:S(2)}) collective-permute-start(bf16[128,768]{1,0:T(8,128)(2,1)S(1)} %collective-permute-done.8.refs_4_.refs_13_), channel_id=1, source_target_pairs={{0,32},{32,64},{64,96},{96,128},{128,160},{160,192},{192,224},{224... | collective-permute-start | bytes 589832 | tf_op jit(solution)/shard_map/up_own_4/ppermute | solution.py:256
  43.9 1.4 %collective-permute-start.16 = (bf16[128,768]{1,0:T(8,128)(2,1)S(1)}, bf16[128,768]{1,0:T(8,128)(2,1)S(1)}, u32[]{:S(2)}, u32[]{:S(2)}) collective-permute-start(bf16[128,768]{1,0:T(8,128)(2,1)S(1)} %collective-permute-done.11.refs_6_.refs_11_), channel_id=1, source_target_pairs={{0,32},{32,64},{64,96},{96,128},{128,160},{160,192},{192,224},{224... | collective-permute-start | bytes 589832 | tf_op jit(solution)/shard_map/up_other_3/ppermute | solution.py:256
  45.4 3.5 %collective-permute-done.17.refs_5_ = bf16[128,768]{1,0:T(8,128)(2,1)S(1)} collective-permute-done((bf16[128,768]{1,0:T(8,128)(2,1)S(1)}, bf16[128,768]{1,0:T(8,128)(2,1)S(1)}, u32[]{:S(2)}, u32[]{:S(2)}) %collective-permute-start.17) | collective-permute-done | bytes 196640 | tf_op jit(solution)/shard_map/down_other_3/ppermute | solution.py:256
  48.9 1.4 %collective-permute-start.19 = (bf16[128,768]{1,0:T(8,128)(2,1)S(1)}, bf16[128,768]{1,0:T(8,128)(2,1)S(1)}, u32[]{:S(2)}, u32[]{:S(2)}) collective-permute-start(bf16[128,768]{1,0:T(8,128)(2,1)S(1)} %collective-permute-done.17.refs_5_), channel_id=1, source_target_pairs={{0,224},{32,0},{64,32},{96,64},{128,96},{160,128},{192,160},{224,1... | collective-permute-start | bytes 589832 | tf_op jit(solution)/shard_map/down_other_4/ppermute | solution.py:256
  50.3 2.8 %collective-permute-done.15.refs_14_ = bf16[128,768]{1,0:T(8,128)(2,1)S(1)} collective-permute-done((bf16[128,768]{1,0:T(8,128)(2,1)S(1)}, bf16[128,768]{1,0:T(8,128)(2,1)S(1)}, u32[]{:S(2)}, u32[]{:S(2)}) %collective-permute-start.15) | collective-permute-done | bytes 196640 | tf_op jit(solution)/shard_map/down_own_3/ppermute | solution.py:256
  53.1 3.9 %early_product.1.refs_3_ = f32[2,512,768]{2,1,0:T(8,128)S(1)} custom-call(s32[37]{0:T(128)S(1)} %copy-done.2, bf16[4096,128]{1,0:T(8,128)(2,1)S(1)} %join_y.1.refs_1_, bf16[4096,128]{1,0:T(8,128)(2,1)S(1)} %collective-permute-done.14.refs_2_, bf16[128,768]{1,0:T(8,128)(2,1)S(1)} %copy-done, bf16[128,768]{1,0:T(8,128)(2,1)S(1)} %collective-permute-done.2.refs_3_.refs_4_, ...), custom_call_target="tpu_custom_call" | custom-call | tf_op jit(solution)/shard_map/early_product/pallas_call | solution.py:167
  57.0 0.3 collective-permute-done.19.refs_7_
  57.3 3.7 %late_product.1 = bf16[1,1024,1536]{2,1,0:T(8,128)(2,1)} custom-call(s32[37]{0:T(128)S(1)} %copy-done.2, bf16[4096,128]{1,0:T(8,128)(2,1)S(1)} %join_y.1.refs_1_, bf16[4096,128]{1,0:T(8,128)(2,1)S(1)} %collective-permute-done.14.refs_2_, f32[2,512,768]{2,1,0:T(8,128)S(1)} %early_product.1.refs_3_, bf16[128,768]{1,0:T(8,128)(2,1)S(1)} %collective-permute-done.16.refs_4_, ...), custom_call_target="tpu_custom_call" | custom-call | tf_op jit(solution)/shard_map/late_product/pallas_call | solution.py:229
  (19 shorter events, 0.1 us)
Async XLA Ops:
  2.0 51.1 %copy-start = (bf16[128,768]{1,0:T(8,128)(2,1)S(1)}, bf16[128,768]{1,0:T(8,128)(2,1)}, u32[]{:S(2)}) copy-start(bf16[128,768]{1,0:T(8,128)(2,1)} %get-tuple-element.12.refs_3_) | copy-start | bytes 589828
  2.1 10.4 %collective-permute-start.3 = (bf16[128,768]{1,0:T(8,128)(2,1)}, bf16[128,768]{1,0:T(8,128)(2,1)S(1)}, u32[]{:S(2)}, u32[]{:S(2)}) collective-permute-start(bf16[128,768]{1,0:T(8,128)(2,1)} %get-tuple-element.12.refs_3_), channel_id=1, source_target_pairs={{0,224},{32,0},{64,32},{96,64},{128,96},{160,128},{192,160},{224,1... | collective-permute-start | bytes 589832 | tf_op jit(solution)/shard_map/down_own_1/ppermute | solution.py:256
  8.5 7.2 %collective-permute-start.2 = (bf16[128,768]{1,0:T(8,128)(2,1)}, bf16[128,768]{1,0:T(8,128)(2,1)S(1)}, u32[]{:S(2)}, u32[]{:S(2)}) collective-permute-start(bf16[128,768]{1,0:T(8,128)(2,1)} %get-tuple-element.12.refs_3_), channel_id=1, source_target_pairs={{0,32},{32,64},{64,96},{96,128},{128,160},{160,192},{192,224},{224... | collective-permute-start | bytes 589832 | tf_op jit(solution)/shard_map/up_own_1/ppermute | solution.py:256
  8.5 10.4 %collective-permute-start.1 = (bf16[128,768]{1,0:T(8,128)(2,1)}, bf16[128,768]{1,0:T(8,128)(2,1)S(1)}, u32[]{:S(2)}, u32[]{:S(2)}) collective-permute-start(bf16[128,768]{1,0:T(8,128)(2,1)} %get-tuple-element.12.refs_3_), channel_id=1, source_target_pairs={{0,1},{1,0},{2,3},{3,2},{4,5},{5,4},{6,7},{7,6},{8,9},{9,8},{10,11... | collective-permute-start | bytes 589832 | tf_op jit(solution)/shard_map/swap_slabs/ppermute | solution.py:256
  9.8 9.2 %collective-permute-start = (bf16[512,128]{1,0:T(8,128)(2,1)}, bf16[512,128]{1,0:T(8,128)(2,1)S(1)}, u32[]{:S(2)}, u32[]{:S(2)}) collective-permute-start(bf16[512,128]{1,0:T(8,128)(2,1)} %get-tuple-element.11.refs_0_), channel_id=1, source_target_pairs={{0,16},{2,18},{4,20},{6,22},{8,24},{10,26},{12,28},{14,30},{16,0},... | collective-permute-start | bytes 393224 | tf_op jit(solution)/shard_map/across_x/ppermute | solution.py:256
  12.4 11.2 %collective-permute-start.9 = (bf16[128,768]{1,0:T(8,128)(2,1)S(1)}, bf16[128,768]{1,0:T(8,128)(2,1)S(1)}, u32[]{:S(2)}, u32[]{:S(2)}) collective-permute-start(bf16[128,768]{1,0:T(8,128)(2,1)S(1)} %collective-permute-done.3.refs_4_.refs_5_), channel_id=1, source_target_pairs={{0,224},{32,0},{64,32},{96,64},{128,96},{160,128},{192,160},{224,1... | collective-permute-start | bytes 589832 | tf_op jit(solution)/shard_map/down_own_2/ppermute | solution.py:256
  15.7 10.5 %collective-permute-start.7 = (bf16[128,768]{1,0:T(8,128)(2,1)S(1)}, bf16[128,768]{1,0:T(8,128)(2,1)S(1)}, u32[]{:S(2)}, u32[]{:S(2)}) collective-permute-start(bf16[128,768]{1,0:T(8,128)(2,1)S(1)} %collective-permute-done.2.refs_3_.refs_4_), channel_id=1, source_target_pairs={{0,32},{32,64},{64,96},{96,128},{128,160},{160,192},{192,224},{224... | collective-permute-start | bytes 589832 | tf_op jit(solution)/shard_map/up_own_2/ppermute | solution.py:256
  18.9 0.9 %copy-start.1 = (bf16[512,128]{1,0:T(8,128)(2,1)S(1)}, bf16[512,128]{1,0:T(8,128)(2,1)}, u32[]{:S(2)}) copy-start(bf16[512,128]{1,0:T(8,128)(2,1)} %get-tuple-element.11.refs_0_) | copy-start | bytes 393220
  19.8 33.3 %copy-start.2 = (s32[37]{0:T(128)S(1)}, s32[37]{0:T(128)}, u32[]{:S(2)}) copy-start(s32[37]{0:T(128)} %get-tuple-element.10.refs_0_) | copy-start | bytes 448
  19.8 10.2 %collective-permute-start.6 = (bf16[1024,128]{1,0:T(8,128)(2,1)S(1)}, bf16[1024,128]{1,0:T(8,128)(2,1)S(1)}, u32[]{:S(2)}, u32[]{:S(2)}) collective-permute-start(bf16[1024,128]{1,0:T(8,128)(2,1)S(1)} %get-tuple-element.13.refs_0_), channel_id=1, source_target_pairs={{12,0},{14,2},{0,4},{2,6},{4,8},{6,10},{8,12},{10,14},{28,16},{30,... | collective-permute-start | bytes 786440 | tf_op jit(solution)/shard_map/from_y_3/ppermute | solution.py:256
  21.2 6.1 %collective-permute-start.12 = (bf16[128,768]{1,0:T(8,128)(2,1)S(1)}, bf16[128,768]{1,0:T(8,128)(2,1)S(1)}, u32[]{:S(2)}, u32[]{:S(2)}) collective-permute-start(bf16[128,768]{1,0:T(8,128)(2,1)S(1)} %get-tuple-element.14.refs_6_), channel_id=1, source_target_pairs={{0,224},{32,0},{64,32},{96,64},{128,96},{160,128},{192,160},{224,1... | collective-permute-start | bytes 589832 | tf_op jit(solution)/shard_map/down_other_1/ppermute | solution.py:256
  23.6 6.0 %collective-permute-start.10 = (bf16[128,768]{1,0:T(8,128)(2,1)S(1)}, bf16[128,768]{1,0:T(8,128)(2,1)S(1)}, u32[]{:S(2)}, u32[]{:S(2)}) collective-permute-start(bf16[128,768]{1,0:T(8,128)(2,1)S(1)} %get-tuple-element.14.refs_6_), channel_id=1, source_target_pairs={{0,32},{32,64},{64,96},{96,128},{128,160},{160,192},{192,224},{224... | collective-permute-start | bytes 589832 | tf_op jit(solution)/shard_map/up_other_1/ppermute | solution.py:256
  23.6 10.0 %collective-permute-start.5 = (bf16[1024,128]{1,0:T(8,128)(2,1)S(1)}, bf16[1024,128]{1,0:T(8,128)(2,1)S(1)}, u32[]{:S(2)}, u32[]{:S(2)}) collective-permute-start(bf16[1024,128]{1,0:T(8,128)(2,1)S(1)} %get-tuple-element.13.refs_0_), channel_id=1, source_target_pairs={{8,0},{10,2},{12,4},{14,6},{0,8},{2,10},{4,12},{6,14},{24,16},{26,... | collective-permute-start | bytes 786440 | tf_op jit(solution)/shard_map/from_y_2/ppermute | solution.py:256
  26.2 9.0 %collective-permute-start.4 = (bf16[1024,128]{1,0:T(8,128)(2,1)S(1)}, bf16[1024,128]{1,0:T(8,128)(2,1)S(1)}, u32[]{:S(2)}, u32[]{:S(2)}) collective-permute-start(bf16[1024,128]{1,0:T(8,128)(2,1)S(1)} %get-tuple-element.13.refs_0_), channel_id=1, source_target_pairs={{4,0},{6,2},{8,4},{10,6},{12,8},{14,10},{0,12},{2,14},{20,16},{22,... | collective-permute-start | bytes 786440 | tf_op jit(solution)/shard_map/from_y_1/ppermute | solution.py:256
  27.3 8.0 %collective-permute-start.8 = (bf16[128,768]{1,0:T(8,128)(2,1)S(1)}, bf16[128,768]{1,0:T(8,128)(2,1)S(1)}, u32[]{:S(2)}, u32[]{:S(2)}) collective-permute-start(bf16[128,768]{1,0:T(8,128)(2,1)S(1)} %collective-permute-done.7.refs_9_), channel_id=1, source_target_pairs={{0,32},{32,64},{64,96},{96,128},{128,160},{160,192},{192,224},{224... | collective-permute-start | bytes 589832 | tf_op jit(solution)/shard_map/up_own_3/ppermute | solution.py:256
  29.6 5.7 %collective-permute-start.13 = (bf16[128,768]{1,0:T(8,128)(2,1)S(1)}, bf16[128,768]{1,0:T(8,128)(2,1)S(1)}, u32[]{:S(2)}, u32[]{:S(2)}) collective-permute-start(bf16[128,768]{1,0:T(8,128)(2,1)S(1)} %collective-permute-done.12.refs_8_), channel_id=1, source_target_pairs={{0,224},{32,0},{64,32},{96,64},{128,96},{160,128},{192,160},{224,1... | collective-permute-start | bytes 589832 | tf_op jit(solution)/shard_map/down_other_2/ppermute | solution.py:256
  30.1 9.2 %collective-permute-start.11 = (bf16[128,768]{1,0:T(8,128)(2,1)S(1)}, bf16[128,768]{1,0:T(8,128)(2,1)S(1)}, u32[]{:S(2)}, u32[]{:S(2)}) collective-permute-start(bf16[128,768]{1,0:T(8,128)(2,1)S(1)} %collective-permute-done.10.refs_7_), channel_id=1, source_target_pairs={{0,32},{32,64},{64,96},{96,128},{128,160},{160,192},{192,224},{224... | collective-permute-start | bytes 589832 | tf_op jit(solution)/shard_map/up_other_2/ppermute | solution.py:256
  39.4 13.7 %collective-permute-start.14 = (bf16[4096,128]{1,0:T(8,128)(2,1)S(1)}, bf16[4096,128]{1,0:T(8,128)(2,1)S(1)}, u32[]{:S(2)}, u32[]{:S(2)}) collective-permute-start(bf16[4096,128]{1,0:T(8,128)(2,1)S(1)} %join_y.1.refs_1_), channel_id=1, source_target_pairs={{0,2},{2,0},{4,6},{6,4},{8,10},{10,8},{12,14},{14,12},{16,18},{18,... | collective-permute-start | bytes 3145736 | tf_op jit(solution)/shard_map/swap_cores/ppermute | solution.py:256
  42.4 6.5 %collective-permute-start.17 = (bf16[128,768]{1,0:T(8,128)(2,1)S(1)}, bf16[128,768]{1,0:T(8,128)(2,1)S(1)}, u32[]{:S(2)}, u32[]{:S(2)}) collective-permute-start(bf16[128,768]{1,0:T(8,128)(2,1)S(1)} %collective-permute-done.13.refs_7_.refs_12_), channel_id=1, source_target_pairs={{0,224},{32,0},{64,32},{96,64},{128,96},{160,128},{192,160},{224,1... | collective-permute-start | bytes 589832 | tf_op jit(solution)/shard_map/down_other_3/ppermute | solution.py:256
  42.4 10.7 %collective-permute-start.15 = (bf16[128,768]{1,0:T(8,128)(2,1)S(1)}, bf16[128,768]{1,0:T(8,128)(2,1)S(1)}, u32[]{:S(2)}, u32[]{:S(2)}) collective-permute-start(bf16[128,768]{1,0:T(8,128)(2,1)S(1)} %collective-permute-done.9.refs_5_.refs_10_), channel_id=1, source_target_pairs={{0,224},{32,0},{64,32},{96,64},{128,96},{160,128},{192,160},{224,1... | collective-permute-start | bytes 589832 | tf_op jit(solution)/shard_map/down_own_3/ppermute | solution.py:256
  42.4 14.6 %collective-permute-start.18 = (bf16[128,768]{1,0:T(8,128)(2,1)S(1)}, bf16[128,768]{1,0:T(8,128)(2,1)S(1)}, u32[]{:S(2)}, u32[]{:S(2)}) collective-permute-start(bf16[128,768]{1,0:T(8,128)(2,1)S(1)} %collective-permute-done.8.refs_4_.refs_13_), channel_id=1, source_target_pairs={{0,32},{32,64},{64,96},{96,128},{128,160},{160,192},{192,224},{224... | collective-permute-start | bytes 589832 | tf_op jit(solution)/shard_map/up_own_4/ppermute | solution.py:256
  43.9 13.1 %collective-permute-start.16 = (bf16[128,768]{1,0:T(8,128)(2,1)S(1)}, bf16[128,768]{1,0:T(8,128)(2,1)S(1)}, u32[]{:S(2)}, u32[]{:S(2)}) collective-permute-start(bf16[128,768]{1,0:T(8,128)(2,1)S(1)} %collective-permute-done.11.refs_6_.refs_11_), channel_id=1, source_target_pairs={{0,32},{32,64},{64,96},{96,128},{128,160},{160,192},{192,224},{224... | collective-permute-start | bytes 589832 | tf_op jit(solution)/shard_map/up_other_3/ppermute | solution.py:256
  48.9 8.4 %collective-permute-start.19 = (bf16[128,768]{1,0:T(8,128)(2,1)S(1)}, bf16[128,768]{1,0:T(8,128)(2,1)S(1)}, u32[]{:S(2)}, u32[]{:S(2)}) collective-permute-start(bf16[128,768]{1,0:T(8,128)(2,1)S(1)} %collective-permute-done.17.refs_5_), channel_id=1, source_target_pairs={{0,224},{32,0},{64,32},{96,64},{128,96},{160,128},{192,160},{224,1... | collective-permute-start | bytes 589832 | tf_op jit(solution)/shard_map/down_other_4/ppermute | solution.py:256

commit v3 on v2

v3 whole, which is shorter than its diff:
```python
import functools

import jax
import jax.numpy as jnp
from jax import lax
from jax.experimental import pallas as pl
from jax.experimental.pallas import tpu as pltpu
from jax.sharding import PartitionSpec as P

TILE = 128
SIDES = ("own", "other")
VMEM_LIMIT = 24 * 1024 * 1024
SMALL_LIMIT = 4 * 1024 * 1024
SMEM = pl.BlockSpec(memory_space=pltpu.SMEM)
VMEM = pl.BlockSpec(memory_space=pltpu.VMEM)
ANY = pl.BlockSpec(memory_space=pl.ANY)


def pack_kernel(rows, pair_count, pair_tiles, vir, out_tiles, amp, ints, amp_out, int_out, meta):
    row_now, slab_now = lax.axis_index("row"), lax.axis_index("slab")
    amp_id = vir[lax.axis_index("col")]
    int_id = vir[row_now * lax.axis_size("slab") + slab_now]
    mt, nt, k_tiles = pair_tiles.shape[1], out_tiles.shape[0], vir.shape[0]
    count = jnp.int32(0)
    for tile in range(mt):
        meta[k_tiles + tile] = pair_tiles[0, tile]
        match = pair_tiles[0, tile] == amp_id

        @pl.when(match)
        def _():
            start = pl.multiple_of(count * TILE, TILE)
            amp_out[pl.ds(start, TILE), :] = amp[0, tile * TILE : (tile + 1) * TILE, :]

        count = count + match.astype(jnp.int32)
    count = jnp.int32(0)
    for tile in range(nt):
        meta[k_tiles + mt + tile] = out_tiles[tile]
        match = out_tiles[tile] == int_id

        @pl.when(match)
        def _():
            start = pl.multiple_of(count * TILE, TILE)
            int_out[:, pl.ds(start, TILE)] = ints[:, tile * TILE : (tile + 1) * TILE]

        count = count + match.astype(jnp.int32)
    for k in range(k_tiles):
        meta[k] = vir[k]
    meta[k_tiles + mt + nt] = pair_count[slab_now] - row_now * rows


def pack(amplitudes, integrals, pair_count, pair_sym, vir_sym, out_sym):
    rows, width = amplitudes.shape[1:]
    depth, cols = integrals.shape
    meta = pair_sym.shape[1] + vir_sym.shape[0] + out_sym.shape[0] + 1
    return pl.pallas_call(
        functools.partial(pack_kernel, rows),
        out_shape=(
            jax.ShapeDtypeStruct((rows // 2, width), jnp.bfloat16),
            jax.ShapeDtypeStruct((depth, cols // 2), jnp.bfloat16),
            jax.ShapeDtypeStruct((meta,), jnp.int32),
        ),
        in_specs=[SMEM] * 4 + [VMEM] * 2,
        out_specs=(VMEM, VMEM, SMEM),
        name="pack",
    )(pair_count, pair_sym, vir_sym, out_sym, amplitudes, integrals)


def join(parts, needed=(), name="join"):
    parts = [part if isinstance(part, tuple) else (part, 0, part.shape[0]) for part in parts]
    n = len(parts)
    height, width = sum(part[2] for part in parts), parts[0][0].shape[1]

    def kernel(*refs):
        out = refs[n + len(needed)]
        at = 0
        for ref, (_, start, size) in zip(refs, parts):
            out[at : at + size, :] = ref[start : start + size, :]
            at += size

    return pl.pallas_call(
        kernel,
        out_shape=jax.ShapeDtypeStruct((height, width), parts[0][0].dtype),
        in_specs=[VMEM] * n + [ANY] * len(needed),
        out_specs=VMEM,
        compiler_params=pltpu.CompilerParams(vmem_limit_bytes=SMALL_LIMIT),
        name=name,
    )(*[part[0] for part in parts], *needed)


def tile_of(step, other):
    n_row, n_slab = lax.axis_size("row"), lax.axis_size("slab")
    slab_now = lax.axis_index("slab")
    row = lax.rem(lax.axis_index("row") + step + n_row, n_row)
    return row, row * n_slab + (slab_now if other == 0 else 1 - slab_now)


def gather_tiles(pairs, meta, blocks, order, int_buf, none_tile):
    ks = [tile_of(*pair)[1] for group in pairs for pair in group]
    ids = [meta[k] for k in ks]
    ones = sum(ids[1:], ids[0])
    zeros = len(ids) - ones
    zero_chunks = (zeros + 1) // 2
    chunks = zero_chunks + (ones + 1) // 2

    @pl.when(zeros % 2 == 1)
    def _():
        order[zeros] = none_tile
        int_buf[zeros] = jnp.zeros(int_buf.shape[1:], int_buf.dtype)

    @pl.when(ones % 2 == 1)
    def _():
        last = 2 * zero_chunks + ones
        order[last] = none_tile
        int_buf[last] = jnp.zeros(int_buf.shape[1:], int_buf.dtype)

    nzero, none = jnp.int32(0), jnp.int32(0)
    sources = [(ref, slot) for ref, group in zip(blocks, pairs) for slot in range(len(group))]
    for k, one, (ref, slot) in zip(ks, ids, sources):
        spot = jnp.where(one == 1, 2 * zero_chunks + none, nzero)
        none = none + one
        nzero = nzero + 1 - one
        order[spot] = k
        int_buf[spot] = ref[slot * TILE : (slot + 1) * TILE, :]
    return zero_chunks, chunks


def chunk_product(amp_all, int_buf, order, chunk):
    left = jnp.concatenate([amp_all[order[2 * chunk]], amp_all[order[2 * chunk + 1]]], axis=1)
    right = jnp.concatenate([int_buf[2 * chunk], int_buf[2 * chunk + 1]], axis=0)
    return jnp.dot(left, right, preferred_element_type=jnp.float32)


def early_kernel(pairs, n_amp, height, *refs):
    n = len(pairs)
    meta, amps, blocks = refs[0], refs[1 : 1 + n_amp], refs[1 + n_amp : 1 + n_amp + n]
    acc, amp_all, int_buf, order = refs[1 + n_amp + n :]
    col = lax.axis_index("col")
    n_y = amps[0].shape[0] // (2 * height)
    hi_now, y_now, core_now = col // (2 * n_y), col // 2 % n_y, col % 2
    for core in range(2):
        for y in range(n_y):
            for hi in range(2):
                k = ((hi_now if hi == 0 else 1 - hi_now) * n_y + jnp.bitwise_xor(y_now, y)) * 2 + (
                    core_now if core == 0 else 1 - core_now
                )
                at = (2 * y + hi) * height
                amp_all[k] = amps[core][at : at + height, :]
    none_tile = amp_all.shape[0] - 1
    amp_all[none_tile] = jnp.zeros(amp_all.shape[1:], amp_all.dtype)
    zero_chunks, chunks = gather_tiles(pairs, meta, blocks, order, int_buf, none_tile)
    acc[...] = jnp.zeros(acc.shape, acc.dtype)

    @pl.loop(0, chunks)
    def _(chunk):
        acc[jnp.where(chunk < zero_chunks, 0, 1)] += chunk_product(amp_all, int_buf, order, chunk)


def buffers(pairs, cols):
    n = sum(len(group) for group in pairs) + 2
    return [pltpu.VMEM((n, TILE, cols // 2), jnp.bfloat16), pltpu.SMEM((n,), jnp.int32)]


def early(rows, cols, k_tiles, pairs, meta, amps, blocks):
    n, n_amp = len(pairs), len(amps)
    return pl.pallas_call(
        functools.partial(early_kernel, pairs, n_amp, rows // 2),
        out_shape=(
            jax.ShapeDtypeStruct((2, rows // 2, cols // 2), jnp.float32),
            jax.ShapeDtypeStruct((k_tiles + 1, rows // 2, TILE), jnp.bfloat16),
        ),
        in_specs=[SMEM] + [VMEM] * (n_amp + n),
        out_specs=(VMEM, VMEM),
        scratch_shapes=buffers(pairs, cols),
        compiler_params=pltpu.CompilerParams(vmem_limit_bytes=VMEM_LIMIT),
        name="early_product",
    )(meta, *amps, *blocks)


def late_kernel(pairs, sizes, *refs):
    n = len(pairs)
    k_tiles, mt, nt = sizes
    meta, acc_in, amp_all, blocks, out = refs[0], refs[1], refs[2], refs[3 : 3 + n], refs[3 + n]
    int_buf, order, acc, out_buf, row_at, col_at, out_sem = refs[4 + n :]
    zero_chunks, chunks = gather_tiles(pairs, meta, blocks, order, int_buf, k_tiles)

    out_buf[...] = jnp.zeros(out_buf.shape, out_buf.dtype)
    for place, count, base in ((row_at, mt, k_tiles), (col_at, nt, k_tiles + mt)):
        nzero, none = jnp.int32(0), jnp.int32(0)
        for tile in range(count):
            is_one = meta[base + tile]
            place[jnp.where(is_one == 1, count // 2 + none, nzero)] = tile
            none = none + is_one
            nzero = nzero + 1 - is_one

    live = meta[k_tiles + mt + nt]
    for group in range(2):
        acc[...] = acc_in[group]
        first = 0 if group == 0 else zero_chunks
        last = zero_chunks if group == 0 else chunks

        @pl.loop(first, last)
        def _(chunk):
            acc[...] += chunk_product(amp_all, int_buf, order, chunk)

        for r in range(mt // 2):
            tile = row_at[group * (mt // 2) + r]
            row_start = pl.multiple_of(tile * TILE, TILE)
            keep = row_start + lax.broadcasted_iota(jnp.int32, (TILE, TILE), 0) < live
            for c in range(nt // 2):
                col_start = pl.multiple_of(col_at[group * (nt // 2) + c] * TILE, TILE)
                value = acc[r * TILE : (r + 1) * TILE, c * TILE : (c + 1) * TILE]
                out_buf[pl.ds(row_start, TILE), pl.ds(col_start, TILE)] = jnp.where(keep, value, 0.0).astype(jnp.bfloat16)
            pltpu.make_async_copy(
                out_buf.at[pl.ds(row_start, TILE)],
                out.at[0, pl.ds(row_start, TILE)],
                out_sem.at[group * (mt // 2) + r],
            ).start()
    for index in range(mt):
        row_start = pl.multiple_of(row_at[index] * TILE, TILE)
        pltpu.make_async_copy(
            out_buf.at[pl.ds(row_start, TILE)], out.at[0, pl.ds(row_start, TILE)], out_sem.at[index]
        ).wait()


def late(rows, cols, k_tiles, pairs, meta, acc, amp_all, blocks):
    n = len(pairs)
    mt, nt = rows // TILE, cols // TILE
    return pl.pallas_call(
        functools.partial(late_kernel, pairs, (k_tiles, mt, nt)),
        out_shape=jax.ShapeDtypeStruct((1, rows, cols), jnp.bfloat16),
        in_specs=[SMEM] + [VMEM] * (2 + n),
        out_specs=ANY,
        scratch_shapes=buffers(pairs, cols)
        + [
            pltpu.VMEM((rows // 2, cols // 2), jnp.float32),
            pltpu.VMEM((rows, cols), jnp.bfloat16),
            pltpu.SMEM((mt,), jnp.int32),
            pltpu.SMEM((nt,), jnp.int32),
            pltpu.SemaphoreType.DMA((mt,)),
        ],
        compiler_params=pltpu.CompilerParams(vmem_limit_bytes=VMEM_LIMIT),
        name="late_product",
    )(meta, acc, amp_all, *blocks)


def body(amplitudes, integrals, pair_count, pair_sym, vir_sym, out_sym):
    rows, cols = amplitudes.shape[1], integrals.shape[1]
    n_row, n_col = lax.axis_size("row"), lax.axis_size("col")
    k_tiles = vir_sym.shape[0]
    n_y = n_col // 4
    amp, block, meta = pack(amplitudes, integrals, pair_count, pair_sym, vir_sym, out_sym)

    def send(a, axis, hops, name):
        with jax.named_scope(name):
            return lax.ppermute(a, axis, hops)

    def across(a):
        return send(a, "col", [(c, (c + n_col // 2) % n_col) for c in range(n_col)], "across_x")

    def swap(a):
        return send(a, "col", [(c, c ^ 1) for c in range(n_col)], "swap_cores")

    def from_y(a, d):
        hops = [(c, c ^ (2 * d)) for c in range(n_col)]
        return send(a, "col", hops, f"from_y_{d}")

    def up(a, name):
        return send(a, "row", [(i, (i + 1) % n_row) for i in range(n_row)], "up_" + name)

    def down(a, name):
        return send(a, "row", [(i, (i - 1) % n_row) for i in range(n_row)], "down_" + name)

    def swap_slabs(a, step):
        return send(a, "slab", [(0, 1), (1, 0)], f"swap_slabs_{step}")

    half = TILE // 2
    other = swap_slabs(block, 0)
    below, above = up(block, "own_1"), down(block, "own_1")
    amp_two = join([amp, across(amp)], needed=[other], name="join_two")
    both = join([below, above], needed=[amp_two], name="join_own_1")
    both_1, others_1 = both, swap_slabs(both, 1)
    below, above = up(join([(both, 0, TILE)], name="split"), "own_2"), down(join([(both, TILE, TILE)], name="split"), "own_2")
    amps = {0: amp_two, 1: from_y(amp_two, 1), 3: from_y(amp_two, 3)}
    both_2 = join([below, above], name="join_own_2")
    others_2 = swap_slabs(both_2, 2)
    below, above = up(join([(both_2, 0, TILE)], name="split"), "own_3"), down(join([(both_2, TILE, TILE)], name="split"), "own_3")
    amps[2] = from_y(join([amp_two], needed=[amps[1], amps[3], others_1], name="hold"), 2)
    both_3 = join([below, above], needed=[amps[1], amps[3]], name="join_own_3")
    low = up(join([(both_3, 0, half)], name="split"), "own_half")
    high = down(join([(both_3, TILE + half, half)], name="split"), "own_half")
    own_4 = join([low, high], needed=[others_2], name="join_own_4")
    other_4 = swap_slabs(own_4, 4)
    other_below = up(join([(others_2, 0, TILE)], name="split"), "other_3")
    other_above = down(join([(others_2, TILE, TILE)], name="split"), "other_3")

    own = join([amps[y] for y in range(n_y)], needed=[own_4], name="join_y")
    amps = [own, swap(own)]
    first = {
        ((0, 0),): block,
        ((0, 1),): other,
        ((-1, 0), (1, 0)): both_1,
        ((-1, 1), (1, 1)): others_1,
        ((-2, 0), (2, 0)): both_2,
        ((-2, 1), (2, 1)): others_2,
        ((-3, 0), (3, 0)): both_3,
    }
    last = {((-4, 0),): own_4, ((-3, 1),): other_below, ((3, 1),): other_above, ((-4, 1),): other_4}
    acc, amp_all = early(rows, cols, k_tiles, list(first), meta, amps, list(first.values()))
    return late(rows, cols, k_tiles, list(last), meta, acc, amp_all, list(last.values()))


def solution(mesh):
    in_specs = (
        P("slab", "row", "col"),
        P(("row", "slab"), "col"),
        P(),
        P("slab", "row"),
        P(),
        P("col"),
    )
    out_specs = P("slab", "row", "col")
    return jax.shard_map(body, mesh=mesh, in_specs=in_specs, out_specs=out_specs, check_vma=False)
```

time: 61.1 us -> 56 us (0.917); the launches traced: 61.2 us -> 55 us
  waiting for transfers between devices: 20.5 us -> 8.67 us
  starting transfers between devices: 29.8 us -> 35.6 us
    ppermute x20 -> x19, waiting for transfers between devices: 20.5 us -> 8.67 us  [send(): return lax.ppermute(a, axis, hops)]
    ppermute x20 -> x19, starting transfers between devices: 29.8 us -> 35.6 us  [send(): return lax.ppermute(a, axis, hops)]
    pallas_call x3 -> x16, Pallas kernels: 3.99 us -> 4.09 us  [the longest x1 3.79 us: early(): pl.pallas_call(functools.partial(early_kernel, pairs, n_amp, rows // 2),...]
  transfers between devices with their start and end apart: 20 -> 19, of which waited for: 9 -> 9; matrix products, arithmetic and copies ran while one was open for 0% -> 0% of each run, Pallas kernels for 6% -> 7%
where the time goes in v3:
time: 56 us; the launch traced here: 55 us
  starting transfers between devices  35.6 us (64%)
  Pallas kernels  9.38 us (17%)
  waiting for transfers between devices  8.67 us (15%)
  local copies, waits for them, and re-layouts  0.92 us (2%)
    ppermute x19, starting transfers between devices, send(): return lax.ppermute(a, axis, hops)  35.6 us
    ppermute x19, waiting for transfers between devices, send(): return lax.ppermute(a, axis, hops)  8.67 us
    pallas_call x1, Pallas kernels, early(): pl.pallas_call(functools.partial(early_kernel, pairs, n_amp, rows // 2),...  3.79 us
    pallas_call x1, Pallas kernels, late(): pl.pallas_call(functools.partial(late_kernel, pairs, (k_tiles, mt, nt)),...  3.26 us
    pallas_call x1, Pallas kernels, pack(): pl.pallas_call(functools.partial(pack_kernel, rows), out_shape=(jax.Shape...  2.03 us
  transfers between devices with their start and end apart: 19, of which 9 were waited for; matrix products, arithmetic and copies ran while one was open for 0% of the time, Pallas kernels for 7%

profile of v3, /device:TPU:1, one launch (start us, length us, event | category | flops | bytes accessed | tf_op | source)
XLA Modules:
  0.0 55.0 jit_solution(16674095819434743864)
XLA Ops:
  0.0 2.0 %pack.1 = (bf16[512,128]{1,0:T(8,128)(2,1)}, bf16[128,768]{1,0:T(8,128)(2,1)}, s32[37]{0:T(128)}) custom-call(s32[2]{0:T(128)} %pair_count.1, s32[1,8]{1,0:T(1,128)} %pair_tiles.1, s32[16]{0:T(128)} %vir.1, s32[12]{0:T(128)} %out_tiles.1, bf16[1,1024,128]{2,1,0:T(8,128)(2,1)} %amp.1, bf16[128,1536]{1,0:T(8,128)(2,1)} %ints.1), custom_call_target="tpu_custom_call" | custom-call | tf_op jit(solution)/shard_map/pack/pallas_call | solution.py:55
  2.0 2.1 %collective-permute-start.1 = (bf16[128,768]{1,0:T(8,128)(2,1)}, bf16[128,768]{1,0:T(8,128)(2,1)S(1)}, u32[]{:S(2)}, u32[]{:S(2)}) collective-permute-start(bf16[128,768]{1,0:T(8,128)(2,1)} %get-tuple-element.12.refs_3_), channel_id=1, source_target_pairs={{0,1},{1,0},{2,3},{3,2},{4,5},{5,4},{6,7},{7,6},{8,9},{9,8},{10,11... | collective-permute-start | bytes 589832 | tf_op jit(solution)/shard_map/swap_slabs_0/ppermute | solution.py:255
  4.2 1.6 %collective-permute-start.4 = (bf16[128,768]{1,0:T(8,128)(2,1)}, bf16[128,768]{1,0:T(8,128)(2,1)S(1)}, u32[]{:S(2)}, u32[]{:S(2)}) collective-permute-start(bf16[128,768]{1,0:T(8,128)(2,1)} %get-tuple-element.12.refs_3_), channel_id=1, source_target_pairs={{0,32},{32,64},{64,96},{96,128},{128,160},{160,192},{192,224},{224... | collective-permute-start | bytes 589832 | tf_op jit(solution)/shard_map/up_own_1/ppermute | solution.py:255
  5.8 3.9 %collective-permute-start.5 = (bf16[128,768]{1,0:T(8,128)(2,1)}, bf16[128,768]{1,0:T(8,128)(2,1)S(1)}, u32[]{:S(2)}, u32[]{:S(2)}) collective-permute-start(bf16[128,768]{1,0:T(8,128)(2,1)} %get-tuple-element.12.refs_3_), channel_id=1, source_target_pairs={{0,224},{32,0},{64,32},{96,64},{128,96},{160,128},{192,160},{224,1... | collective-permute-start | bytes 589832 | tf_op jit(solution)/shard_map/down_own_1/ppermute | solution.py:255
  9.7 2.5 %collective-permute-start = (bf16[512,128]{1,0:T(8,128)(2,1)}, bf16[512,128]{1,0:T(8,128)(2,1)S(1)}, u32[]{:S(2)}, u32[]{:S(2)}) collective-permute-start(bf16[512,128]{1,0:T(8,128)(2,1)} %get-tuple-element.11.refs_0_), channel_id=1, source_target_pairs={{0,16},{2,18},{4,20},{6,22},{8,24},{10,26},{12,28},{14,30},{16,0},... | collective-permute-start | bytes 393224 | tf_op jit(solution)/shard_map/across_x/ppermute | solution.py:255
  12.2 3.1 %collective-permute-done.refs_1_ = bf16[512,128]{1,0:T(8,128)(2,1)S(1)} collective-permute-done((bf16[512,128]{1,0:T(8,128)(2,1)}, bf16[512,128]{1,0:T(8,128)(2,1)S(1)}, u32[]{:S(2)}, u32[]{:S(2)}) %collective-permute-start) | collective-permute-done | bytes 131104 | tf_op jit(solution)/shard_map/across_x/ppermute | solution.py:255
  15.3 0.9 %copy-done.1 = bf16[512,128]{1,0:T(8,128)(2,1)S(1)} copy-done((bf16[512,128]{1,0:T(8,128)(2,1)S(1)}, bf16[512,128]{1,0:T(8,128)(2,1)}, u32[]{:S(2)}) %copy-start.1) | copy-done | bytes 131096
  16.3 0.5 collective-permute-start.6
  16.8 0.1 collective-permute-start.8
  16.9 3.9 %collective-permute-start.9 = (bf16[128,768]{1,0:T(8,128)(2,1)S(1)}, bf16[128,768]{1,0:T(8,128)(2,1)S(1)}, u32[]{:S(2)}, u32[]{:S(2)}) collective-permute-start(bf16[128,768]{1,0:T(8,128)(2,1)S(1)} %split.9), channel_id=1, source_target_pairs={{0,224},{32,0},{64,32},{96,64},{128,96},{160,128},{192,160},{224,1... | collective-permute-start | bytes 589832 | tf_op jit(solution)/shard_map/down_own_2/ppermute | solution.py:255
  20.8 1.3 %collective-permute-start.2 = (bf16[1024,128]{1,0:T(8,128)(2,1)S(1)}, bf16[1024,128]{1,0:T(8,128)(2,1)S(1)}, u32[]{:S(2)}, u32[]{:S(2)}) collective-permute-start(bf16[1024,128]{1,0:T(8,128)(2,1)S(1)} %join_two.1.refs_2_.refs_0_), channel_id=1, source_target_pairs={{0,4},{2,6},{4,0},{6,2},{8,12},{10,14},{12,8},{14,10},{16,20},{18,... | collective-permute-start | bytes 786440 | tf_op jit(solution)/shard_map/from_y_1/ppermute | solution.py:255
  22.1 1.9 %collective-permute-start.3 = (bf16[1024,128]{1,0:T(8,128)(2,1)S(1)}, bf16[1024,128]{1,0:T(8,128)(2,1)S(1)}, u32[]{:S(2)}, u32[]{:S(2)}) collective-permute-start(bf16[1024,128]{1,0:T(8,128)(2,1)S(1)} %join_two.1.refs_2_.refs_0_), channel_id=1, source_target_pairs={{0,12},{2,14},{4,8},{6,10},{8,4},{10,6},{12,0},{14,2},{16,28},{18,... | collective-permute-start | bytes 786440 | tf_op jit(solution)/shard_map/from_y_3/ppermute | solution.py:255
  24.0 0.2 collective-permute-done.8.refs_0_
  24.2 1.5 %collective-permute-start.14 = (bf16[256,768]{1,0:T(8,128)(2,1)S(1)}, bf16[256,768]{1,0:T(8,128)(2,1)S(1)}, u32[]{:S(2)}, u32[]{:S(2)}) collective-permute-start(bf16[256,768]{1,0:T(8,128)(2,1)S(1)} %join_own_2.1.refs_0_.refs_7_), channel_id=1, source_target_pairs={{0,1},{1,0},{2,3},{3,2},{4,5},{5,4},{6,7},{7,6},{8,9},{9,8},{10,11... | collective-permute-start | bytes 1179656 | tf_op jit(solution)/shard_map/swap_slabs_2/ppermute | solution.py:255
  25.7 0.1 collective-permute-start.10
  25.8 0.8 %collective-permute-done.2.refs_1_.refs_2_ = bf16[1024,128]{1,0:T(8,128)(2,1)S(1)} collective-permute-done((bf16[1024,128]{1,0:T(8,128)(2,1)S(1)}, bf16[1024,128]{1,0:T(8,128)(2,1)S(1)}, u32[]{:S(2)}, u32[]{:S(2)}) %collective-permute-start.2) | collective-permute-done | bytes 262176 | tf_op jit(solution)/shard_map/from_y_1/ppermute | solution.py:255
  26.6 1.9 %collective-permute-start.11 = (bf16[128,768]{1,0:T(8,128)(2,1)S(1)}, bf16[128,768]{1,0:T(8,128)(2,1)S(1)}, u32[]{:S(2)}, u32[]{:S(2)}) collective-permute-start(bf16[128,768]{1,0:T(8,128)(2,1)S(1)} %split.11), channel_id=1, source_target_pairs={{0,224},{32,0},{64,32},{96,64},{128,96},{160,128},{192,160},{224,1... | collective-permute-start | bytes 589832 | tf_op jit(solution)/shard_map/down_own_3/ppermute | solution.py:255
  28.5 0.1 collective-permute-done.3.refs_2_.refs_3_
  28.6 2.9 %collective-permute-start.7 = (bf16[1024,128]{1,0:T(8,128)(2,1)S(1)}, bf16[1024,128]{1,0:T(8,128)(2,1)S(1)}, u32[]{:S(2)}, u32[]{:S(2)}) collective-permute-start(bf16[1024,128]{1,0:T(8,128)(2,1)S(1)} %hold.1), channel_id=1, source_target_pairs={{0,8},{2,10},{4,12},{6,14},{8,0},{10,2},{12,4},{14,6},{16,24},{18,... | collective-permute-start | bytes 786440 | tf_op jit(solution)/shard_map/from_y_2/ppermute | solution.py:255
  31.5 0.1 collective-permute-done.10.refs_0_
  31.7 2.2 %collective-permute-start.12 = (bf16[64,768]{1,0:T(8,128)(2,1)S(1)}, bf16[64,768]{1,0:T(8,128)(2,1)S(1)}, u32[]{:S(2)}, u32[]{:S(2)}) collective-permute-start(bf16[64,768]{1,0:T(8,128)(2,1)S(1)} %split.12), channel_id=1, source_target_pairs={{0,32},{32,64},{64,96},{96,128},{128,160},{160,192},{192,224},{224... | collective-permute-start | bytes 294920 | tf_op jit(solution)/shard_map/up_own_half/ppermute | solution.py:255
  33.9 0.5 collective-permute-start.13
  34.5 2.0 %collective-permute-done.12.refs_0_ = bf16[64,768]{1,0:T(8,128)(2,1)S(1)} collective-permute-done((bf16[64,768]{1,0:T(8,128)(2,1)S(1)}, bf16[64,768]{1,0:T(8,128)(2,1)S(1)}, u32[]{:S(2)}, u32[]{:S(2)}) %collective-permute-start.12) | collective-permute-done | bytes 98336 | tf_op jit(solution)/shard_map/up_own_half/ppermute | solution.py:255
  36.5 1.2 %collective-permute-done.13.refs_1_ = bf16[64,768]{1,0:T(8,128)(2,1)S(1)} collective-permute-done((bf16[64,768]{1,0:T(8,128)(2,1)S(1)}, bf16[64,768]{1,0:T(8,128)(2,1)S(1)}, u32[]{:S(2)}, u32[]{:S(2)}) %collective-permute-start.13) | collective-permute-done | bytes 98336 | tf_op jit(solution)/shard_map/down_own_half/ppermute | solution.py:255
  37.7 0.1 join_y.1.refs_1_
  37.8 5.7 %collective-permute-start.15 = (bf16[4096,128]{1,0:T(8,128)(2,1)S(1)}, bf16[4096,128]{1,0:T(8,128)(2,1)S(1)}, u32[]{:S(2)}, u32[]{:S(2)}) collective-permute-start(bf16[4096,128]{1,0:T(8,128)(2,1)S(1)} %join_y.1.refs_1_), channel_id=1, source_target_pairs={{0,2},{2,0},{4,6},{6,4},{8,10},{10,8},{12,14},{14,12},{16,18},{18,... | collective-permute-start | bytes 3145736 | tf_op jit(solution)/shard_map/swap_cores/ppermute | solution.py:255
  43.5 2.0 %collective-permute-start.16 = (bf16[128,768]{1,0:T(8,128)(2,1)S(1)}, bf16[128,768]{1,0:T(8,128)(2,1)S(1)}, u32[]{:S(2)}, u32[]{:S(2)}) collective-permute-start(bf16[128,768]{1,0:T(8,128)(2,1)S(1)} %split.14), channel_id=1, source_target_pairs={{0,32},{32,64},{64,96},{96,128},{128,160},{160,192},{192,224},{224... | collective-permute-start | bytes 589832 | tf_op jit(solution)/shard_map/up_other_3/ppermute | solution.py:255
  45.5 1.0 %collective-permute-start.17 = (bf16[128,768]{1,0:T(8,128)(2,1)S(1)}, bf16[128,768]{1,0:T(8,128)(2,1)S(1)}, u32[]{:S(2)}, u32[]{:S(2)}) collective-permute-start(bf16[128,768]{1,0:T(8,128)(2,1)S(1)} %split.15), channel_id=1, source_target_pairs={{0,224},{32,0},{64,32},{96,64},{128,96},{160,128},{192,160},{224,1... | collective-permute-start | bytes 589832 | tf_op jit(solution)/shard_map/down_other_3/ppermute | solution.py:255
  46.5 3.8 %early_product.1 = (f32[2,512,768]{2,1,0:T(8,128)S(1)}, bf16[17,512,128]{2,1,0:T(8,128)(2,1)S(1)}) custom-call(s32[37]{0:T(128)S(1)} %copy-done.2, bf16[4096,128]{1,0:T(8,128)(2,1)S(1)} %join_y.1.refs_1_, bf16[4096,128]{1,0:T(8,128)(2,1)S(1)} %collective-permute-done.15.refs_2_, bf16[128,768]{1,0:T(8,128)(2,1)S(1)} %copy-done, ...), custom_call_target="tpu_custom_call" | custom-call | tf_op jit(solution)/shard_map/early_product/pallas_call | solution.py:165
  50.3 0.9 %collective-permute-done.16.refs_4_ = bf16[128,768]{1,0:T(8,128)(2,1)S(1)} collective-permute-done((bf16[128,768]{1,0:T(8,128)(2,1)S(1)}, bf16[128,768]{1,0:T(8,128)(2,1)S(1)}, u32[]{:S(2)}, u32[]{:S(2)}) %collective-permute-start.16) | collective-permute-done | bytes 196640 | tf_op jit(solution)/shard_map/up_other_3/ppermute | solution.py:255
  51.2 0.3 collective-permute-done.17.refs_5_
  51.5 3.3 %late_product.1 = bf16[1,1024,1536]{2,1,0:T(8,128)(2,1)} custom-call(s32[37]{0:T(128)S(1)} %copy-done.2, f32[2,512,768]{2,1,0:T(8,128)S(1)} %get-tuple-element.13.refs_1_, bf16[17,512,128]{2,1,0:T(8,128)(2,1)S(1)} %get-tuple-element.14.refs_2_, bf16[128,768]{1,0:T(8,128)(2,1)S(1)} %join_own_4.1.refs_4_.refs_3_, ...), custom_call_target="tpu_custom_call" | custom-call | tf_op jit(solution)/shard_map/late_product/pallas_call | solution.py:228
  (30 shorter events, 0.3 us)
Async XLA Ops:
  2.0 13.2 %collective-permute-start.1 = (bf16[128,768]{1,0:T(8,128)(2,1)}, bf16[128,768]{1,0:T(8,128)(2,1)S(1)}, u32[]{:S(2)}, u32[]{:S(2)}) collective-permute-start(bf16[128,768]{1,0:T(8,128)(2,1)} %get-tuple-element.12.refs_3_), channel_id=1, source_target_pairs={{0,1},{1,0},{2,3},{3,2},{4,5},{5,4},{6,7},{7,6},{8,9},{9,8},{10,11... | collective-permute-start | bytes 589832 | tf_op jit(solution)/shard_map/swap_slabs_0/ppermute | solution.py:255
  4.2 12.0 %collective-permute-start.4 = (bf16[128,768]{1,0:T(8,128)(2,1)}, bf16[128,768]{1,0:T(8,128)(2,1)S(1)}, u32[]{:S(2)}, u32[]{:S(2)}) collective-permute-start(bf16[128,768]{1,0:T(8,128)(2,1)} %get-tuple-element.12.refs_3_), channel_id=1, source_target_pairs={{0,32},{32,64},{64,96},{96,128},{128,160},{160,192},{192,224},{224... | collective-permute-start | bytes 589832 | tf_op jit(solution)/shard_map/up_own_1/ppermute | solution.py:255
  5.8 10.4 %collective-permute-start.5 = (bf16[128,768]{1,0:T(8,128)(2,1)}, bf16[128,768]{1,0:T(8,128)(2,1)S(1)}, u32[]{:S(2)}, u32[]{:S(2)}) collective-permute-start(bf16[128,768]{1,0:T(8,128)(2,1)} %get-tuple-element.12.refs_3_), channel_id=1, source_target_pairs={{0,224},{32,0},{64,32},{96,64},{128,96},{160,128},{192,160},{224,1... | collective-permute-start | bytes 589832 | tf_op jit(solution)/shard_map/down_own_1/ppermute | solution.py:255
  9.7 5.5 %collective-permute-start = (bf16[512,128]{1,0:T(8,128)(2,1)}, bf16[512,128]{1,0:T(8,128)(2,1)S(1)}, u32[]{:S(2)}, u32[]{:S(2)}) collective-permute-start(bf16[512,128]{1,0:T(8,128)(2,1)} %get-tuple-element.11.refs_0_), channel_id=1, source_target_pairs={{0,16},{2,18},{4,20},{6,22},{8,24},{10,26},{12,28},{14,30},{16,0},... | collective-permute-start | bytes 393224 | tf_op jit(solution)/shard_map/across_x/ppermute | solution.py:255
  15.3 0.9 %copy-start.1 = (bf16[512,128]{1,0:T(8,128)(2,1)S(1)}, bf16[512,128]{1,0:T(8,128)(2,1)}, u32[]{:S(2)}) copy-start(bf16[512,128]{1,0:T(8,128)(2,1)} %get-tuple-element.11.refs_0_) | copy-start | bytes 393220
  16.3 12.3 %collective-permute-start.6 = (bf16[256,768]{1,0:T(8,128)(2,1)S(1)}, bf16[256,768]{1,0:T(8,128)(2,1)S(1)}, u32[]{:S(2)}, u32[]{:S(2)}) collective-permute-start(bf16[256,768]{1,0:T(8,128)(2,1)S(1)} %join_own_1.1.refs_0_.refs_5_), channel_id=1, source_target_pairs={{0,1},{1,0},{2,3},{3,2},{4,5},{5,4},{6,7},{7,6},{8,9},{9,8},{10,11... | collective-permute-start | bytes 1179656 | tf_op jit(solution)/shard_map/swap_slabs_1/ppermute | solution.py:255
  16.8 7.4 %collective-permute-start.8 = (bf16[128,768]{1,0:T(8,128)(2,1)S(1)}, bf16[128,768]{1,0:T(8,128)(2,1)S(1)}, u32[]{:S(2)}, u32[]{:S(2)}) collective-permute-start(bf16[128,768]{1,0:T(8,128)(2,1)S(1)} %split.8), channel_id=1, source_target_pairs={{0,32},{32,64},{64,96},{96,128},{128,160},{160,192},{192,224},{224... | collective-permute-start | bytes 589832 | tf_op jit(solution)/shard_map/up_own_2/ppermute | solution.py:255
  16.9 7.3 %collective-permute-start.9 = (bf16[128,768]{1,0:T(8,128)(2,1)S(1)}, bf16[128,768]{1,0:T(8,128)(2,1)S(1)}, u32[]{:S(2)}, u32[]{:S(2)}) collective-permute-start(bf16[128,768]{1,0:T(8,128)(2,1)S(1)} %split.9), channel_id=1, source_target_pairs={{0,224},{32,0},{64,32},{96,64},{128,96},{160,128},{192,160},{224,1... | collective-permute-start | bytes 589832 | tf_op jit(solution)/shard_map/down_own_2/ppermute | solution.py:255
  20.8 5.8 %collective-permute-start.2 = (bf16[1024,128]{1,0:T(8,128)(2,1)S(1)}, bf16[1024,128]{1,0:T(8,128)(2,1)S(1)}, u32[]{:S(2)}, u32[]{:S(2)}) collective-permute-start(bf16[1024,128]{1,0:T(8,128)(2,1)S(1)} %join_two.1.refs_2_.refs_0_), channel_id=1, source_target_pairs={{0,4},{2,6},{4,0},{6,2},{8,12},{10,14},{12,8},{14,10},{16,20},{18,... | collective-permute-start | bytes 786440 | tf_op jit(solution)/shard_map/from_y_1/ppermute | solution.py:255
  22.1 6.4 %collective-permute-start.3 = (bf16[1024,128]{1,0:T(8,128)(2,1)S(1)}, bf16[1024,128]{1,0:T(8,128)(2,1)S(1)}, u32[]{:S(2)}, u32[]{:S(2)}) collective-permute-start(bf16[1024,128]{1,0:T(8,128)(2,1)S(1)} %join_two.1.refs_2_.refs_0_), channel_id=1, source_target_pairs={{0,12},{2,14},{4,8},{6,10},{8,4},{10,6},{12,0},{14,2},{16,28},{18,... | collective-permute-start | bytes 786440 | tf_op jit(solution)/shard_map/from_y_3/ppermute | solution.py:255
  24.2 13.5 %collective-permute-start.14 = (bf16[256,768]{1,0:T(8,128)(2,1)S(1)}, bf16[256,768]{1,0:T(8,128)(2,1)S(1)}, u32[]{:S(2)}, u32[]{:S(2)}) collective-permute-start(bf16[256,768]{1,0:T(8,128)(2,1)S(1)} %join_own_2.1.refs_0_.refs_7_), channel_id=1, source_target_pairs={{0,1},{1,0},{2,3},{3,2},{4,5},{5,4},{6,7},{7,6},{8,9},{9,8},{10,11... | collective-permute-start | bytes 1179656 | tf_op jit(solution)/shard_map/swap_slabs_2/ppermute | solution.py:255
  25.7 5.9 %collective-permute-start.10 = (bf16[128,768]{1,0:T(8,128)(2,1)S(1)}, bf16[128,768]{1,0:T(8,128)(2,1)S(1)}, u32[]{:S(2)}, u32[]{:S(2)}) collective-permute-start(bf16[128,768]{1,0:T(8,128)(2,1)S(1)} %split.10), channel_id=1, source_target_pairs={{0,32},{32,64},{64,96},{96,128},{128,160},{160,192},{192,224},{224... | collective-permute-start | bytes 589832 | tf_op jit(solution)/shard_map/up_own_3/ppermute | solution.py:255
  26.6 5.1 %collective-permute-start.11 = (bf16[128,768]{1,0:T(8,128)(2,1)S(1)}, bf16[128,768]{1,0:T(8,128)(2,1)S(1)}, u32[]{:S(2)}, u32[]{:S(2)}) collective-permute-start(bf16[128,768]{1,0:T(8,128)(2,1)S(1)} %split.11), channel_id=1, source_target_pairs={{0,224},{32,0},{64,32},{96,64},{128,96},{160,128},{192,160},{224,1... | collective-permute-start | bytes 589832 | tf_op jit(solution)/shard_map/down_own_3/ppermute | solution.py:255
  28.6 18.0 %copy-start = (bf16[128,768]{1,0:T(8,128)(2,1)S(1)}, bf16[128,768]{1,0:T(8,128)(2,1)}, u32[]{:S(2)}) copy-start(bf16[128,768]{1,0:T(8,128)(2,1)} %get-tuple-element.12.refs_3_) | copy-start | bytes 589828
  28.6 18.0 %copy-start.2 = (s32[37]{0:T(128)S(1)}, s32[37]{0:T(128)}, u32[]{:S(2)}) copy-start(s32[37]{0:T(128)} %get-tuple-element.10.refs_0_) | copy-start | bytes 448
  28.6 9.1 %collective-permute-start.7 = (bf16[1024,128]{1,0:T(8,128)(2,1)S(1)}, bf16[1024,128]{1,0:T(8,128)(2,1)S(1)}, u32[]{:S(2)}, u32[]{:S(2)}) collective-permute-start(bf16[1024,128]{1,0:T(8,128)(2,1)S(1)} %hold.1), channel_id=1, source_target_pairs={{0,8},{2,10},{4,12},{6,14},{8,0},{10,2},{12,4},{14,6},{16,24},{18,... | collective-permute-start | bytes 786440 | tf_op jit(solution)/shard_map/from_y_2/ppermute | solution.py:255
  31.7 4.8 %collective-permute-start.12 = (bf16[64,768]{1,0:T(8,128)(2,1)S(1)}, bf16[64,768]{1,0:T(8,128)(2,1)S(1)}, u32[]{:S(2)}, u32[]{:S(2)}) collective-permute-start(bf16[64,768]{1,0:T(8,128)(2,1)S(1)} %split.12), channel_id=1, source_target_pairs={{0,32},{32,64},{64,96},{96,128},{128,160},{160,192},{192,224},{224... | collective-permute-start | bytes 294920 | tf_op jit(solution)/shard_map/up_own_half/ppermute | solution.py:255
  33.9 3.8 %collective-permute-start.13 = (bf16[64,768]{1,0:T(8,128)(2,1)S(1)}, bf16[64,768]{1,0:T(8,128)(2,1)S(1)}, u32[]{:S(2)}, u32[]{:S(2)}) collective-permute-start(bf16[64,768]{1,0:T(8,128)(2,1)S(1)} %split.13), channel_id=1, source_target_pairs={{0,224},{32,0},{64,32},{96,64},{128,96},{160,128},{192,160},{224,1... | collective-permute-start | bytes 294920 | tf_op jit(solution)/shard_map/down_own_half/ppermute | solution.py:255
  37.8 8.7 %collective-permute-start.15 = (bf16[4096,128]{1,0:T(8,128)(2,1)S(1)}, bf16[4096,128]{1,0:T(8,128)(2,1)S(1)}, u32[]{:S(2)}, u32[]{:S(2)}) collective-permute-start(bf16[4096,128]{1,0:T(8,128)(2,1)S(1)} %join_y.1.refs_1_), channel_id=1, source_target_pairs={{0,2},{2,0},{4,6},{6,4},{8,10},{10,8},{12,14},{14,12},{16,18},{18,... | collective-permute-start | bytes 3145736 | tf_op jit(solution)/shard_map/swap_cores/ppermute | solution.py:255
  43.5 6.9 %collective-permute-start.18 = (bf16[128,768]{1,0:T(8,128)(2,1)S(1)}, bf16[128,768]{1,0:T(8,128)(2,1)S(1)}, u32[]{:S(2)}, u32[]{:S(2)}) collective-permute-start(bf16[128,768]{1,0:T(8,128)(2,1)S(1)} %join_own_4.1.refs_4_.refs_3_), channel_id=1, source_target_pairs={{0,1},{1,0},{2,3},{3,2},{4,5},{5,4},{6,7},{7,6},{8,9},{9,8},{10,11... | collective-permute-start | bytes 589832 | tf_op jit(solution)/shard_map/swap_slabs_4/ppermute | solution.py:255
  43.5 7.7 %collective-permute-start.16 = (bf16[128,768]{1,0:T(8,128)(2,1)S(1)}, bf16[128,768]{1,0:T(8,128)(2,1)S(1)}, u32[]{:S(2)}, u32[]{:S(2)}) collective-permute-start(bf16[128,768]{1,0:T(8,128)(2,1)S(1)} %split.14), channel_id=1, source_target_pairs={{0,32},{32,64},{64,96},{96,128},{128,160},{160,192},{192,224},{224... | collective-permute-start | bytes 589832 | tf_op jit(solution)/shard_map/up_other_3/ppermute | solution.py:255
  45.5 6.0 %collective-permute-start.17 = (bf16[128,768]{1,0:T(8,128)(2,1)S(1)}, bf16[128,768]{1,0:T(8,128)(2,1)S(1)}, u32[]{:S(2)}, u32[]{:S(2)}) collective-permute-start(bf16[128,768]{1,0:T(8,128)(2,1)S(1)} %split.15), channel_id=1, source_target_pairs={{0,224},{32,0},{64,32},{96,64},{128,96},{160,128},{192,160},{224,1... | collective-permute-start | bytes 589832 | tf_op jit(solution)/shard_map/down_other_3/ppermute | solution.py:255

commit v4 on v3

--- a/solution.py
+++ b/solution.py
@@ -65,7 +65,7 @@
     )(pair_count, pair_sym, vir_sym, out_sym, amplitudes, integrals)
 
 
-def join(parts, needed=(), name="join"):
+def join(parts, needed=(), name="join", flops=0):
     parts = [part if isinstance(part, tuple) else (part, 0, part.shape[0]) for part in parts]
     n = len(parts)
     height, width = sum(part[2] for part in parts), parts[0][0].shape[1]
@@ -83,6 +83,7 @@
         in_specs=[VMEM] * n + [ANY] * len(needed),
         out_specs=VMEM,
         compiler_params=pltpu.CompilerParams(vmem_limit_bytes=SMALL_LIMIT),
+        cost_estimate=pl.CostEstimate(flops=flops, bytes_accessed=0, transcendentals=0) if flops else None,
         name=name,
     )(*[part[0] for part in parts], *needed)
 
@@ -183,7 +184,6 @@
     int_buf, order, acc, out_buf, row_at, col_at, out_sem = refs[4 + n :]
     zero_chunks, chunks = gather_tiles(pairs, meta, blocks, order, int_buf, k_tiles)
 
-    out_buf[...] = jnp.zeros(out_buf.shape, out_buf.dtype)
     for place, count, base in ((row_at, mt, k_tiles), (col_at, nt, k_tiles + mt)):
         nzero, none = jnp.int32(0), jnp.int32(0)
         for tile in range(count):
@@ -194,11 +194,18 @@
 
     live = meta[k_tiles + mt + nt]
     for group in range(2):
-        acc[...] = acc_in[group]
         first = 0 if group == 0 else zero_chunks
         last = zero_chunks if group == 0 else chunks
 
-        @pl.loop(first, last)
+        @pl.when(first == last)
+        def _():
+            acc[...] = acc_in[group]
+
+        @pl.when(first < last)
+        def _():
+            acc[...] = acc_in[group] + chunk_product(amp_all, int_buf, order, first)
+
+        @pl.loop(first + 1, last)
         def _(chunk):
             acc[...] += chunk_product(amp_all, int_buf, order, chunk)
 
@@ -210,6 +217,8 @@
                 col_start = pl.multiple_of(col_at[group * (nt // 2) + c] * TILE, TILE)
                 value = acc[r * TILE : (r + 1) * TILE, c * TILE : (c + 1) * TILE]
                 out_buf[pl.ds(row_start, TILE), pl.ds(col_start, TILE)] = jnp.where(keep, value, 0.0).astype(jnp.bfloat16)
+                empty = pl.multiple_of(col_at[(1 - group) * (nt // 2) + c] * TILE, TILE)
+                out_buf[pl.ds(row_start, TILE), pl.ds(empty, TILE)] = jnp.zeros((TILE, TILE), jnp.bfloat16)
             pltpu.make_async_copy(
                 out_buf.at[pl.ds(row_start, TILE)],
                 out.at[0, pl.ds(row_start, TILE)],
@@ -276,16 +285,16 @@
     half = TILE // 2
     other = swap_slabs(block, 0)
     below, above = up(block, "own_1"), down(block, "own_1")
-    amp_two = join([amp, across(amp)], needed=[other], name="join_two")
-    both = join([below, above], needed=[amp_two], name="join_own_1")
+    amp_two = join([join([amp], name="hold"), across(amp)], needed=[other], name="join_two", flops=3000000000)
+    both = join([below, above], needed=[amp_two], name="join_own_1", flops=0)
     both_1, others_1 = both, swap_slabs(both, 1)
     below, above = up(join([(both, 0, TILE)], name="split"), "own_2"), down(join([(both, TILE, TILE)], name="split"), "own_2")
     amps = {0: amp_two, 1: from_y(amp_two, 1), 3: from_y(amp_two, 3)}
-    both_2 = join([below, above], name="join_own_2")
+    both_2 = join([below, above], name="join_own_2", flops=5000000000)
     others_2 = swap_slabs(both_2, 2)
     below, above = up(join([(both_2, 0, TILE)], name="split"), "own_3"), down(join([(both_2, TILE, TILE)], name="split"), "own_3")
-    amps[2] = from_y(join([amp_two], needed=[amps[1], amps[3], others_1], name="hold"), 2)
-    both_3 = join([below, above], needed=[amps[1], amps[3]], name="join_own_3")
+    amps[2] = from_y(join([amp_two], needed=[amps[1], amps[3]], name="hold"), 2)
+    both_3 = join([below, above], needed=[others_1], name="join_own_3", flops=5000000000)
     low = up(join([(both_3, 0, half)], name="split"), "own_half")
     high = down(join([(both_3, TILE + half, half)], name="split"), "own_half")
     own_4 = join([low, high], needed=[others_2], name="join_own_4")

time: 56 us -> 54.1 us (0.966); the launches traced: 55 us -> 54.1 us
  starting transfers between devices: 35.6 us -> 33.7 us
  waiting for transfers between devices: 8.67 us -> 9.98 us
    ppermute x19, starting transfers between devices: 35.6 us -> 33.7 us  [send(): return lax.ppermute(a, axis, hops)]
    ppermute x19, waiting for transfers between devices: 8.67 us -> 9.98 us  [send(): return lax.ppermute(a, axis, hops)]
  transfers between devices with their start and end apart: 19 -> 19, of which waited for: 9 -> 8; matrix products, arithmetic and copies ran while one was open for 0% -> 0% of each run, Pallas kernels for 7% -> 7%
where the time goes in v4:
time: 54.1 us
  starting transfers between devices  33.7 us (62%)
  waiting for transfers between devices  9.98 us (18%)
  Pallas kernels  9.15 us (17%)
  local copies, waits for them, and re-layouts  0.91 us (2%)
    ppermute x19, starting transfers between devices, send(): return lax.ppermute(a, axis, hops)  33.7 us
    ppermute x19, waiting for transfers between devices, send(): return lax.ppermute(a, axis, hops)  9.98 us
    pallas_call x1, Pallas kernels, late(): pl.pallas_call(functools.partial(late_kernel, pairs, (k_tiles, mt, nt)),...  3.41 us
    pallas_call x1, Pallas kernels, early(): pl.pallas_call(functools.partial(early_kernel, pairs, n_amp, rows // 2),...  3.39 us
    pallas_call x1, Pallas kernels, pack(): pl.pallas_call(functools.partial(pack_kernel, rows), out_shape=(jax.Shape...  2.03 us
  transfers between devices with their start and end apart: 19, of which 8 were waited for; matrix products, arithmetic and copies ran while one was open for 0% of the time, Pallas kernels for 7%

profile of v4, /device:TPU:1, one launch (start us, length us, event | category | flops | bytes accessed | tf_op | source)
XLA Modules:
  0.0 54.1 jit_solution(12309075268102416866)
XLA Ops:
  0.0 2.0 %pack.1 = (bf16[512,128]{1,0:T(8,128)(2,1)}, bf16[128,768]{1,0:T(8,128)(2,1)}, s32[37]{0:T(128)}) custom-call(s32[2]{0:T(128)} %pair_count.1, s32[1,8]{1,0:T(1,128)} %pair_tiles.1, s32[16]{0:T(128)} %vir.1, s32[12]{0:T(128)} %out_tiles.1, bf16[1,1024,128]{2,1,0:T(8,128)(2,1)} %amp.1, bf16[128,1536]{1,0:T(8,128)(2,1)} %ints.1), custom_call_target="tpu_custom_call" | custom-call | tf_op jit(solution)/shard_map/pack/pallas_call | solution.py:55
  2.0 2.1 %collective-permute-start.1 = (bf16[128,768]{1,0:T(8,128)(2,1)}, bf16[128,768]{1,0:T(8,128)(2,1)S(1)}, u32[]{:S(2)}, u32[]{:S(2)}) collective-permute-start(bf16[128,768]{1,0:T(8,128)(2,1)} %get-tuple-element.12.refs_3_), channel_id=1, source_target_pairs={{0,1},{1,0},{2,3},{3,2},{4,5},{5,4},{6,7},{7,6},{8,9},{9,8},{10,11... | collective-permute-start | bytes 589832 | tf_op jit(solution)/shard_map/swap_slabs_0/ppermute | solution.py:264
  4.2 2.4 %collective-permute-start = (bf16[512,128]{1,0:T(8,128)(2,1)}, bf16[512,128]{1,0:T(8,128)(2,1)S(1)}, u32[]{:S(2)}, u32[]{:S(2)}) collective-permute-start(bf16[512,128]{1,0:T(8,128)(2,1)} %get-tuple-element.11.refs_0_), channel_id=1, source_target_pairs={{0,16},{2,18},{4,20},{6,22},{8,24},{10,26},{12,28},{14,30},{16,0},... | collective-permute-start | bytes 393224 | tf_op jit(solution)/shard_map/across_x/ppermute | solution.py:264
  6.6 1.6 %collective-permute-start.5 = (bf16[128,768]{1,0:T(8,128)(2,1)}, bf16[128,768]{1,0:T(8,128)(2,1)S(1)}, u32[]{:S(2)}, u32[]{:S(2)}) collective-permute-start(bf16[128,768]{1,0:T(8,128)(2,1)} %get-tuple-element.12.refs_3_), channel_id=1, source_target_pairs={{0,32},{32,64},{64,96},{96,128},{128,160},{160,192},{192,224},{224... | collective-permute-start | bytes 589832 | tf_op jit(solution)/shard_map/up_own_1/ppermute | solution.py:264
  8.3 3.9 %collective-permute-start.6 = (bf16[128,768]{1,0:T(8,128)(2,1)}, bf16[128,768]{1,0:T(8,128)(2,1)S(1)}, u32[]{:S(2)}, u32[]{:S(2)}) collective-permute-start(bf16[128,768]{1,0:T(8,128)(2,1)} %get-tuple-element.12.refs_3_), channel_id=1, source_target_pairs={{0,224},{32,0},{64,32},{96,64},{128,96},{160,128},{192,160},{224,1... | collective-permute-start | bytes 589832 | tf_op jit(solution)/shard_map/down_own_1/ppermute | solution.py:264
  12.2 0.9 %copy-done.1 = bf16[512,128]{1,0:T(8,128)(2,1)S(1)} copy-done((bf16[512,128]{1,0:T(8,128)(2,1)S(1)}, bf16[512,128]{1,0:T(8,128)(2,1)}, u32[]{:S(2)}) %copy-start.1) | copy-done | bytes 131096
  13.1 0.8 %collective-permute-done.refs_1_ = bf16[512,128]{1,0:T(8,128)(2,1)S(1)} collective-permute-done((bf16[512,128]{1,0:T(8,128)(2,1)}, bf16[512,128]{1,0:T(8,128)(2,1)S(1)}, u32[]{:S(2)}, u32[]{:S(2)}) %collective-permute-start) | collective-permute-done | bytes 131104 | tf_op jit(solution)/shard_map/across_x/ppermute | solution.py:264
  14.0 2.4 %collective-permute-done.5.refs_0_ = bf16[128,768]{1,0:T(8,128)(2,1)S(1)} collective-permute-done((bf16[128,768]{1,0:T(8,128)(2,1)}, bf16[128,768]{1,0:T(8,128)(2,1)S(1)}, u32[]{:S(2)}, u32[]{:S(2)}) %collective-permute-start.5) | collective-permute-done | bytes 196640 | tf_op jit(solution)/shard_map/up_own_1/ppermute | solution.py:264
  16.4 0.0 collective-permute-done.6.refs_1_
  16.5 0.1 collective-permute-start.7
  16.6 3.2 %collective-permute-start.8 = (bf16[128,768]{1,0:T(8,128)(2,1)S(1)}, bf16[128,768]{1,0:T(8,128)(2,1)S(1)}, u32[]{:S(2)}, u32[]{:S(2)}) collective-permute-start(bf16[128,768]{1,0:T(8,128)(2,1)S(1)} %split.9), channel_id=1, source_target_pairs={{0,224},{32,0},{64,32},{96,64},{128,96},{160,128},{192,160},{224,1... | collective-permute-start | bytes 589832 | tf_op jit(solution)/shard_map/down_own_2/ppermute | solution.py:264
  19.8 1.3 %collective-permute-start.2 = (bf16[1024,128]{1,0:T(8,128)(2,1)S(1)}, bf16[1024,128]{1,0:T(8,128)(2,1)S(1)}, u32[]{:S(2)}, u32[]{:S(2)}) collective-permute-start(bf16[1024,128]{1,0:T(8,128)(2,1)S(1)} %join_two.1.refs_0_.refs_2_), channel_id=1, source_target_pairs={{0,4},{2,6},{4,0},{6,2},{8,12},{10,14},{12,8},{14,10},{16,20},{18,... | collective-permute-start | bytes 786440 | tf_op jit(solution)/shard_map/from_y_1/ppermute | solution.py:264
  21.1 1.9 %collective-permute-start.3 = (bf16[1024,128]{1,0:T(8,128)(2,1)S(1)}, bf16[1024,128]{1,0:T(8,128)(2,1)S(1)}, u32[]{:S(2)}, u32[]{:S(2)}) collective-permute-start(bf16[1024,128]{1,0:T(8,128)(2,1)S(1)} %join_two.1.refs_0_.refs_2_), channel_id=1, source_target_pairs={{0,12},{2,14},{4,8},{6,10},{8,4},{10,6},{12,0},{14,2},{16,28},{18,... | collective-permute-start | bytes 786440 | tf_op jit(solution)/shard_map/from_y_3/ppermute | solution.py:264
  23.0 0.3 collective-permute-done.7.refs_0_
  23.4 2.6 %collective-permute-start.10 = (bf16[128,768]{1,0:T(8,128)(2,1)S(1)}, bf16[128,768]{1,0:T(8,128)(2,1)S(1)}, u32[]{:S(2)}, u32[]{:S(2)}) collective-permute-start(bf16[128,768]{1,0:T(8,128)(2,1)S(1)} %split.11), channel_id=1, source_target_pairs={{0,224},{32,0},{64,32},{96,64},{128,96},{160,128},{192,160},{224,1... | collective-permute-start | bytes 589832 | tf_op jit(solution)/shard_map/down_own_3/ppermute | solution.py:264
  26.0 0.9 %collective-permute-start.14 = (bf16[256,768]{1,0:T(8,128)(2,1)S(1)}, bf16[256,768]{1,0:T(8,128)(2,1)S(1)}, u32[]{:S(2)}, u32[]{:S(2)}) collective-permute-start(bf16[256,768]{1,0:T(8,128)(2,1)S(1)} %join_own_2.1.refs_0_.refs_7_), channel_id=1, source_target_pairs={{0,1},{1,0},{2,3},{3,2},{4,5},{5,4},{6,7},{7,6},{8,9},{9,8},{10,11... | collective-permute-start | bytes 1179656 | tf_op jit(solution)/shard_map/swap_slabs_2/ppermute | solution.py:264
  26.9 0.6 %collective-permute-done.3.refs_2_.refs_3_ = bf16[1024,128]{1,0:T(8,128)(2,1)S(1)} collective-permute-done((bf16[1024,128]{1,0:T(8,128)(2,1)S(1)}, bf16[1024,128]{1,0:T(8,128)(2,1)S(1)}, u32[]{:S(2)}, u32[]{:S(2)}) %collective-permute-start.3) | collective-permute-done | bytes 262176 | tf_op jit(solution)/shard_map/from_y_3/ppermute | solution.py:264
  27.6 2.4 %collective-permute-start.4 = (bf16[1024,128]{1,0:T(8,128)(2,1)S(1)}, bf16[1024,128]{1,0:T(8,128)(2,1)S(1)}, u32[]{:S(2)}, u32[]{:S(2)}) collective-permute-start(bf16[1024,128]{1,0:T(8,128)(2,1)S(1)} %hold.3), channel_id=1, source_target_pairs={{0,8},{2,10},{4,12},{6,14},{8,0},{10,2},{12,4},{14,6},{16,24},{18,... | collective-permute-start | bytes 786440 | tf_op jit(solution)/shard_map/from_y_2/ppermute | solution.py:264
  30.0 1.8 %collective-permute-done.9.refs_0_ = bf16[128,768]{1,0:T(8,128)(2,1)S(1)} collective-permute-done((bf16[128,768]{1,0:T(8,128)(2,1)S(1)}, bf16[128,768]{1,0:T(8,128)(2,1)S(1)}, u32[]{:S(2)}, u32[]{:S(2)}) %collective-permute-start.9) | collective-permute-done | bytes 196640 | tf_op jit(solution)/shard_map/up_own_3/ppermute | solution.py:264
  31.8 0.0 copy-start
  31.8 0.1 collective-permute-start.12
  31.9 2.7 %collective-permute-start.13 = (bf16[64,768]{1,0:T(8,128)(2,1)S(1)}, bf16[64,768]{1,0:T(8,128)(2,1)S(1)}, u32[]{:S(2)}, u32[]{:S(2)}) collective-permute-start(bf16[64,768]{1,0:T(8,128)(2,1)S(1)} %split.13), channel_id=1, source_target_pairs={{0,224},{32,0},{64,32},{96,64},{128,96},{160,128},{192,160},{224,1... | collective-permute-start | bytes 294920 | tf_op jit(solution)/shard_map/down_own_half/ppermute | solution.py:264
  34.6 2.3 %collective-permute-done.12.refs_0_ = bf16[64,768]{1,0:T(8,128)(2,1)S(1)} collective-permute-done((bf16[64,768]{1,0:T(8,128)(2,1)S(1)}, bf16[64,768]{1,0:T(8,128)(2,1)S(1)}, u32[]{:S(2)}, u32[]{:S(2)}) %collective-permute-start.12) | collective-permute-done | bytes 98336 | tf_op jit(solution)/shard_map/up_own_half/ppermute | solution.py:264
  36.9 0.3 collective-permute-done.14.refs_2_.refs_8_.refs_0_
  37.2 0.1 join_y.1.refs_1_
  37.3 4.5 %collective-permute-start.15 = (bf16[4096,128]{1,0:T(8,128)(2,1)S(1)}, bf16[4096,128]{1,0:T(8,128)(2,1)S(1)}, u32[]{:S(2)}, u32[]{:S(2)}) collective-permute-start(bf16[4096,128]{1,0:T(8,128)(2,1)S(1)} %join_y.1.refs_1_), channel_id=1, source_target_pairs={{0,2},{2,0},{4,6},{6,4},{8,10},{10,8},{12,14},{14,12},{16,18},{18,... | collective-permute-start | bytes 3145736 | tf_op jit(solution)/shard_map/swap_cores/ppermute | solution.py:264
  41.8 0.5 collective-permute-start.18
  42.4 0.5 collective-permute-start.16
  42.9 2.8 %collective-permute-start.17 = (bf16[128,768]{1,0:T(8,128)(2,1)S(1)}, bf16[128,768]{1,0:T(8,128)(2,1)S(1)}, u32[]{:S(2)}, u32[]{:S(2)}) collective-permute-start(bf16[128,768]{1,0:T(8,128)(2,1)S(1)} %split.15), channel_id=1, source_target_pairs={{0,224},{32,0},{64,32},{96,64},{128,96},{160,128},{192,160},{224,1... | collective-permute-start | bytes 589832 | tf_op jit(solution)/shard_map/down_other_3/ppermute | solution.py:264
  45.7 3.4 %early_product.1 = (f32[2,512,768]{2,1,0:T(8,128)S(1)}, bf16[17,512,128]{2,1,0:T(8,128)(2,1)S(1)}) custom-call(s32[37]{0:T(128)S(1)} %copy-done.2, bf16[4096,128]{1,0:T(8,128)(2,1)S(1)} %join_y.1.refs_1_, bf16[4096,128]{1,0:T(8,128)(2,1)S(1)} %collective-permute-done.15.refs_2_, bf16[128,768]{1,0:T(8,128)(2,1)S(1)} %copy-done, ...), custom_call_target="tpu_custom_call" | custom-call | tf_op jit(solution)/shard_map/early_product/pallas_call | solution.py:166
  49.1 1.5 %collective-permute-done.16.refs_4_ = bf16[128,768]{1,0:T(8,128)(2,1)S(1)} collective-permute-done((bf16[128,768]{1,0:T(8,128)(2,1)S(1)}, bf16[128,768]{1,0:T(8,128)(2,1)S(1)}, u32[]{:S(2)}, u32[]{:S(2)}) %collective-permute-start.16) | collective-permute-done | bytes 196640 | tf_op jit(solution)/shard_map/up_other_3/ppermute | solution.py:264
  50.6 3.4 %late_product.1 = bf16[1,1024,1536]{2,1,0:T(8,128)(2,1)} custom-call(s32[37]{0:T(128)S(1)} %copy-done.2, f32[2,512,768]{2,1,0:T(8,128)S(1)} %get-tuple-element.13.refs_1_, bf16[17,512,128]{2,1,0:T(8,128)(2,1)S(1)} %get-tuple-element.14.refs_2_, bf16[128,768]{1,0:T(8,128)(2,1)S(1)} %join_own_4.1.refs_4_.refs_3_, ...), custom_call_target="tpu_custom_call" | custom-call | tf_op jit(solution)/shard_map/late_product/pallas_call | solution.py:237
  (31 shorter events, 0.3 us)
Async XLA Ops:
  2.0 11.9 %collective-permute-start.1 = (bf16[128,768]{1,0:T(8,128)(2,1)}, bf16[128,768]{1,0:T(8,128)(2,1)S(1)}, u32[]{:S(2)}, u32[]{:S(2)}) collective-permute-start(bf16[128,768]{1,0:T(8,128)(2,1)} %get-tuple-element.12.refs_3_), channel_id=1, source_target_pairs={{0,1},{1,0},{2,3},{3,2},{4,5},{5,4},{6,7},{7,6},{8,9},{9,8},{10,11... | collective-permute-start | bytes 589832 | tf_op jit(solution)/shard_map/swap_slabs_0/ppermute | solution.py:264
  4.2 9.8 %collective-permute-start = (bf16[512,128]{1,0:T(8,128)(2,1)}, bf16[512,128]{1,0:T(8,128)(2,1)S(1)}, u32[]{:S(2)}, u32[]{:S(2)}) collective-permute-start(bf16[512,128]{1,0:T(8,128)(2,1)} %get-tuple-element.11.refs_0_), channel_id=1, source_target_pairs={{0,16},{2,18},{4,20},{6,22},{8,24},{10,26},{12,28},{14,30},{16,0},... | collective-permute-start | bytes 393224 | tf_op jit(solution)/shard_map/across_x/ppermute | solution.py:264
  6.6 9.8 %collective-permute-start.5 = (bf16[128,768]{1,0:T(8,128)(2,1)}, bf16[128,768]{1,0:T(8,128)(2,1)S(1)}, u32[]{:S(2)}, u32[]{:S(2)}) collective-permute-start(bf16[128,768]{1,0:T(8,128)(2,1)} %get-tuple-element.12.refs_3_), channel_id=1, source_target_pairs={{0,32},{32,64},{64,96},{96,128},{128,160},{160,192},{192,224},{224... | collective-permute-start | bytes 589832 | tf_op jit(solution)/shard_map/up_own_1/ppermute | solution.py:264
  8.3 8.1 %collective-permute-start.6 = (bf16[128,768]{1,0:T(8,128)(2,1)}, bf16[128,768]{1,0:T(8,128)(2,1)S(1)}, u32[]{:S(2)}, u32[]{:S(2)}) collective-permute-start(bf16[128,768]{1,0:T(8,128)(2,1)} %get-tuple-element.12.refs_3_), channel_id=1, source_target_pairs={{0,224},{32,0},{64,32},{96,64},{128,96},{160,128},{192,160},{224,1... | collective-permute-start | bytes 589832 | tf_op jit(solution)/shard_map/down_own_1/ppermute | solution.py:264
  12.2 0.9 %copy-start.1 = (bf16[512,128]{1,0:T(8,128)(2,1)S(1)}, bf16[512,128]{1,0:T(8,128)(2,1)}, u32[]{:S(2)}) copy-start(bf16[512,128]{1,0:T(8,128)(2,1)} %get-tuple-element.11.refs_0_) | copy-start | bytes 393220
  16.5 6.8 %collective-permute-start.7 = (bf16[128,768]{1,0:T(8,128)(2,1)S(1)}, bf16[128,768]{1,0:T(8,128)(2,1)S(1)}, u32[]{:S(2)}, u32[]{:S(2)}) collective-permute-start(bf16[128,768]{1,0:T(8,128)(2,1)S(1)} %split.8), channel_id=1, source_target_pairs={{0,32},{32,64},{64,96},{96,128},{128,160},{160,192},{192,224},{224... | collective-permute-start | bytes 589832 | tf_op jit(solution)/shard_map/up_own_2/ppermute | solution.py:264
  16.6 6.7 %collective-permute-start.8 = (bf16[128,768]{1,0:T(8,128)(2,1)S(1)}, bf16[128,768]{1,0:T(8,128)(2,1)S(1)}, u32[]{:S(2)}, u32[]{:S(2)}) collective-permute-start(bf16[128,768]{1,0:T(8,128)(2,1)S(1)} %split.9), channel_id=1, source_target_pairs={{0,224},{32,0},{64,32},{96,64},{128,96},{160,128},{192,160},{224,1... | collective-permute-start | bytes 589832 | tf_op jit(solution)/shard_map/down_own_2/ppermute | solution.py:264
  19.8 11.9 %collective-permute-start.11 = (bf16[256,768]{1,0:T(8,128)(2,1)S(1)}, bf16[256,768]{1,0:T(8,128)(2,1)S(1)}, u32[]{:S(2)}, u32[]{:S(2)}) collective-permute-start(bf16[256,768]{1,0:T(8,128)(2,1)S(1)} %join_own_1.1.refs_0_.refs_5_), channel_id=1, source_target_pairs={{0,1},{1,0},{2,3},{3,2},{4,5},{5,4},{6,7},{7,6},{8,9},{9,8},{10,11... | collective-permute-start | bytes 1179656 | tf_op jit(solution)/shard_map/swap_slabs_1/ppermute | solution.py:264
  19.8 6.2 %collective-permute-start.2 = (bf16[1024,128]{1,0:T(8,128)(2,1)S(1)}, bf16[1024,128]{1,0:T(8,128)(2,1)S(1)}, u32[]{:S(2)}, u32[]{:S(2)}) collective-permute-start(bf16[1024,128]{1,0:T(8,128)(2,1)S(1)} %join_two.1.refs_0_.refs_2_), channel_id=1, source_target_pairs={{0,4},{2,6},{4,0},{6,2},{8,12},{10,14},{12,8},{14,10},{16,20},{18,... | collective-permute-start | bytes 786440 | tf_op jit(solution)/shard_map/from_y_1/ppermute | solution.py:264
  21.1 6.4 %collective-permute-start.3 = (bf16[1024,128]{1,0:T(8,128)(2,1)S(1)}, bf16[1024,128]{1,0:T(8,128)(2,1)S(1)}, u32[]{:S(2)}, u32[]{:S(2)}) collective-permute-start(bf16[1024,128]{1,0:T(8,128)(2,1)S(1)} %join_two.1.refs_0_.refs_2_), channel_id=1, source_target_pairs={{0,12},{2,14},{4,8},{6,10},{8,4},{10,6},{12,0},{14,2},{16,28},{18,... | collective-permute-start | bytes 786440 | tf_op jit(solution)/shard_map/from_y_3/ppermute | solution.py:264
  23.4 6.6 %collective-permute-start.10 = (bf16[128,768]{1,0:T(8,128)(2,1)S(1)}, bf16[128,768]{1,0:T(8,128)(2,1)S(1)}, u32[]{:S(2)}, u32[]{:S(2)}) collective-permute-start(bf16[128,768]{1,0:T(8,128)(2,1)S(1)} %split.11), channel_id=1, source_target_pairs={{0,224},{32,0},{64,32},{96,64},{128,96},{160,128},{192,160},{224,1... | collective-permute-start | bytes 589832 | tf_op jit(solution)/shard_map/down_own_3/ppermute | solution.py:264
  26.0 5.7 %collective-permute-start.9 = (bf16[128,768]{1,0:T(8,128)(2,1)S(1)}, bf16[128,768]{1,0:T(8,128)(2,1)S(1)}, u32[]{:S(2)}, u32[]{:S(2)}) collective-permute-start(bf16[128,768]{1,0:T(8,128)(2,1)S(1)} %split.10), channel_id=1, source_target_pairs={{0,32},{32,64},{64,96},{96,128},{128,160},{160,192},{192,224},{224... | collective-permute-start | bytes 589832 | tf_op jit(solution)/shard_map/up_own_3/ppermute | solution.py:264
  26.0 11.2 %collective-permute-start.14 = (bf16[256,768]{1,0:T(8,128)(2,1)S(1)}, bf16[256,768]{1,0:T(8,128)(2,1)S(1)}, u32[]{:S(2)}, u32[]{:S(2)}) collective-permute-start(bf16[256,768]{1,0:T(8,128)(2,1)S(1)} %join_own_2.1.refs_0_.refs_7_), channel_id=1, source_target_pairs={{0,1},{1,0},{2,3},{3,2},{4,5},{5,4},{6,7},{7,6},{8,9},{9,8},{10,11... | collective-permute-start | bytes 1179656 | tf_op jit(solution)/shard_map/swap_slabs_2/ppermute | solution.py:264
  27.6 9.7 %collective-permute-start.4 = (bf16[1024,128]{1,0:T(8,128)(2,1)S(1)}, bf16[1024,128]{1,0:T(8,128)(2,1)S(1)}, u32[]{:S(2)}, u32[]{:S(2)}) collective-permute-start(bf16[1024,128]{1,0:T(8,128)(2,1)S(1)} %hold.3), channel_id=1, source_target_pairs={{0,8},{2,10},{4,12},{6,14},{8,0},{10,2},{12,4},{14,6},{16,24},{18,... | collective-permute-start | bytes 786440 | tf_op jit(solution)/shard_map/from_y_2/ppermute | solution.py:264
  31.8 13.9 %copy-start = (bf16[128,768]{1,0:T(8,128)(2,1)S(1)}, bf16[128,768]{1,0:T(8,128)(2,1)}, u32[]{:S(2)}) copy-start(bf16[128,768]{1,0:T(8,128)(2,1)} %get-tuple-element.12.refs_3_) | copy-start | bytes 589828
  31.8 13.9 %copy-start.2 = (s32[37]{0:T(128)S(1)}, s32[37]{0:T(128)}, u32[]{:S(2)}) copy-start(s32[37]{0:T(128)} %get-tuple-element.10.refs_0_) | copy-start | bytes 448
  31.8 5.1 %collective-permute-start.12 = (bf16[64,768]{1,0:T(8,128)(2,1)S(1)}, bf16[64,768]{1,0:T(8,128)(2,1)S(1)}, u32[]{:S(2)}, u32[]{:S(2)}) collective-permute-start(bf16[64,768]{1,0:T(8,128)(2,1)S(1)} %split.12), channel_id=1, source_target_pairs={{0,32},{32,64},{64,96},{96,128},{128,160},{160,192},{192,224},{224... | collective-permute-start | bytes 294920 | tf_op jit(solution)/shard_map/up_own_half/ppermute | solution.py:264
  31.9 5.0 %collective-permute-start.13 = (bf16[64,768]{1,0:T(8,128)(2,1)S(1)}, bf16[64,768]{1,0:T(8,128)(2,1)S(1)}, u32[]{:S(2)}, u32[]{:S(2)}) collective-permute-start(bf16[64,768]{1,0:T(8,128)(2,1)S(1)} %split.13), channel_id=1, source_target_pairs={{0,224},{32,0},{64,32},{96,64},{128,96},{160,128},{192,160},{224,1... | collective-permute-start | bytes 294920 | tf_op jit(solution)/shard_map/down_own_half/ppermute | solution.py:264
  37.3 8.4 %collective-permute-start.15 = (bf16[4096,128]{1,0:T(8,128)(2,1)S(1)}, bf16[4096,128]{1,0:T(8,128)(2,1)S(1)}, u32[]{:S(2)}, u32[]{:S(2)}) collective-permute-start(bf16[4096,128]{1,0:T(8,128)(2,1)S(1)} %join_y.1.refs_1_), channel_id=1, source_target_pairs={{0,2},{2,0},{4,6},{6,4},{8,10},{10,8},{12,14},{14,12},{16,18},{18,... | collective-permute-start | bytes 3145736 | tf_op jit(solution)/shard_map/swap_cores/ppermute | solution.py:264
  41.8 7.2 %collective-permute-start.18 = (bf16[128,768]{1,0:T(8,128)(2,1)S(1)}, bf16[128,768]{1,0:T(8,128)(2,1)S(1)}, u32[]{:S(2)}, u32[]{:S(2)}) collective-permute-start(bf16[128,768]{1,0:T(8,128)(2,1)S(1)} %join_own_4.1.refs_4_.refs_3_), channel_id=1, source_target_pairs={{0,1},{1,0},{2,3},{3,2},{4,5},{5,4},{6,7},{7,6},{8,9},{9,8},{10,11... | collective-permute-start | bytes 589832 | tf_op jit(solution)/shard_map/swap_slabs_4/ppermute | solution.py:264
  42.4 8.2 %collective-permute-start.16 = (bf16[128,768]{1,0:T(8,128)(2,1)S(1)}, bf16[128,768]{1,0:T(8,128)(2,1)S(1)}, u32[]{:S(2)}, u32[]{:S(2)}) collective-permute-start(bf16[128,768]{1,0:T(8,128)(2,1)S(1)} %split.14), channel_id=1, source_target_pairs={{0,32},{32,64},{64,96},{96,128},{128,160},{160,192},{192,224},{224... | collective-permute-start | bytes 589832 | tf_op jit(solution)/shard_map/up_other_3/ppermute | solution.py:264
  42.9 7.6 %collective-permute-start.17 = (bf16[128,768]{1,0:T(8,128)(2,1)S(1)}, bf16[128,768]{1,0:T(8,128)(2,1)S(1)}, u32[]{:S(2)}, u32[]{:S(2)}) collective-permute-start(bf16[128,768]{1,0:T(8,128)(2,1)S(1)} %split.15), channel_id=1, source_target_pairs={{0,224},{32,0},{64,32},{96,64},{128,96},{160,128},{192,160},{224,1... | collective-permute-start | bytes 589832 | tf_op jit(solution)/shard_map/down_other_3/ppermute | solution.py:264

commit v5 on v4

--- a/solution.py
+++ b/solution.py
@@ -136,7 +136,7 @@
     meta, amps, blocks = refs[0], refs[1 : 1 + n_amp], refs[1 + n_amp : 1 + n_amp + n]
     acc, amp_all, int_buf, order = refs[1 + n_amp + n :]
     col = lax.axis_index("col")
-    n_y = amps[0].shape[0] // (2 * height)
+    n_y = n_amp // 2
     hi_now, y_now, core_now = col // (2 * n_y), col // 2 % n_y, col % 2
     for core in range(2):
         for y in range(n_y):
@@ -144,8 +144,7 @@
                 k = ((hi_now if hi == 0 else 1 - hi_now) * n_y + jnp.bitwise_xor(y_now, y)) * 2 + (
                     core_now if core == 0 else 1 - core_now
                 )
-                at = (2 * y + hi) * height
-                amp_all[k] = amps[core][at : at + height, :]
+                amp_all[k] = amps[core * n_y + y][hi * height : (hi + 1) * height, :]
     none_tile = amp_all.shape[0] - 1
     amp_all[none_tile] = jnp.zeros(amp_all.shape[1:], amp_all.dtype)
     zero_chunks, chunks = gather_tiles(pairs, meta, blocks, order, int_buf, none_tile)
@@ -297,13 +296,13 @@
     both_3 = join([below, above], needed=[others_1], name="join_own_3", flops=5000000000)
     low = up(join([(both_3, 0, half)], name="split"), "own_half")
     high = down(join([(both_3, TILE + half, half)], name="split"), "own_half")
-    own_4 = join([low, high], needed=[others_2], name="join_own_4")
+    own_4 = join([low, high], name="join_own_4")
     other_4 = swap_slabs(own_4, 4)
     other_below = up(join([(others_2, 0, TILE)], name="split"), "other_3")
     other_above = down(join([(others_2, TILE, TILE)], name="split"), "other_3")
 
-    own = join([amps[y] for y in range(n_y)], needed=[own_4], name="join_y")
-    amps = [own, swap(own)]
+    amps = [join([amps[y]], needed=[both_3], name="hold") for y in range(n_y)]
+    amps += [swap(a) for a in amps]
     first = {
         ((0, 0),): block,
         ((0, 1),): other,
@@ -313,8 +312,9 @@
         ((-2, 1), (2, 1)): others_2,
         ((-3, 0), (3, 0)): both_3,
     }
-    last = {((-4, 0),): own_4, ((-3, 1),): other_below, ((3, 1),): other_above, ((-4, 1),): other_4}
+    last = {((-4, 0),): own_4, ((-3, 1), (3, 1)): None, ((-4, 1),): other_4}
     acc, amp_all = early(rows, cols, k_tiles, list(first), meta, amps, list(first.values()))
+    last[((-3, 1), (3, 1))] = join([other_below, other_above], needed=[acc], name="join_other_3", flops=4000000000)
     return late(rows, cols, k_tiles, list(last), meta, acc, amp_all, list(last.values()))
 
 

time: 54.1 us -> 52.8 us (0.976); the launches traced: 54.1 us -> 52.3 us
  waiting for transfers between devices: 9.98 us -> 5.44 us
  starting transfers between devices: 33.7 us -> 36.3 us
    ppermute x19 -> x22, waiting for transfers between devices: 9.98 us -> 5.44 us  [send(): return lax.ppermute(a, axis, hops)]
    ppermute x19 -> x22, starting transfers between devices: 33.7 us -> 36.3 us  [send(): return lax.ppermute(a, axis, hops)]
  transfers between devices with their start and end apart: 19 -> 22, of which waited for: 8 -> 5; matrix products, arithmetic and copies ran while one was open for 0% -> 0% of each run, Pallas kernels for 7% -> 7%
where the time goes in v5:
time: 52.8 us; the launch traced here: 52.3 us
  starting transfers between devices  36.3 us (69%)
  Pallas kernels  9.19 us (17%)
  waiting for transfers between devices  5.44 us (10%)
  local copies, waits for them, and re-layouts  0.91 us (2%)
    ppermute x22, starting transfers between devices, send(): return lax.ppermute(a, axis, hops)  36.3 us
    ppermute x22, waiting for transfers between devices, send(): return lax.ppermute(a, axis, hops)  5.44 us
    pallas_call x1, Pallas kernels, late(): pl.pallas_call(functools.partial(late_kernel, pairs, (k_tiles, mt, nt)),...  3.41 us
    pallas_call x1, Pallas kernels, early(): pl.pallas_call(functools.partial(early_kernel, pairs, n_amp, rows // 2),...  3.4 us
    pallas_call x1, Pallas kernels, pack(): pl.pallas_call(functools.partial(pack_kernel, rows), out_shape=(jax.Shape...  2.03 us
  transfers between devices with their start and end apart: 22, of which 5 were waited for; matrix products, arithmetic and copies ran while one was open for 0% of the time, Pallas kernels for 7%

profile of v5, /device:TPU:1, one launch (start us, length us, event | category | flops | bytes accessed | tf_op | source)
XLA Modules:
  0.0 52.3 jit_solution(1474744424379560183)
XLA Ops:
  0.0 2.0 %pack.1 = (bf16[512,128]{1,0:T(8,128)(2,1)}, bf16[128,768]{1,0:T(8,128)(2,1)}, s32[37]{0:T(128)}) custom-call(s32[2]{0:T(128)} %pair_count.1, s32[1,8]{1,0:T(1,128)} %pair_tiles.1, s32[16]{0:T(128)} %vir.1, s32[12]{0:T(128)} %out_tiles.1, bf16[1,1024,128]{2,1,0:T(8,128)(2,1)} %amp.1, bf16[128,1536]{1,0:T(8,128)(2,1)} %ints.1), custom_call_target="tpu_custom_call" | custom-call | tf_op jit(solution)/shard_map/pack/pallas_call | solution.py:55
  2.0 2.1 %collective-permute-start.1 = (bf16[128,768]{1,0:T(8,128)(2,1)}, bf16[128,768]{1,0:T(8,128)(2,1)S(1)}, u32[]{:S(2)}, u32[]{:S(2)}) collective-permute-start(bf16[128,768]{1,0:T(8,128)(2,1)} %get-tuple-element.12.refs_9_), channel_id=1, source_target_pairs={{0,1},{1,0},{2,3},{3,2},{4,5},{5,4},{6,7},{7,6},{8,9},{9,8},{10,11... | collective-permute-start | bytes 589832 | tf_op jit(solution)/shard_map/swap_slabs_0/ppermute | solution.py:263
  4.2 2.5 %collective-permute-start = (bf16[512,128]{1,0:T(8,128)(2,1)}, bf16[512,128]{1,0:T(8,128)(2,1)S(1)}, u32[]{:S(2)}, u32[]{:S(2)}) collective-permute-start(bf16[512,128]{1,0:T(8,128)(2,1)} %get-tuple-element.11.refs_0_), channel_id=1, source_target_pairs={{0,16},{2,18},{4,20},{6,22},{8,24},{10,26},{12,28},{14,30},{16,0},... | collective-permute-start | bytes 393224 | tf_op jit(solution)/shard_map/across_x/ppermute | solution.py:263
  6.6 1.6 %collective-permute-start.2 = (bf16[128,768]{1,0:T(8,128)(2,1)}, bf16[128,768]{1,0:T(8,128)(2,1)S(1)}, u32[]{:S(2)}, u32[]{:S(2)}) collective-permute-start(bf16[128,768]{1,0:T(8,128)(2,1)} %get-tuple-element.12.refs_9_), channel_id=1, source_target_pairs={{0,32},{32,64},{64,96},{96,128},{128,160},{160,192},{192,224},{224... | collective-permute-start | bytes 589832 | tf_op jit(solution)/shard_map/up_own_1/ppermute | solution.py:263
  8.3 3.9 %collective-permute-start.3 = (bf16[128,768]{1,0:T(8,128)(2,1)}, bf16[128,768]{1,0:T(8,128)(2,1)S(1)}, u32[]{:S(2)}, u32[]{:S(2)}) collective-permute-start(bf16[128,768]{1,0:T(8,128)(2,1)} %get-tuple-element.12.refs_9_), channel_id=1, source_target_pairs={{0,224},{32,0},{64,32},{96,64},{128,96},{160,128},{192,160},{224,1... | collective-permute-start | bytes 589832 | tf_op jit(solution)/shard_map/down_own_1/ppermute | solution.py:263
  12.2 0.9 %copy-done.1 = bf16[512,128]{1,0:T(8,128)(2,1)S(1)} copy-done((bf16[512,128]{1,0:T(8,128)(2,1)S(1)}, bf16[512,128]{1,0:T(8,128)(2,1)}, u32[]{:S(2)}) %copy-start.1) | copy-done | bytes 131096
  13.1 0.8 %collective-permute-done.refs_1_ = bf16[512,128]{1,0:T(8,128)(2,1)S(1)} collective-permute-done((bf16[512,128]{1,0:T(8,128)(2,1)}, bf16[512,128]{1,0:T(8,128)(2,1)S(1)}, u32[]{:S(2)}, u32[]{:S(2)}) %collective-permute-start) | collective-permute-done | bytes 131104 | tf_op jit(solution)/shard_map/across_x/ppermute | solution.py:263
  13.9 0.0 collective-permute-done.1.refs_2_.refs_10_
  14.0 2.4 %collective-permute-done.2.refs_0_ = bf16[128,768]{1,0:T(8,128)(2,1)S(1)} collective-permute-done((bf16[128,768]{1,0:T(8,128)(2,1)}, bf16[128,768]{1,0:T(8,128)(2,1)S(1)}, u32[]{:S(2)}, u32[]{:S(2)}) %collective-permute-start.2) | collective-permute-done | bytes 196640 | tf_op jit(solution)/shard_map/up_own_1/ppermute | solution.py:263
  16.4 0.0 collective-permute-done.3.refs_1_
  16.5 0.1 collective-permute-start.4
  16.6 3.2 %collective-permute-start.5 = (bf16[128,768]{1,0:T(8,128)(2,1)S(1)}, bf16[128,768]{1,0:T(8,128)(2,1)S(1)}, u32[]{:S(2)}, u32[]{:S(2)}) collective-permute-start(bf16[128,768]{1,0:T(8,128)(2,1)S(1)} %split.9), channel_id=1, source_target_pairs={{0,224},{32,0},{64,32},{96,64},{128,96},{160,128},{192,160},{224,1... | collective-permute-start | bytes 589832 | tf_op jit(solution)/shard_map/down_own_2/ppermute | solution.py:263
  19.8 2.7 %collective-permute-start.10 = (bf16[1024,128]{1,0:T(8,128)(2,1)S(1)}, bf16[1024,128]{1,0:T(8,128)(2,1)S(1)}, u32[]{:S(2)}, u32[]{:S(2)}) collective-permute-start(bf16[1024,128]{1,0:T(8,128)(2,1)S(1)} %join_two.1.refs_2_.refs_0_), channel_id=1, source_target_pairs={{0,12},{2,14},{4,8},{6,10},{8,4},{10,6},{12,0},{14,2},{16,28},{18,... | collective-permute-start | bytes 786440 | tf_op jit(solution)/shard_map/from_y_3/ppermute | solution.py:263
  22.6 0.7 %collective-permute-done.4.refs_0_ = bf16[128,768]{1,0:T(8,128)(2,1)S(1)} collective-permute-done((bf16[128,768]{1,0:T(8,128)(2,1)S(1)}, bf16[128,768]{1,0:T(8,128)(2,1)S(1)}, u32[]{:S(2)}, u32[]{:S(2)}) %collective-permute-start.4) | collective-permute-done | bytes 196640 | tf_op jit(solution)/shard_map/up_own_2/ppermute | solution.py:263
  23.4 1.0 %collective-permute-start.6 = (bf16[128,768]{1,0:T(8,128)(2,1)S(1)}, bf16[128,768]{1,0:T(8,128)(2,1)S(1)}, u32[]{:S(2)}, u32[]{:S(2)}) collective-permute-start(bf16[128,768]{1,0:T(8,128)(2,1)S(1)} %split.10), channel_id=1, source_target_pairs={{0,32},{32,64},{64,96},{96,128},{128,160},{160,192},{192,224},{224... | collective-permute-start | bytes 589832 | tf_op jit(solution)/shard_map/up_own_3/ppermute | solution.py:263
  24.3 1.8 %collective-permute-start.7 = (bf16[128,768]{1,0:T(8,128)(2,1)S(1)}, bf16[128,768]{1,0:T(8,128)(2,1)S(1)}, u32[]{:S(2)}, u32[]{:S(2)}) collective-permute-start(bf16[128,768]{1,0:T(8,128)(2,1)S(1)} %split.11), channel_id=1, source_target_pairs={{0,224},{32,0},{64,32},{96,64},{128,96},{160,128},{192,160},{224,1... | collective-permute-start | bytes 589832 | tf_op jit(solution)/shard_map/down_own_3/ppermute | solution.py:263
  26.1 0.8 %collective-permute-done.10.refs_2_.refs_0_ = bf16[1024,128]{1,0:T(8,128)(2,1)S(1)} collective-permute-done((bf16[1024,128]{1,0:T(8,128)(2,1)S(1)}, bf16[1024,128]{1,0:T(8,128)(2,1)S(1)}, u32[]{:S(2)}, u32[]{:S(2)}) %collective-permute-start.10) | collective-permute-done | bytes 262176 | tf_op jit(solution)/shard_map/from_y_3/ppermute | solution.py:263
  26.9 1.4 %collective-permute-start.16 = (bf16[256,768]{1,0:T(8,128)(2,1)S(1)}, bf16[256,768]{1,0:T(8,128)(2,1)S(1)}, u32[]{:S(2)}, u32[]{:S(2)}) collective-permute-start(bf16[256,768]{1,0:T(8,128)(2,1)S(1)} %join_own_2.1.refs_0_.refs_13_), channel_id=1, source_target_pairs={{0,1},{1,0},{2,3},{3,2},{4,5},{5,4},{6,7},{7,6},{8,9},{9,8},{10,11... | collective-permute-start | bytes 1179656 | tf_op jit(solution)/shard_map/swap_slabs_2/ppermute | solution.py:263
  28.3 1.7 %collective-permute-start.11 = (bf16[1024,128]{1,0:T(8,128)(2,1)S(1)}, bf16[1024,128]{1,0:T(8,128)(2,1)S(1)}, u32[]{:S(2)}, u32[]{:S(2)}) collective-permute-start(bf16[1024,128]{1,0:T(8,128)(2,1)S(1)} %hold.9), channel_id=1, source_target_pairs={{0,8},{2,10},{4,12},{6,14},{8,0},{10,2},{12,4},{14,6},{16,24},{18,... | collective-permute-start | bytes 786440 | tf_op jit(solution)/shard_map/from_y_2/ppermute | solution.py:263
  30.0 0.0 copy-start
  30.1 3.7 %collective-permute-start.15 = (bf16[1024,128]{1,0:T(8,128)(2,1)S(1)}, bf16[1024,128]{1,0:T(8,128)(2,1)S(1)}, u32[]{:S(2)}, u32[]{:S(2)}) collective-permute-start(bf16[1024,128]{1,0:T(8,128)(2,1)S(1)} %hold.11.refs_4_), channel_id=1, source_target_pairs={{0,2},{2,0},{4,6},{6,4},{8,10},{10,8},{12,14},{14,12},{16,18},{18,... | collective-permute-start | bytes 786440 | tf_op jit(solution)/shard_map/swap_cores/ppermute | solution.py:263
  33.8 1.8 %collective-permute-start.17 = (bf16[64,768]{1,0:T(8,128)(2,1)S(1)}, bf16[64,768]{1,0:T(8,128)(2,1)S(1)}, u32[]{:S(2)}, u32[]{:S(2)}) collective-permute-start(bf16[64,768]{1,0:T(8,128)(2,1)S(1)} %split.12), channel_id=1, source_target_pairs={{0,32},{32,64},{64,96},{96,128},{128,160},{160,192},{192,224},{224... | collective-permute-start | bytes 294920 | tf_op jit(solution)/shard_map/up_own_half/ppermute | solution.py:263
  35.6 1.0 %collective-permute-start.18 = (bf16[64,768]{1,0:T(8,128)(2,1)S(1)}, bf16[64,768]{1,0:T(8,128)(2,1)S(1)}, u32[]{:S(2)}, u32[]{:S(2)}) collective-permute-start(bf16[64,768]{1,0:T(8,128)(2,1)S(1)} %split.13), channel_id=1, source_target_pairs={{0,224},{32,0},{64,32},{96,64},{128,96},{160,128},{192,160},{224,1... | collective-permute-start | bytes 294920 | tf_op jit(solution)/shard_map/down_own_half/ppermute | solution.py:263
  36.7 2.9 %collective-permute-start.13 = (bf16[1024,128]{1,0:T(8,128)(2,1)S(1)}, bf16[1024,128]{1,0:T(8,128)(2,1)S(1)}, u32[]{:S(2)}, u32[]{:S(2)}) collective-permute-start(bf16[1024,128]{1,0:T(8,128)(2,1)S(1)} %hold.8.refs_2_), channel_id=1, source_target_pairs={{0,2},{2,0},{4,6},{6,4},{8,10},{10,8},{12,14},{14,12},{16,18},{18,... | collective-permute-start | bytes 786440 | tf_op jit(solution)/shard_map/swap_cores/ppermute | solution.py:263
  39.6 0.7 %collective-permute-start.12 = (bf16[1024,128]{1,0:T(8,128)(2,1)S(1)}, bf16[1024,128]{1,0:T(8,128)(2,1)S(1)}, u32[]{:S(2)}, u32[]{:S(2)}) collective-permute-start(bf16[1024,128]{1,0:T(8,128)(2,1)S(1)} %hold.7.refs_1_), channel_id=1, source_target_pairs={{0,2},{2,0},{4,6},{6,4},{8,10},{10,8},{12,14},{14,12},{16,18},{18,... | collective-permute-start | bytes 786440 | tf_op jit(solution)/shard_map/swap_cores/ppermute | solution.py:263
  40.3 0.1 collective-permute-start.14
  40.4 0.7 %collective-permute-start.19 = (bf16[128,768]{1,0:T(8,128)(2,1)S(1)}, bf16[128,768]{1,0:T(8,128)(2,1)S(1)}, u32[]{:S(2)}, u32[]{:S(2)}) collective-permute-start(bf16[128,768]{1,0:T(8,128)(2,1)S(1)} %split.14), channel_id=1, source_target_pairs={{0,32},{32,64},{64,96},{96,128},{128,160},{160,192},{192,224},{224... | collective-permute-start | bytes 589832 | tf_op jit(solution)/shard_map/up_other_3/ppermute | solution.py:263
  41.1 2.0 %collective-permute-start.20 = (bf16[128,768]{1,0:T(8,128)(2,1)S(1)}, bf16[128,768]{1,0:T(8,128)(2,1)S(1)}, u32[]{:S(2)}, u32[]{:S(2)}) collective-permute-start(bf16[128,768]{1,0:T(8,128)(2,1)S(1)} %split.15), channel_id=1, source_target_pairs={{0,224},{32,0},{64,32},{96,64},{128,96},{160,128},{192,160},{224,1... | collective-permute-start | bytes 589832 | tf_op jit(solution)/shard_map/down_other_3/ppermute | solution.py:263
  43.2 1.3 %collective-permute-start.21 = (bf16[128,768]{1,0:T(8,128)(2,1)S(1)}, bf16[128,768]{1,0:T(8,128)(2,1)S(1)}, u32[]{:S(2)}, u32[]{:S(2)}) collective-permute-start(bf16[128,768]{1,0:T(8,128)(2,1)S(1)} %join_own_4.1.refs_3_), channel_id=1, source_target_pairs={{0,1},{1,0},{2,3},{3,2},{4,5},{5,4},{6,7},{7,6},{8,9},{9,8},{10,11... | collective-permute-start | bytes 589832 | tf_op jit(solution)/shard_map/swap_slabs_4/ppermute | solution.py:263
  44.6 3.4 %early_product.1 = (f32[2,512,768]{2,1,0:T(8,128)S(1)}, bf16[17,512,128]{2,1,0:T(8,128)(2,1)S(1)}) custom-call(s32[37]{0:T(128)S(1)} %copy-done.2, bf16[1024,128]{1,0:T(8,128)(2,1)S(1)} %hold.7.refs_1_, bf16[1024,128]{1,0:T(8,128)(2,1)S(1)} %hold.8.refs_2_, bf16[1024,128]{1,0:T(8,128)(2,1)S(1)} %hold.10.refs_3_, bf16[1024,128]{1,0:T(8,128)(2,1)S(1)} %hold.11.refs_4_, ...), custom_call_target="tpu_custom_call" | custom-call | tf_op jit(solution)/shard_map/early_product/pallas_call | solution.py:165
  48.0 0.7 %collective-permute-done.21.refs_5_ = bf16[128,768]{1,0:T(8,128)(2,1)S(1)} collective-permute-done((bf16[128,768]{1,0:T(8,128)(2,1)S(1)}, bf16[128,768]{1,0:T(8,128)(2,1)S(1)}, u32[]{:S(2)}, u32[]{:S(2)}) %collective-permute-start.21) | collective-permute-done | bytes 196640 | tf_op jit(solution)/shard_map/swap_slabs_4/ppermute | solution.py:263
  48.7 3.4 %late_product.1 = bf16[1,1024,1536]{2,1,0:T(8,128)(2,1)} custom-call(s32[37]{0:T(128)S(1)} %copy-done.2, f32[2,512,768]{2,1,0:T(8,128)S(1)} %get-tuple-element.13.refs_2_.refs_1_, bf16[17,512,128]{2,1,0:T(8,128)(2,1)S(1)} %get-tuple-element.14.refs_2_, bf16[128,768]{1,0:T(8,128)(2,1)S(1)} %join_own_4.1.refs_3_, bf16[256,768]{1,0:T(8,128)(2,1)S(1)} %join_other_3.1.refs_4_, ...), custom_call_target="tpu_custom_call" | custom-call | tf_op jit(solution)/shard_map/late_product/pallas_call | solution.py:236
  (41 shorter events, 0.4 us)
Async XLA Ops:
  2.0 11.9 %collective-permute-start.1 = (bf16[128,768]{1,0:T(8,128)(2,1)}, bf16[128,768]{1,0:T(8,128)(2,1)S(1)}, u32[]{:S(2)}, u32[]{:S(2)}) collective-permute-start(bf16[128,768]{1,0:T(8,128)(2,1)} %get-tuple-element.12.refs_9_), channel_id=1, source_target_pairs={{0,1},{1,0},{2,3},{3,2},{4,5},{5,4},{6,7},{7,6},{8,9},{9,8},{10,11... | collective-permute-start | bytes 589832 | tf_op jit(solution)/shard_map/swap_slabs_0/ppermute | solution.py:263
  4.2 9.8 %collective-permute-start = (bf16[512,128]{1,0:T(8,128)(2,1)}, bf16[512,128]{1,0:T(8,128)(2,1)S(1)}, u32[]{:S(2)}, u32[]{:S(2)}) collective-permute-start(bf16[512,128]{1,0:T(8,128)(2,1)} %get-tuple-element.11.refs_0_), channel_id=1, source_target_pairs={{0,16},{2,18},{4,20},{6,22},{8,24},{10,26},{12,28},{14,30},{16,0},... | collective-permute-start | bytes 393224 | tf_op jit(solution)/shard_map/across_x/ppermute | solution.py:263
  6.6 9.8 %collective-permute-start.2 = (bf16[128,768]{1,0:T(8,128)(2,1)}, bf16[128,768]{1,0:T(8,128)(2,1)S(1)}, u32[]{:S(2)}, u32[]{:S(2)}) collective-permute-start(bf16[128,768]{1,0:T(8,128)(2,1)} %get-tuple-element.12.refs_9_), channel_id=1, source_target_pairs={{0,32},{32,64},{64,96},{96,128},{128,160},{160,192},{192,224},{224... | collective-permute-start | bytes 589832 | tf_op jit(solution)/shard_map/up_own_1/ppermute | solution.py:263
  8.3 8.1 %collective-permute-start.3 = (bf16[128,768]{1,0:T(8,128)(2,1)}, bf16[128,768]{1,0:T(8,128)(2,1)S(1)}, u32[]{:S(2)}, u32[]{:S(2)}) collective-permute-start(bf16[128,768]{1,0:T(8,128)(2,1)} %get-tuple-element.12.refs_9_), channel_id=1, source_target_pairs={{0,224},{32,0},{64,32},{96,64},{128,96},{160,128},{192,160},{224,1... | collective-permute-start | bytes 589832 | tf_op jit(solution)/shard_map/down_own_1/ppermute | solution.py:263
  12.2 0.9 %copy-start.1 = (bf16[512,128]{1,0:T(8,128)(2,1)S(1)}, bf16[512,128]{1,0:T(8,128)(2,1)}, u32[]{:S(2)}) copy-start(bf16[512,128]{1,0:T(8,128)(2,1)} %get-tuple-element.11.refs_0_) | copy-start | bytes 393220
  16.5 6.8 %collective-permute-start.4 = (bf16[128,768]{1,0:T(8,128)(2,1)S(1)}, bf16[128,768]{1,0:T(8,128)(2,1)S(1)}, u32[]{:S(2)}, u32[]{:S(2)}) collective-permute-start(bf16[128,768]{1,0:T(8,128)(2,1)S(1)} %split.8), channel_id=1, source_target_pairs={{0,32},{32,64},{64,96},{96,128},{128,160},{160,192},{192,224},{224... | collective-permute-start | bytes 589832 | tf_op jit(solution)/shard_map/up_own_2/ppermute | solution.py:263
  16.6 6.7 %collective-permute-start.5 = (bf16[128,768]{1,0:T(8,128)(2,1)S(1)}, bf16[128,768]{1,0:T(8,128)(2,1)S(1)}, u32[]{:S(2)}, u32[]{:S(2)}) collective-permute-start(bf16[128,768]{1,0:T(8,128)(2,1)S(1)} %split.9), channel_id=1, source_target_pairs={{0,224},{32,0},{64,32},{96,64},{128,96},{160,128},{192,160},{224,1... | collective-permute-start | bytes 589832 | tf_op jit(solution)/shard_map/down_own_2/ppermute | solution.py:263
  19.8 10.2 %collective-permute-start.8 = (bf16[256,768]{1,0:T(8,128)(2,1)S(1)}, bf16[256,768]{1,0:T(8,128)(2,1)S(1)}, u32[]{:S(2)}, u32[]{:S(2)}) collective-permute-start(bf16[256,768]{1,0:T(8,128)(2,1)S(1)} %join_own_1.1.refs_0_.refs_11_), channel_id=1, source_target_pairs={{0,1},{1,0},{2,3},{3,2},{4,5},{5,4},{6,7},{7,6},{8,9},{9,8},{10,11... | collective-permute-start | bytes 1179656 | tf_op jit(solution)/shard_map/swap_slabs_1/ppermute | solution.py:263
  19.8 7.1 %collective-permute-start.10 = (bf16[1024,128]{1,0:T(8,128)(2,1)S(1)}, bf16[1024,128]{1,0:T(8,128)(2,1)S(1)}, u32[]{:S(2)}, u32[]{:S(2)}) collective-permute-start(bf16[1024,128]{1,0:T(8,128)(2,1)S(1)} %join_two.1.refs_2_.refs_0_), channel_id=1, source_target_pairs={{0,12},{2,14},{4,8},{6,10},{8,4},{10,6},{12,0},{14,2},{16,28},{18,... | collective-permute-start | bytes 786440 | tf_op jit(solution)/shard_map/from_y_3/ppermute | solution.py:263
  22.6 5.7 %collective-permute-start.9 = (bf16[1024,128]{1,0:T(8,128)(2,1)S(1)}, bf16[1024,128]{1,0:T(8,128)(2,1)S(1)}, u32[]{:S(2)}, u32[]{:S(2)}) collective-permute-start(bf16[1024,128]{1,0:T(8,128)(2,1)S(1)} %join_two.1.refs_2_.refs_0_), channel_id=1, source_target_pairs={{0,4},{2,6},{4,0},{6,2},{8,12},{10,14},{12,8},{14,10},{16,20},{18,... | collective-permute-start | bytes 786440 | tf_op jit(solution)/shard_map/from_y_1/ppermute | solution.py:263
  23.4 6.6 %collective-permute-start.6 = (bf16[128,768]{1,0:T(8,128)(2,1)S(1)}, bf16[128,768]{1,0:T(8,128)(2,1)S(1)}, u32[]{:S(2)}, u32[]{:S(2)}) collective-permute-start(bf16[128,768]{1,0:T(8,128)(2,1)S(1)} %split.10), channel_id=1, source_target_pairs={{0,32},{32,64},{64,96},{96,128},{128,160},{160,192},{192,224},{224... | collective-permute-start | bytes 589832 | tf_op jit(solution)/shard_map/up_own_3/ppermute | solution.py:263
  24.3 5.7 %collective-permute-start.7 = (bf16[128,768]{1,0:T(8,128)(2,1)S(1)}, bf16[128,768]{1,0:T(8,128)(2,1)S(1)}, u32[]{:S(2)}, u32[]{:S(2)}) collective-permute-start(bf16[128,768]{1,0:T(8,128)(2,1)S(1)} %split.11), channel_id=1, source_target_pairs={{0,224},{32,0},{64,32},{96,64},{128,96},{160,128},{192,160},{224,1... | collective-permute-start | bytes 589832 | tf_op jit(solution)/shard_map/down_own_3/ppermute | solution.py:263
  26.9 13.4 %collective-permute-start.16 = (bf16[256,768]{1,0:T(8,128)(2,1)S(1)}, bf16[256,768]{1,0:T(8,128)(2,1)S(1)}, u32[]{:S(2)}, u32[]{:S(2)}) collective-permute-start(bf16[256,768]{1,0:T(8,128)(2,1)S(1)} %join_own_2.1.refs_0_.refs_13_), channel_id=1, source_target_pairs={{0,1},{1,0},{2,3},{3,2},{4,5},{5,4},{6,7},{7,6},{8,9},{9,8},{10,11... | collective-permute-start | bytes 1179656 | tf_op jit(solution)/shard_map/swap_slabs_2/ppermute | solution.py:263
  28.3 8.3 %collective-permute-start.11 = (bf16[1024,128]{1,0:T(8,128)(2,1)S(1)}, bf16[1024,128]{1,0:T(8,128)(2,1)S(1)}, u32[]{:S(2)}, u32[]{:S(2)}) collective-permute-start(bf16[1024,128]{1,0:T(8,128)(2,1)S(1)} %hold.9), channel_id=1, source_target_pairs={{0,8},{2,10},{4,12},{6,14},{8,0},{10,2},{12,4},{14,6},{16,24},{18,... | collective-permute-start | bytes 786440 | tf_op jit(solution)/shard_map/from_y_2/ppermute | solution.py:263
  30.0 14.5 %copy-start = (bf16[128,768]{1,0:T(8,128)(2,1)S(1)}, bf16[128,768]{1,0:T(8,128)(2,1)}, u32[]{:S(2)}) copy-start(bf16[128,768]{1,0:T(8,128)(2,1)} %get-tuple-element.12.refs_9_) | copy-start | bytes 589828
  30.0 14.5 %copy-start.2 = (s32[37]{0:T(128)S(1)}, s32[37]{0:T(128)}, u32[]{:S(2)}) copy-start(s32[37]{0:T(128)} %get-tuple-element.10.refs_0_) | copy-start | bytes 448
  30.1 11.1 %collective-permute-start.15 = (bf16[1024,128]{1,0:T(8,128)(2,1)S(1)}, bf16[1024,128]{1,0:T(8,128)(2,1)S(1)}, u32[]{:S(2)}, u32[]{:S(2)}) collective-permute-start(bf16[1024,128]{1,0:T(8,128)(2,1)S(1)} %hold.11.refs_4_), channel_id=1, source_target_pairs={{0,2},{2,0},{4,6},{6,4},{8,10},{10,8},{12,14},{14,12},{16,18},{18,... | collective-permute-start | bytes 786440 | tf_op jit(solution)/shard_map/swap_cores/ppermute | solution.py:263
  33.8 5.8 %collective-permute-start.17 = (bf16[64,768]{1,0:T(8,128)(2,1)S(1)}, bf16[64,768]{1,0:T(8,128)(2,1)S(1)}, u32[]{:S(2)}, u32[]{:S(2)}) collective-permute-start(bf16[64,768]{1,0:T(8,128)(2,1)S(1)} %split.12), channel_id=1, source_target_pairs={{0,32},{32,64},{64,96},{96,128},{128,160},{160,192},{192,224},{224... | collective-permute-start | bytes 294920 | tf_op jit(solution)/shard_map/up_own_half/ppermute | solution.py:263
  35.6 4.8 %collective-permute-start.18 = (bf16[64,768]{1,0:T(8,128)(2,1)S(1)}, bf16[64,768]{1,0:T(8,128)(2,1)S(1)}, u32[]{:S(2)}, u32[]{:S(2)}) collective-permute-start(bf16[64,768]{1,0:T(8,128)(2,1)S(1)} %split.13), channel_id=1, source_target_pairs={{0,224},{32,0},{64,32},{96,64},{128,96},{160,128},{192,160},{224,1... | collective-permute-start | bytes 294920 | tf_op jit(solution)/shard_map/down_own_half/ppermute | solution.py:263
  36.7 6.5 %collective-permute-start.13 = (bf16[1024,128]{1,0:T(8,128)(2,1)S(1)}, bf16[1024,128]{1,0:T(8,128)(2,1)S(1)}, u32[]{:S(2)}, u32[]{:S(2)}) collective-permute-start(bf16[1024,128]{1,0:T(8,128)(2,1)S(1)} %hold.8.refs_2_), channel_id=1, source_target_pairs={{0,2},{2,0},{4,6},{6,4},{8,10},{10,8},{12,14},{14,12},{16,18},{18,... | collective-permute-start | bytes 786440 | tf_op jit(solution)/shard_map/swap_cores/ppermute | solution.py:263
  39.6 5.0 %collective-permute-start.12 = (bf16[1024,128]{1,0:T(8,128)(2,1)S(1)}, bf16[1024,128]{1,0:T(8,128)(2,1)S(1)}, u32[]{:S(2)}, u32[]{:S(2)}) collective-permute-start(bf16[1024,128]{1,0:T(8,128)(2,1)S(1)} %hold.7.refs_1_), channel_id=1, source_target_pairs={{0,2},{2,0},{4,6},{6,4},{8,10},{10,8},{12,14},{14,12},{16,18},{18,... | collective-permute-start | bytes 786440 | tf_op jit(solution)/shard_map/swap_cores/ppermute | solution.py:263
  40.3 4.3 %collective-permute-start.14 = (bf16[1024,128]{1,0:T(8,128)(2,1)S(1)}, bf16[1024,128]{1,0:T(8,128)(2,1)S(1)}, u32[]{:S(2)}, u32[]{:S(2)}) collective-permute-start(bf16[1024,128]{1,0:T(8,128)(2,1)S(1)} %hold.10.refs_3_), channel_id=1, source_target_pairs={{0,2},{2,0},{4,6},{6,4},{8,10},{10,8},{12,14},{14,12},{16,18},{18,... | collective-permute-start | bytes 786440 | tf_op jit(solution)/shard_map/swap_cores/ppermute | solution.py:263
  40.4 7.6 %collective-permute-start.19 = (bf16[128,768]{1,0:T(8,128)(2,1)S(1)}, bf16[128,768]{1,0:T(8,128)(2,1)S(1)}, u32[]{:S(2)}, u32[]{:S(2)}) collective-permute-start(bf16[128,768]{1,0:T(8,128)(2,1)S(1)} %split.14), channel_id=1, source_target_pairs={{0,32},{32,64},{64,96},{96,128},{128,160},{160,192},{192,224},{224... | collective-permute-start | bytes 589832 | tf_op jit(solution)/shard_map/up_other_3/ppermute | solution.py:263
  41.1 6.8 %collective-permute-start.20 = (bf16[128,768]{1,0:T(8,128)(2,1)S(1)}, bf16[128,768]{1,0:T(8,128)(2,1)S(1)}, u32[]{:S(2)}, u32[]{:S(2)}) collective-permute-start(bf16[128,768]{1,0:T(8,128)(2,1)S(1)} %split.15), channel_id=1, source_target_pairs={{0,224},{32,0},{64,32},{96,64},{128,96},{160,128},{192,160},{224,1... | collective-permute-start | bytes 589832 | tf_op jit(solution)/shard_map/down_other_3/ppermute | solution.py:263
  43.2 5.5 %collective-permute-start.21 = (bf16[128,768]{1,0:T(8,128)(2,1)S(1)}, bf16[128,768]{1,0:T(8,128)(2,1)S(1)}, u32[]{:S(2)}, u32[]{:S(2)}) collective-permute-start(bf16[128,768]{1,0:T(8,128)(2,1)S(1)} %join_own_4.1.refs_3_), channel_id=1, source_target_pairs={{0,1},{1,0},{2,3},{3,2},{4,5},{5,4},{6,7},{7,6},{8,9},{9,8},{10,11... | collective-permute-start | bytes 589832 | tf_op jit(solution)/shard_map/swap_slabs_4/ppermute | solution.py:263
